TPU v7x, 32 devices: a whole 2x2x4 slice. The times are simulated.
32 devices in a mesh: dp: 16 (over z, y, x), seq: 2 (over core).
Axes of the slice: x: 2, y: 2, z: 4, core: 2. Of those that a mesh axis runs over, the one named last changes fastest.
Arguments:
- block_in: bfloat16 [32, 1024, 768], P('dp', 'seq'), may hold values from -6 to 6
- lengths: int32 [32], P('dp'), may hold values from 128 to 1024, as said below
- out_grad: bfloat16 [32, 1024, 768], P('dp', 'seq'), may hold values from -6 to 6
- w_qkv: float32 [768, 2304], P('dp'), may hold values from -0.21875 to 0.21875
- w_out: float32 [768, 768], P('dp'), may hold values from -1.75 to 1.75
- w_up: float32 [768, 3072], P('dp'), may hold values from -0.21875 to 0.21875
- w_down: float32 [3072, 768], P('dp'), may hold values from -0.109375 to 0.109375
- vectors: float32 [12, 768], P(None, 'dp'), may hold values from -0.4 to 1.4
- first_qkv: float32 [768, 2304], P('dp'), may hold values from -896 to 896
- first_out: float32 [768, 768], P('dp'), may hold values from -64 to 64
- first_up: float32 [768, 3072], P('dp'), may hold values from -224 to 224
- first_down: float32 [3072, 768], P('dp'), may hold values from -512 to 512
- first_vectors: float32 [12, 768], P(None, 'dp'), may hold values from -448 to 448
- second_qkv: float32 [768, 2304], P('dp'), may hold values from 21299.2 to 85196.8
- second_out: float32 [768, 768], P('dp'), may hold values from 104.36608 to 417.46432
- second_up: float32 [768, 3072], P('dp'), may hold values from 1331.2 to 5324.8
- second_down: float32 [3072, 768], P('dp'), may hold values from 7667.712 to 30670.848
- second_vectors: float32 [12, 768], P(None, 'dp'), may hold values from 5324.8 to 21299.2
Outputs:
- block_out: bfloat16 [32, 1024, 768], P('dp', 'seq')
- in_grad: float32 [32, 1024, 768], P('dp', 'seq')
- new_qkv: float32 [768, 2304], P('dp')
- new_out: float32 [768, 768], P('dp')
- new_up: float32 [768, 3072], P('dp')
- new_down: float32 [3072, 768], P('dp')
- new_vectors: float32 [12, 768], P(None, 'dp')
- new_first_qkv: float32 [768, 2304], P('dp')
- new_first_out: float32 [768, 768], P('dp')
- new_first_up: float32 [768, 3072], P('dp')
- new_first_down: float32 [3072, 768], P('dp')
- new_first_vectors: float32 [12, 768], P(None, 'dp')
- new_second_qkv: float32 [768, 2304], P('dp')
- new_second_out: float32 [768, 768], P('dp')
- new_second_up: float32 [768, 3072], P('dp')
- new_second_down: float32 [3072, 768], P('dp')
- new_second_vectors: float32 [12, 768], P(None, 'dp')
Inputs may be any that keep to these rules, and one draw needn't show every extreme that they name: `lengths`: among the 2 slots of each index of dp, one has length 1024.
All inputs are finite; a program needn't handle non-finite values.
Results may differ from a plain program's by a relative error of at most 0.0085.
The roundings to bfloat16 on the way count: a program that leaves them out, or rounds other values in their place, can miss the bound.
Values may be sent and summed in bfloat16 or wider, within the bound.
No kernel may reach another device: no remote copies, remote signals or barrier semaphores. Data moves between devices by JAX's collectives and lax.ppermute only.
A program may use at most 192 MiB of HBM per device.

v0:
```python
import functools

import jax
import jax.numpy as jnp
from jax import lax
from jax.experimental import pallas as pl
from jax.experimental.pallas import tpu as pltpu
from jax.sharding import PartitionSpec as P

D = 768
HEADS = 12
HEAD_DIM = 64
FF = 3072
STEP = 10

EPS_NORM = 1e-05
EPS_ADAM = 1e-08
BETA_ONE = 0.5
BETA_TWO = 0.5
MATRIX_DECAY = 0.1
VECTOR_RATE = 0.1
NEG_FILL = -1e30
GELU_ROOT = 0.7978845608028654
GELU_CUBE = 0.044715
QKV_HALF = 3 * D // 2

F32 = jnp.float32
BF16 = jnp.bfloat16

NN = (((1,), (0,)), ((), ()))
NT = (((1,), (1,)), ((), ()))
TN = (((0,), (0,)), ((), ()))


def mm(left, right, dims=NN):
    return lax.dot_general(left, right, dims, preferred_element_type=F32)


def cost(flops, nbytes, trans=0):
    return pl.CostEstimate(flops=int(4 * flops), bytes_accessed=int(4 * nbytes), transcendentals=int(trans))


def params(mib=60):
    return pltpu.CompilerParams(vmem_limit_bytes=mib * 1024 * 1024)


def held_spec():
    return pl.BlockSpec(memory_space=pltpu.VMEM)


def at_rows(block):
    return pl.ds(pl.multiple_of(pl.program_id(0) * block, block), block)


def whole_spec(shape):
    return pl.BlockSpec(shape, lambda *idx: (0,) * len(shape), pipeline_mode=pl.Buffered(1))


class Pieces:
    def __init__(self, arrays, rows, ordered=False):
        self.arrays = arrays
        self.rows = rows
        self.ordered = ordered
        self.halves = 2
        self.count = len(arrays) // self.halves
        self.lines, self.depth = arrays[0].shape[:2]

    def specs(self):
        return [pl.BlockSpec(memory_space=pltpu.HBM)] * len(self.arrays)

    def row(self, seat_ref, at):
        return 0 if self.ordered else pl.multiple_of(seat_ref[at] * self.rows, 16)

    def start(self, refs, core_ref, seat_ref, start_col, width, target, sem):
        core = core_ref[0]
        at = 0
        for half in range(self.halves):
            where = core if half == 0 else 1 - core
            for s2 in range(self.count):
                ref = refs[half * self.count + s2]
                for s1 in range(self.lines):
                    for sz in range(self.depth):
                        row = self.row(seat_ref, at)
                        at += 1
                        col = pl.multiple_of(where * width, 128)
                        pltpu.make_async_copy(
                            ref.at[s1, sz, :, pl.ds(start_col, width)],
                            target.at[pl.ds(row, self.rows), pl.ds(col, width)],
                            sem,
                        ).start()

    def start_once(self, refs, seat_ref, start_col, width, target, sem):
        at = 0
        for s2 in range(self.count):
            for s1 in range(self.lines):
                for sz in range(self.depth):
                    row = self.row(seat_ref, at)
                    at += 1
                    pltpu.make_async_copy(
                        refs[s2].at[s1, sz, :, pl.ds(start_col, width)],
                        target.at[pl.ds(row, self.rows), :],
                        sem,
                    ).start()


def wait_all(target, sem):
    pltpu.make_async_copy(target, target, sem).wait()


def norm_parts(rows):
    mean = jnp.mean(rows, axis=-1, keepdims=True)
    centred = rows - mean
    variance = jnp.mean(centred * centred, axis=-1, keepdims=True)
    scale = lax.rsqrt(variance + EPS_NORM)
    return centred * scale, scale


def norm_back(d_normed, normed, scale):
    first = jnp.mean(d_normed, axis=-1, keepdims=True)
    second = jnp.mean(d_normed * normed, axis=-1, keepdims=True)
    return scale * (d_normed - first - normed * second)


def qkv_kernel(group, core_ref, seat_ref, x_ref, *refs):
    refs, (h_ref, qkv_ref, vec_ref, back_ref, w_ref, turned_ref, sems) = refs[:-7], refs[-7:]

    @pl.when(pl.program_id(0) == 0)
    def _():
        group.start(refs, core_ref, seat_ref, 0, QKV_HALF, w_ref, sems.at[0])
        group.start_once(refs, seat_ref, QKV_HALF, 128, turned_ref, sems.at[1])
        wait_all(turned_ref, sems.at[1])
        vec_ref[...] = turned_ref[...].astype(F32).T[:16]
        wait_all(w_ref, sems.at[0])

    def norm(rows):
        normed, _ = norm_parts(x_ref[rows, :].astype(F32))
        h = (normed * vec_ref[0:1, :] + vec_ref[1:2, :]).astype(BF16)
        h_ref[rows, :] = h
        return h

    block = x_ref.shape[0]
    h = norm(slice(0, block))
    for part, bias in enumerate((2, None, 3)):
        cols = slice(part * D, (part + 1) * D)
        product = mm(h, w_ref[:, cols])
        if bias is not None:
            product = product + vec_ref[bias : bias + 1, :]
        qkv_ref[:, cols] = product.astype(BF16)

    @pl.when(pl.program_id(0) < 3)
    def _():
        back_ref[...] = w_ref[:, at_rows(D)].T


def sub_blocks(rows):
    return [slice(at, at + 256) for at in range(0, rows, 256)]


def qkv_call(core, seats, x, group, block=256):
    rows = x.shape[0]
    return pl.pallas_call(
        functools.partial(qkv_kernel, group),
        name="qkv",
        grid_spec=pltpu.PrefetchScalarGridSpec(
            num_scalar_prefetch=2,
            grid=(rows // block,),
            in_specs=[pl.BlockSpec((block, D), lambda i, *s: (i, 0))] + group.specs(),
            out_specs=[
                pl.BlockSpec((block, D), lambda i, *s: (i, 0)),
                pl.BlockSpec((block, 3 * D), lambda i, *s: (i, 0)),
                pl.BlockSpec((16, D), lambda i, *s: (0, 0)),
                pl.BlockSpec((D, D), lambda i, *s: (jnp.minimum(i, 2), 0)),
            ],
            scratch_shapes=[
                pltpu.VMEM((D, 3 * D), BF16),
                pltpu.VMEM((D, 128), BF16),
                pltpu.SemaphoreType.DMA((2,)),
            ],
        ),
        out_shape=[
            jax.ShapeDtypeStruct((rows, D), BF16),
            jax.ShapeDtypeStruct((rows, 3 * D), BF16),
            jax.ShapeDtypeStruct((16, D), F32),
            jax.ShapeDtypeStruct((3 * D, D), BF16),
        ],
        compiler_params=params(12),
        cost_estimate=cost(2 * rows * D * 3 * D, 10e6),
    )(core, seats, x, *group.arrays)


def head_parts(length, k_all, q_turned, head):
    full_len = k_all.shape[0]
    lane = lax.broadcasted_iota(jnp.int32, (1, 128), 1)
    row = lax.broadcasted_iota(jnp.int32, (128, 1), 0)
    zero, one = jnp.zeros((), BF16), jnp.ones((), BF16)
    mine = (lane // HEAD_DIM) == head
    spare = HEAD_DIM * (1 - head)
    pos = lax.broadcasted_iota(jnp.int32, (full_len, 128), 0)
    fill = jnp.where(pos < length, 0.0, NEG_FILL).astype(BF16)
    k_head = jnp.where(mine, k_all, jnp.where(lane == spare, fill, zero))
    q_head = jnp.where((row // HEAD_DIM) == head, q_turned, jnp.where(row == spare, one, zero))
    return mine, k_head, q_head


def causal_mask(scores, block):
    full = scores.shape[0]
    key_pos = lax.broadcasted_iota(jnp.int32, (block, block), 0)
    query_pos = lax.broadcasted_iota(jnp.int32, (block, block), 1)
    last = jnp.where(key_pos <= query_pos, scores[full - block :], NEG_FILL)
    if full == block:
        return last
    return jnp.concatenate([scores[: full - block], last], axis=0)


def attend_kernel(start, core_ref, len_ref, qkv_ref, *refs):
    a_ref, lse_ref, mixed_ref, scores_ref = refs[-4:]
    block = 256
    full_len = qkv_ref.shape[0]
    length = len_ref[core_ref[0]]
    q_all, k_all, v_all = [
        qkv_ref[:, pl.ds(pl.multiple_of((pl.program_id(0) + start) * 128 + part * D, 128), 128)] for part in range(3)
    ]
    q_all = q_all * jnp.asarray(HEAD_DIM ** (-0.5), BF16)
    v_turned = v_all.T
    q_turned = q_all.T
    ones = jnp.ones((16, full_len), BF16)
    parts = []
    for head in range(2):
        _, k_head, q_head = head_parts(length, k_all, q_turned, head)
        v_head = jnp.concatenate([v_turned[head * HEAD_DIM : (head + 1) * HEAD_DIM], ones], axis=0)
        parts.append((k_head, q_head, v_head))
    units = [(head, j) for j in reversed(range(full_len // block)) for head in range(2)]

    def score(at):
        head, j = units[at]
        k_head, q_head, _ = parts[head]
        top = None
        for i in range(j + 1):
            rows = slice(i * block, (i + 1) * block)
            tile = mm(k_head[rows], q_head[:, j * block : (j + 1) * block])
            if i == j:
                tile = causal_mask(tile, block)
            scores_ref[at % 2, rows, :] = tile
            part = jnp.max(tile.reshape(block // 8, 8, block), axis=0)
            top = part if top is None else jnp.maximum(top, part)
        return jnp.max(top, axis=0, keepdims=True)

    def finish(at, top):
        head, j = units[at]
        v_head = parts[head][2]
        cols = slice(j * block, (j + 1) * block)
        mixed = None
        for i in range(j + 1):
            rows = slice(i * block, (i + 1) * block)
            exped = jnp.exp(scores_ref[at % 2, rows, :] - top).astype(BF16)
            part = mm(v_head[:, rows], exped)
            mixed = part if mixed is None else mixed + part
        total = mixed[HEAD_DIM : HEAD_DIM + 1]
        mixed_ref[head * HEAD_DIM : (head + 1) * HEAD_DIM, cols] = mixed[:HEAD_DIM] / total
        lse_ref[0, head : head + 1, cols] = top + jnp.log(total)

    top = score(0)
    for at in range(len(units)):
        later = score(at + 1) if at + 1 < len(units) else None
        finish(at, top)
        top = later
    a_ref[...] = mixed_ref[...].T.astype(BF16)


def attend_call(core, lengths, qkv, first, count, before):
    rows = qkv.shape[0]
    pairs = HEADS // 2
    before = list(before)
    return pl.pallas_call(
        functools.partial(attend_kernel, first),
        name="attend",
        grid_spec=pltpu.PrefetchScalarGridSpec(
            num_scalar_prefetch=2,
            grid=(count,),
            in_specs=[held_spec()] + [pl.BlockSpec(memory_space=pl.ANY)] * len(before),
            out_specs=[
                pl.BlockSpec((rows, 128), lambda i, c, n: (0, i + first)),
                pl.BlockSpec((1, 8, rows), lambda i, c, n: (i + first, 0, 0)),
            ],
            scratch_shapes=[pltpu.VMEM((128, rows), F32), pltpu.VMEM((2, rows, 256), F32)],
        ),
        out_shape=[
            jax.ShapeDtypeStruct((rows, D), BF16),
            jax.ShapeDtypeStruct((pairs, 8, rows), F32),
        ],
        input_output_aliases={3 + i: i for i in range(len(before))},
        compiler_params=params(12),
        cost_estimate=cost(3e9 * count, 1.2e6 * count, 2 * rows * rows * 0.6 * count),
    )(core, lengths, qkv, *before)


def attend_back_kernel(core_ref, len_ref, q_ref, k_ref, v_ref, a_ref, da_ref, lse_ref, *refs):
    dq_ref, dk_ref, dv_ref, dqt_ref, dk_acc, dv_acc = refs[-6:]
    block = 256
    full_len = q_ref.shape[0]
    length = len_ref[core_ref[0]]
    scale = HEAD_DIM ** (-0.5)
    q_all = q_ref[...] * jnp.asarray(scale, BF16)
    k_all = k_ref[...]
    k_turned = k_all.T
    v_all = v_ref[...]
    da_all = da_ref[...]
    inner = (da_all.astype(F32) * a_ref[...].astype(F32)).T
    q_turned, da_turned = q_all.T, da_all.T
    parts = []
    for head in range(2):
        mine, k_head, q_head = head_parts(length, k_all, q_turned, head)
        zero = jnp.zeros((), BF16)
        q_plain = jnp.where(mine, q_all, zero)
        da_head = jnp.where(mine, da_all, zero)
        row = lax.broadcasted_iota(jnp.int32, (128, 1), 0)
        da_cols = jnp.where((row // HEAD_DIM) == head, da_turned, zero)
        lanes = slice(head * HEAD_DIM, (head + 1) * HEAD_DIM)
        centre = jnp.sum(inner[lanes], axis=0, keepdims=True)
        parts.append((k_head, q_plain, q_head, da_head, da_cols, lanes, centre))
    units = [
        (head, j, i)
        for j in reversed(range(full_len // block))
        for head in range(2)
        for i in range(j + 1)
    ]

    def score(at):
        head, j, i = units[at]
        k_head, _, q_head, _, da_cols, _, _ = parts[head]
        rows, cols = slice(i * block, (i + 1) * block), slice(j * block, (j + 1) * block)
        tile = mm(k_head[rows], q_head[:, cols])
        if i == j:
            tile = causal_mask(tile, block)
        return tile, mm(v_all[rows], da_cols[:, cols])

    seen = set()
    ready = score(0)
    dq_part = None
    for at, (head, j, i) in enumerate(units):
        later = score(at + 1) if at + 1 < len(units) else None
        scores, d_probs = ready
        _, q_plain, _, da_head, _, lanes, centre = parts[head]
        rows, cols = slice(i * block, (i + 1) * block), slice(j * block, (j + 1) * block)
        probs = jnp.exp(scores - lse_ref[0, head : head + 1, cols])
        d_scores = (probs * (d_probs - centre[:, cols])).astype(BF16)
        dv_part = mm(probs.astype(BF16), da_head[cols])
        dk_part = mm(d_scores, q_plain[cols])
        if i in seen:
            dv_acc[rows] += dv_part
            dk_acc[rows] += dk_part
        else:
            seen.add(i)
            dv_acc[rows] = dv_part
            dk_acc[rows] = dk_part
        part = mm(k_turned[lanes, rows], d_scores)
        dq_part = part if i == 0 else dq_part + part
        if i == j:
            dqt_ref[lanes, cols] = dq_part * scale
        ready = later
    dq_ref[...] = dqt_ref[...].T.astype(BF16)
    dk_ref[...] = dk_acc[...].astype(BF16)
    dv_ref[...] = dv_acc[...].astype(BF16)


def attend_back_call(core, lengths, qkv, a, da, lse, start, count, before):
    rows = qkv.shape[0]
    pairs = HEADS // 2
    before = list(before)
    pair_spec = pl.BlockSpec((rows, 128), lambda i, c, n: (0, i + start))
    return pl.pallas_call(
        attend_back_kernel,
        name="attend_back",
        grid_spec=pltpu.PrefetchScalarGridSpec(
            num_scalar_prefetch=2,
            grid=(count,),
            in_specs=[
                pair_spec,
                pl.BlockSpec((rows, 128), lambda i, c, n: (0, i + start + pairs)),
                pl.BlockSpec((rows, 128), lambda i, c, n: (0, i + start + 2 * pairs)),
                pair_spec,
                pair_spec,
                pl.BlockSpec((1, 8, rows), lambda i, c, n: (i + start, 0, 0)),
            ]
            + [pl.BlockSpec(memory_space=pl.ANY)] * len(before),
            out_specs=[pair_spec, pair_spec, pair_spec],
            scratch_shapes=[
                pltpu.VMEM((128, rows), F32),
                pltpu.VMEM((rows, 128), F32),
                pltpu.VMEM((rows, 128), F32),
            ],
        ),
        out_shape=[jax.ShapeDtypeStruct((rows, D), BF16)] * 3,
        input_output_aliases={8 + i: i for i in range(len(before))},
        compiler_params=params(16),
        cost_estimate=cost(6e9 * count, 2e6 * count, 2 * rows * rows * 0.6 * count),
    )(core, lengths, qkv, qkv, qkv, a, da, lse, *before)


def valid_rows(core_ref, len_ref, block):
    pos = pl.program_id(0) * block + lax.broadcasted_iota(jnp.int32, (block, 1), 0)
    return pos < len_ref[core_ref[0]]


def add_row(acc_ref, row, value):
    acc_ref[row : row + 1, :] += jnp.sum(value, axis=0, keepdims=True)


def row_block(core, i, steps):
    half = steps // 2
    return jnp.where(i < half, (1 - core) * half + i, core * half + i - half)


def up_kernel(group, core_ref, len_ref, seat_ref, x_ref, a_ref, og_ref, vec_ref, *refs):
    refs, (
        mid_ref, h_ref, e_ref, slope_ref, dy_ref, wo_back_ref, wu_back_ref, wo_ref, wu_ref, sems,
    ) = refs[:-10], refs[-10:]
    block = x_ref.shape[0]

    @pl.when(pl.program_id(0) == 0)
    def _():
        group.start(refs, core_ref, seat_ref, 0, D // 2, wo_ref, sems.at[0])
        group.start(refs, core_ref, seat_ref, D // 2, FF // 2, wu_ref, sems.at[1])
        wait_all(wo_ref, sems.at[0])
        wait_all(wu_ref, sems.at[1])

    valid = valid_rows(core_ref, len_ref, block)
    dy_ref[...] = jnp.where(valid, og_ref[...].astype(F32), 0.0).astype(BF16)
    mid = x_ref[...].astype(F32) + mm(a_ref[...], wo_ref[...]) + vec_ref[4:5, :]
    mid_ref[...] = mid
    normed, _ = norm_parts(mid)
    h = (normed * vec_ref[5:6, :] + vec_ref[6:7, :]).astype(BF16)
    h_ref[...] = h

    def act(j, z):
        cols = slice(j * D, (j + 1) * D)
        z = z + vec_ref[8 + j : 9 + j, :]
        squared = z * z
        turned = jnp.tanh(z * (GELU_ROOT + (GELU_ROOT * GELU_CUBE) * squared))
        half = 0.5 * turned + 0.5
        act = z * half
        e_ref[:, cols] = act.astype(BF16)
        slope = half + act * (1.0 - turned) * (GELU_ROOT + (3.0 * GELU_ROOT * GELU_CUBE) * squared)
        slope_ref[:, cols] = slope.astype(BF16)

    quarter = at_rows(D)
    wu_back_ref[...] = wu_ref[:, quarter].T

    @pl.when(pl.program_id(0) == 0)
    def _():
        wo_back_ref[...] = wo_ref[...].T

    waiting = None
    for j in range(FF // D):
        z = mm(h, wu_ref[:, j * D : (j + 1) * D])
        if waiting is not None:
            act(*waiting)
        waiting = (j, z)
    act(*waiting)


def up_call(core, lengths, seats, x, a, og, vec, group, block=256):
    rows = x.shape[0]
    assert rows // block == FF // D
    row_spec = pl.BlockSpec((block, D), lambda i, *s: (i, 0))
    wide_spec = pl.BlockSpec((block, FF), lambda i, *s: (i, 0))
    low, wide = [jax.ShapeDtypeStruct((rows, width), BF16) for width in (D, FF)]
    return pl.pallas_call(
        functools.partial(up_kernel, group),
        name="up",
        grid_spec=pltpu.PrefetchScalarGridSpec(
            num_scalar_prefetch=3,
            grid=(rows // block,),
            in_specs=[row_spec, row_spec, row_spec, whole_spec(vec.shape)] + group.specs(),
            out_specs=[
                row_spec, row_spec, wide_spec, wide_spec, row_spec,
                pl.BlockSpec((D, D), lambda i, *s: (0, 0)),
                pl.BlockSpec((D, D), lambda i, *s: (i, 0)),
            ],
            scratch_shapes=[
                pltpu.VMEM((D, D), BF16),
                pltpu.VMEM((D, FF), BF16),
                pltpu.SemaphoreType.DMA((2,)),
            ],
        ),
        out_shape=[
            jax.ShapeDtypeStruct((rows, D), F32),
            low,
            wide,
            wide,
            low,
            jax.ShapeDtypeStruct((D, D), BF16),
            jax.ShapeDtypeStruct((FF, D), BF16),
        ],
        compiler_params=params(48),
        cost_estimate=cost(6e9, 30e6, rows * FF),
    )(core, lengths, seats, x, a, og, vec, *group.arrays)


def down_kernel(
    group, core_ref, len_ref, seat_ref, mid_ref, e_ref, slope_ref, dy_ref, wo_back_ref, wu_back_ref, vec_ref, *refs
):
    refs, (
        theirs_ref, mine_ref, dz_ref, dmb_ref, dm_ref, da_ref, acc_ref, wd_ref, wd_back_ref, sems,
    ) = refs[:-10], refs[-10:]
    block = da_ref.shape[0]
    step, steps = pl.program_id(0), pl.num_programs(0)

    @pl.when(step == 0)
    def _():
        group.start(refs, core_ref, seat_ref, 0, D // 2, wd_ref, sems.at[0])
        acc_ref[...] = jnp.zeros_like(acc_ref)
        wait_all(wd_ref, sems.at[0])
        for j in range(FF // D):
            cols = slice(j * D, (j + 1) * D)
            wd_back_ref[:, cols] = wd_ref[cols, :].T

    mid = mid_ref[...]
    down = vec_ref[7:8, :] + mid + mm(e_ref[...], wd_ref[...])
    pos = row_block(core_ref[0], step, steps) * block + lax.broadcasted_iota(jnp.int32, (block, 1), 0)
    down = jnp.where(pos < len_ref[core_ref[0]], down, 0.0).astype(BF16)

    @pl.when(step < steps // 2)
    def _():
        theirs_ref[...] = down

    @pl.when(step >= steps // 2)
    def _():
        mine_ref[0] = down

    dy = dy_ref[...]
    add_row(acc_ref, 7, dy.astype(F32))
    dh = None
    waiting = None
    for j in range(FF // D + 1):
        later = None
        if j < FF // D:
            later = (j, mm(dy, wd_back_ref[:, j * D : (j + 1) * D]))
        if waiting is not None:
            at, de = waiting
            cols = slice(at * D, (at + 1) * D)
            dz = (de * slope_ref[:, cols].astype(F32)).astype(BF16)
            dz_ref[:, cols] = dz
            add_row(acc_ref, 8 + at, dz.astype(F32))
            part = mm(dz, wu_back_ref[cols, :])
            dh = part if dh is None else dh + part
        waiting = later
    normed, scale = norm_parts(mid)
    add_row(acc_ref, 5, dh * normed)
    add_row(acc_ref, 6, dh)
    dm = dy.astype(F32) + norm_back(dh * vec_ref[5:6, :], normed, scale)
    dm_ref[...] = dm
    dm_low = dm.astype(BF16)
    dmb_ref[...] = dm_low
    add_row(acc_ref, 4, dm_low.astype(F32))
    da_ref[...] = mm(dm_low, wo_back_ref[...]).astype(BF16)


def down_call(core, lengths, seats, mid, e, slope, dy, wo, wu, vec, group, block=256):
    rows = mid.shape[0]
    steps = rows // block
    half = steps // 2
    row_spec, wide_spec = [
        pl.BlockSpec((block, width), lambda i, c, *s: (row_block(c[0], i, steps), 0)) for width in (D, FF)
    ]
    return pl.pallas_call(
        functools.partial(down_kernel, group),
        name="down",
        grid_spec=pltpu.PrefetchScalarGridSpec(
            num_scalar_prefetch=3,
            grid=(steps,),
            in_specs=[row_spec, wide_spec, wide_spec, row_spec]
            + [whole_spec(part.shape) for part in (wo, wu, vec)]
            + group.specs(),
            out_specs=[
                pl.BlockSpec((block, D), lambda i, *s: (jnp.minimum(i, half - 1), 0)),
                pl.BlockSpec((1, block, D), lambda i, c, *s: (c[0], jnp.maximum(i - half, 0), 0)),
                wide_spec, row_spec, row_spec, row_spec,
                pl.BlockSpec((16, D), lambda i, *s: (0, 0)),
            ],
            scratch_shapes=[pltpu.VMEM((FF, D), BF16), pltpu.VMEM((D, FF), BF16), pltpu.SemaphoreType.DMA((1,))],
        ),
        out_shape=[
            jax.ShapeDtypeStruct((rows // 2, D), BF16),
            jax.ShapeDtypeStruct((2, rows // 2, D), BF16),
            jax.ShapeDtypeStruct((rows, FF), BF16),
            jax.ShapeDtypeStruct((rows, D), BF16),
            jax.ShapeDtypeStruct((rows, D), F32),
            jax.ShapeDtypeStruct((rows, D), BF16),
            jax.ShapeDtypeStruct((16, D), F32),
        ],
        compiler_params=params(48),
        cost_estimate=cost(1.6e10, 35e6),
    )(core, lengths, seats, mid, e, slope, dy, wo, wu, vec, *group.arrays)


def pick(values, half, mode):
    if mode == "split":
        width = values.shape[1] // 2
        return [values[:, half * width : (half + 1) * width]]
    return [values[:, at : at + 128] for at in range(half * 128, values.shape[1], 256)]


def weight_grad_kernel(lefts, rights, mode, core_ref, *refs):
    left_refs, right_refs = refs[:lefts], refs[lefts : lefts + sum(rights)]
    own_ref, other_ref = refs[-2:]
    halves = ([], [])
    at = 0
    for left_ref, count in zip(left_refs, rights):
        left = left_ref[...]
        for right_ref in right_refs[at : at + count]:
            whole = mm(left, right_ref[...], TN).astype(BF16)
            for half in range(2):
                halves[half].extend(pick(whole, half, mode))
        at += count
    low, high = [part[0] if len(part) == 1 else jnp.concatenate(part, axis=1) for part in halves]

    @pl.when(core_ref[0] == 0)
    def _():
        own_ref[...] = low
        other_ref[...] = high

    @pl.when(core_ref[0] != 0)
    def _():
        own_ref[...] = high
        other_ref[...] = low


def weight_grad_call(core, products, block, name, mode="split", cols=None):
    rows, height = products[0][0].shape
    lefts = [left for left, _ in products]
    rights = [right for _, group in products for right in group]
    widths = [right.shape[1] if cols is None else cols[0] for right in rights]
    width = sum(widths)
    seat = 0 if cols is None else cols[1]
    return pl.pallas_call(
        functools.partial(weight_grad_kernel, len(lefts), [len(group) for _, group in products], mode),
        name=name,
        grid_spec=pltpu.PrefetchScalarGridSpec(
            num_scalar_prefetch=1,
            grid=(height // block,),
            in_specs=[pl.BlockSpec((rows, block), lambda i, c: (0, i))] * len(lefts)
            + [
                pl.BlockSpec((rows, w), lambda i, c: (0, seat), pipeline_mode=pl.Buffered(1)) for w in widths
            ],
            out_specs=[pl.BlockSpec((block, width // 2), lambda i, c: (i, 0))] * 2,
        ),
        out_shape=[jax.ShapeDtypeStruct((height, width // 2), BF16)] * 2,
        compiler_params=params(16 if mode == "turns" else 48),
        cost_estimate=cost(2 * rows * height * width, rows * (height + width) * 2 + height * width * 2),
    )(core, *lefts, *rights)


def last_kernel(
    core_ref, x_ref, dm_ref, dq_ref, dk_ref, dv_ref, w_ref, vec_ref, before_ref, theirs_ref, mine_ref, acc_ref
):
    step, steps = pl.program_id(0), pl.num_programs(0)

    @pl.when(step == 0)
    def _():
        acc_ref[...] = before_ref[...]

    subs = sub_blocks(x_ref.shape[0])

    def product(rows):
        return (
            mm(dq_ref[rows, :], w_ref[:D])
            + mm(dk_ref[rows, :], w_ref[D : 2 * D])
            + mm(dv_ref[rows, :], w_ref[2 * D :])
        )

    grads = []
    dh = product(subs[0])
    add_row(acc_ref, 2, dq_ref[...].astype(F32))
    add_row(acc_ref, 3, dv_ref[...].astype(F32))
    for at, rows in enumerate(subs):
        later = product(subs[at + 1]) if at + 1 < len(subs) else None
        normed, scale = norm_parts(x_ref[rows, :].astype(F32))
        add_row(acc_ref, 0, dh * normed)
        add_row(acc_ref, 1, dh)
        grads.append(dm_ref[rows, :] + norm_back(dh * vec_ref[0:1, :], normed, scale))
        dh = later

    @pl.when(step < steps // 2)
    def _():
        for rows, grad in zip(subs, grads):
            theirs_ref[rows, :] = grad

    @pl.when(step >= steps // 2)
    def _():
        for rows, grad in zip(subs, grads):
            mine_ref[0, rows, :] = grad


def last_call(core, x, dm, dq, dk, dv, w, vec, before, block=256):
    rows = x.shape[0]
    steps = rows // block
    half = steps // 2
    row_spec = pl.BlockSpec((block, D), lambda i, c, *s: (row_block(c[0], i, steps), 0))
    return pl.pallas_call(
        last_kernel,
        name="last",
        grid_spec=pltpu.PrefetchScalarGridSpec(
            num_scalar_prefetch=1,
            grid=(steps,),
            in_specs=[row_spec] * 5 + [whole_spec(part.shape) for part in (w, vec, before)],
            out_specs=[
                pl.BlockSpec((block, D), lambda i, *s: (jnp.minimum(i, half - 1), 0)),
                pl.BlockSpec((1, block, D), lambda i, c, *s: (c[0], jnp.maximum(i - half, 0), 0)),
                pl.BlockSpec((16, D), lambda i, *s: (0, 0)),
            ],
        ),
        out_shape=[
            jax.ShapeDtypeStruct((rows // 2, D), F32),
            jax.ShapeDtypeStruct((2, rows // 2, D), F32),
            jax.ShapeDtypeStruct((16, D), F32),
        ],
        compiler_params=params(12),
        cost_estimate=cost(rows * 6 * D * D, 16e6),
    )(core, x, dm, dq, dk, dv, w, vec, before)


def adam_kernel(plans, sources, core_ref, *refs):
    halves = [refs[2 * i : 2 * i + 2] for i in range(sources)]
    count = len(plans)
    states = refs[2 * sources : 2 * sources + 3 * count]
    outs = refs[2 * sources + 3 * count : 2 * sources + 6 * count]
    grads = refs[2 * sources + 6 * count :]
    for core in range(2):

        @pl.when(core_ref[0] == core)
        def _():
            for (_, _, moves), grad_ref in zip(plans, grads):
                for source, start, width, place0, place1 in moves:
                    for half, place in ((0, place0), (1, place1)):
                        ref = halves[source][0 if half == core else 1]
                        grad_ref[:, place : place + width] = ref[:, start : start + width].astype(F32)

    for i, (rate, decay, _) in enumerate(plans):
        weight, first, second = states[3 * i : 3 * i + 3]
        new = adamw(weight[...], grads[i][...], first[...], second[...], rate, decay)
        for out, value in zip(outs[3 * i : 3 * i + 3], new):
            out[...] = value


def adam_call(core, halves, states, plans):
    flat = [part for pair in halves for part in pair]
    held = [part for state in states for part in state]
    spec = pl.BlockSpec(memory_space=pltpu.VMEM)
    news = pl.pallas_call(
        functools.partial(adam_kernel, plans, len(halves)),
        name="adam",
        in_specs=[pl.BlockSpec(memory_space=pltpu.SMEM)] + [spec] * (len(flat) + len(held)),
        out_specs=[spec] * len(held),
        out_shape=[jax.ShapeDtypeStruct(part.shape, F32) for part in held],
        scratch_shapes=[pltpu.VMEM(state[0].shape, F32) for state in states],
        compiler_params=params(12),
        cost_estimate=cost(1e6, 24 * sum(state[0].size for state in states)),
    )(core, *flat, *held)
    return [news[3 * i : 3 * i + 3] for i in range(len(states))]


def after(value, *others):
    if not others:
        return value
    return lax.optimization_barrier((value,) + others)[0]


def cut(array, axis, index, size=1):
    starts = [jnp.uint32(0)] * array.ndim
    sizes = list(array.shape)
    starts[axis], sizes[axis] = index, size
    return lax.dynamic_slice(array, starts, sizes)


class Grid:
    def __init__(self, chips):
        log = chips.bit_length() - 1
        side = 1 << (log // 3)
        if side * side * (chips // (side * side)) != chips:
            side = 1
        self.chips = chips
        self.n = side
        self.nz = chips // (side * side)
        self.core = lax.axis_index("seq")
        self.chip = lax.axis_index("dp")
        self.x = self.chip % side
        self.y = self.chip // side % side
        self.z = self.chip // (side * side)

    def pin(self, value):
        n, core = self.n, self.core
        first, second = self.coords(core)
        places = {
            "core": core,
            "other": 1 - core,
            "chip": self.chip,
            "seats": self.seats(True),
            "q_seats": self.seats(False),
        }
        for s in range(n):
            for t in range(n):
                places["plane", s, t] = self.plane((first + s) % n, (second + t) % n, core)
        for at in range(self.nz):
            places["z", at] = self.z ^ at
        names = list(places)
        held = lax.optimization_barrier((value, *[places[name].astype(jnp.uint32) for name in names]))
        self.places = dict(zip(names, held[1:]))
        return held[0]

    def plane(self, first, second, core):
        return jnp.where(core == 0, second * self.n + first, first * self.n + second)

    def coords(self, core):
        return jnp.where(core == 0, self.x, self.y), jnp.where(core == 0, self.y, self.x)

    def permute(self, value, axis, shift=0):
        pairs = []
        for chip in range(self.chips):
            for core in range(2):
                x, y, z = chip % self.n, chip // self.n % self.n, chip // (self.n * self.n)
                to_core = core
                if axis == "z":
                    z = (z + shift) % self.nz
                elif axis == "zx":
                    z = z ^ shift
                elif axis == "core":
                    to_core = 1 - core
                elif (axis == "first") == (core == 0):
                    x = (x + shift) % self.n
                else:
                    y = (y + shift) % self.n
                pairs.append((chip * 2 + core, ((z * self.n + y) * self.n + x) * 2 + to_core))
        return lax.ppermute(value, ("dp", "seq"), pairs)

    def swap(self, value):
        return self.permute(value, "core")

    def join(self, own, other, axis):
        return jnp.where(
            self.places["core"] == 0,
            jnp.concatenate([own, other], axis),
            jnp.concatenate([other, own], axis),
        )

    def seats(self, halving):
        found = []
        for half in range(2):
            core = self.core if half == 0 else 1 - self.core
            first, second = self.coords(core)
            for s2 in range(self.n):
                for s1 in range(self.n):
                    flat = self.plane((first - s1) % self.n, (second - s2) % self.n, core)
                    for sz in range(self.nz):
                        z = self.z ^ sz if halving else (self.z - sz) % self.nz
                        found.append(z * self.n * self.n + flat)
        return jnp.stack(found).astype(jnp.int32)

    def total_small(self, value, *untils):
        steps = [("core", 0), ("first", 1), ("second", 1)] if self.n == 2 else [("core", 0)]
        if self.n != 2:
            for axis in ("first", "second"):
                value = value + sum(self.permute(value, axis, s) for s in range(1, self.n))
        bit = 1
        while bit < self.nz:
            steps.append(("zx", bit))
            bit *= 2
        for at, (axis, shift) in enumerate(steps):
            until = untils[at] if at < len(untils) else ()
            value = value + after(self.permute(value, axis, shift), *until)
        return value

    def gather_z(self, block, *until):
        return jnp.stack([block] + [after(self.permute(block, "z", s), *until) for s in range(1, self.nz)])

    def gather_bit(self, held, bit, *until):
        return jnp.concatenate([held, after(self.permute(held, "zx", bit), *until)])

    def gather_first(self, column, *until):
        return jnp.stack([column] + [after(self.permute(column, "first", s), *until) for s in range(1, self.n)])

    def gather_second(self, line, *until):
        return [after(self.permute(line, "second", s), *until) for s in range(1, self.n)]

    def scatter_first(self, own, pair, *until):
        rows, cols = own.shape[0] // self.chips, own.shape[1]
        n = self.n

        def seat(s1, s2):
            own_part, pair_part = [
                cut(part.reshape(self.nz, n * n, rows, cols), 1, self.places["plane", s1, s2]).astype(F32)
                for part in (own, pair)
            ]
            return own_part + pair_part

        kept = [seat(0, t) for t in range(n)]
        for s in range(1, n):
            send = jnp.stack([seat(s, t).astype(BF16) for t in range(n)])
            got = after(self.permute(send, "first", s), *until)
            kept = [kept[t] + got[t].astype(F32) for t in range(n)]
        return kept[0], [part.astype(BF16) for part in kept[1:]]

    def scatter_second(self, kept, *until):
        mine, rest = kept
        got = [after(self.permute(rest[s - 1], "second", s), *until) for s in range(1, self.n)]
        for part in got:
            mine = mine + part.astype(F32)
        return mine.reshape((self.nz,) + mine.shape[2:]), got

    def order_z(self, mine):
        return [cut(mine, 0, self.places["z", at])[0] for at in range(self.nz)]

    def scatter_bit(self, parts, *until):
        half = len(parts) // 2
        send = parts[half] if half == 1 else jnp.stack([part.astype(BF16) for part in parts[half:]])
        got = after(self.permute(send.astype(BF16), "zx", half), *until)
        if half == 1:
            return [parts[0] + got.astype(F32)], got
        return [part + got[at].astype(F32) for at, part in enumerate(parts[:half])], got

    def scatter_z(self, parts):
        while len(parts) > 1:
            parts, _ = self.scatter_bit(parts)
        return parts[0]


def adamw(weight, gradient, first_moment, second_moment, step_rate, weight_decay):
    first_moment = BETA_ONE * first_moment + (1.0 - BETA_ONE) * gradient
    second_moment = BETA_TWO * second_moment + (1.0 - BETA_TWO) * gradient * gradient
    first_fix = 1.0 - BETA_ONE**STEP
    second_fix = 1.0 - BETA_TWO**STEP
    direction = first_moment / first_fix / (jnp.sqrt(second_moment / second_fix) + EPS_ADAM)
    return (weight - step_rate * (direction + weight_decay * weight), first_moment, second_moment)


def local(
    block_in, lengths, out_grad, w_qkv, w_out, w_up, w_down, vectors,
    first_qkv, first_out, first_up, first_down, first_vectors,
    second_qkv, second_out, second_up, second_down, second_vectors,
):
    grid = Grid(lax.axis_size("dp"))
    core = grid.core
    w_qkv_first = grid.pin(w_qkv)
    places = grid.places
    core_arr = places["core"].reshape(1).astype(jnp.int32)
    half_len = block_in.shape[1]
    vec_count, vec_here = vectors.shape

    def own_slot(halves):
        mine, theirs = [cut(halves, 0, places[name])[0] for name in ("core", "other")]
        return grid.join(mine, grid.swap(theirs), 0)

    def both_slots(mine, got):
        zero = jnp.uint32(0)
        return lax.dynamic_update_slice(mine, got[None], (places["other"], zero, zero))

    def half_of(shard):
        width = shard.shape[1] // 2
        return jnp.where(places["core"] == 0, shard[:, :width], shard[:, width:]).astype(BF16)

    seats, q_seats = [places[name].astype(jnp.int32) for name in ("seats", "q_seats")]

    turned = jnp.pad(vectors.T.astype(BF16), ((0, 0), (0, 128 - vec_count)))
    q_block = jnp.concatenate([half_of(w_qkv_first), turned], axis=1)
    u_block = jnp.concatenate([half_of(w_out), half_of(w_up)], axis=1)
    d_block = half_of(w_down)
    q_col = grid.gather_z(q_block)
    x = own_slot(block_in)
    bits = [1 << at for at in range((grid.nz - 1).bit_length())]
    u_col, d_col = u_block[None], d_block[None]
    for bit in bits[:-1]:
        u_col = grid.gather_bit(u_col, bit)
        d_col = grid.gather_bit(d_col, bit)
    q_line = after(grid.gather_first(q_col, x), u_col, d_col)
    q_rest = grid.gather_second(q_line)
    u_col = grid.gather_bit(after(u_col, q_line), bits[-1])
    q_line_swap = grid.swap(q_line)
    q_rest_swap = [grid.swap(after(part, u_col)) for part in q_rest]
    q_group = finish_group(grid, q_seats, [q_line] + q_rest, [q_line_swap] + q_rest_swap)

    h1, qkv, vec, w_back = qkv_call(core_arr, q_seats, x, q_group)
    u_line = grid.gather_first(u_col, qkv)
    d_col = grid.gather_bit(after(d_col, u_col), bits[-1], qkv)
    og = own_slot(after(out_grad, qkv))
    att = attend_call(core_arr, lengths, after(qkv, u_line, d_col), 0, 4, ())
    u_line_swap = after(grid.swap(u_line), *att)
    u_rest = grid.gather_second(u_line, *att)
    d_col = after(d_col, *u_rest)
    a, lse = attend_call(core_arr, lengths, after(qkv, d_col), 4, 2, att)
    u_rest_swap = [after(grid.swap(part), a) for part in u_rest]
    d_line = grid.gather_first(d_col, a)
    u_group = finish_group(grid, seats, [u_line] + u_rest, [u_line_swap] + u_rest_swap)
    mid, h2, e, slope, dy, wo, wu = up_call(core_arr, lengths, seats, x, after(a, d_line), og, vec, u_group)
    d_line_swap = after(grid.swap(d_line), mid)
    d_rest = grid.gather_second(d_line, mid)
    d_own, d_other = weight_grad_call(core_arr, [(after(e, *d_rest), [dy])], 512, "grad_down")
    d_rest_swap = [after(grid.swap(part), d_own) for part in d_rest]
    d_group = finish_group(grid, seats, [d_line] + d_rest, [d_line_swap] + d_rest_swap)
    out_theirs, out_mine, dz, dmb, dm, da, acc_mid = down_call(
        core_arr, lengths, seats, mid, e, slope, dy, wo, wu, vec, d_group
    )

    d_pair = after(grid.swap(d_other), dz)
    u_own, u_other = weight_grad_call(
        core_arr, [(a, [dmb]), (h2, [after(dz, d_pair)])], 384, "grad_up"
    )
    d_kept = grid.scatter_first(d_own, d_pair, u_own)

    def back_call(start, count, before, *needs):
        return attend_back_call(core_arr, lengths, qkv, a, after(da, *needs), lse, start, count, before)

    back = back_call(0, 2, (), u_own, *d_kept[1])
    d_sum, d_here = grid.scatter_second(d_kept, *back)
    u_pair = after(grid.swap(u_other), *back)
    back = back_call(2, 4, back, u_pair, *d_here)
    d_parts, _ = grid.scatter_bit(grid.order_z(d_sum), *back)
    u_kept = grid.scatter_first(u_own, u_pair, *back)
    dq, dk, dv = back
    block_out = both_slots(out_mine, after(grid.swap(after(out_theirs, back[0])), dq))
    q_own, q_other = weight_grad_call(
        core_arr, [(h1, [after(dq, *u_kept[1]), dk, dv])], 384, "grad_qkv", "turns"
    )
    u_sum, u_here = grid.scatter_second(u_kept, q_own)
    d_mine = grid.scatter_z(d_parts)
    d_other_mine = grid.swap(d_mine)
    q_pair = after(grid.swap(q_other), *u_here)
    in_theirs, in_mine, acc = last_call(
        core_arr, x, dm, after(dq, q_own, q_pair), dk, dv, w_back, vec, acc_mid
    )
    q_kept = grid.scatter_first(q_own, q_pair, in_theirs)
    u_parts, u_got = grid.scatter_bit(grid.order_z(u_sum), *q_kept[1])
    q_sum, q_here = grid.scatter_second(q_kept, u_got)
    down_new, = adam_call(
        core_arr,
        [(d_mine, d_other_mine)],
        [(after(w_down, *q_kept[1]), first_down, second_down)],
        [(FF ** (-0.5), MATRIX_DECAY, [(0, 0, D // 2, 0, D // 2)])],
    )
    in_got = grid.swap(after(in_theirs, *q_kept[1]))
    u_mine = grid.scatter_z([after(part, *q_here) for part in u_parts])
    u_other_mine = grid.swap(u_mine)
    q_parts = grid.order_z(q_sum)
    q_gots = []
    while len(q_parts) > 1:
        q_parts, got = grid.scatter_bit(q_parts)
        q_gots.append((got,))
    q_mine = q_parts[0]
    q_other_mine = grid.swap(q_mine)
    in_grad = both_slots(in_mine, after(in_got, *q_here))
    w_qkv = after(w_qkv, in_grad)
    vec_total = grid.total_small(acc, q_kept[1], q_here, *q_gots)

    half, wide = D // 2, FF // 2
    out_new, up_new = adam_call(
        core_arr,
        [(u_mine, u_other_mine)],
        [(after(w_out, in_grad), first_out, second_out), (w_up, first_up, second_up)],
        [
            ((D // 64) ** (-0.5), MATRIX_DECAY, [(0, 0, half, 0, half)]),
            (D ** (-0.5), MATRIX_DECAY, [(0, half, wide, 0, wide)]),
        ],
    )
    moves = []
    for turn in range(3 * D // 256):
        moves.append((0, turn * 128, 128, turn * 256, turn * 256 + 128))
    qkv_new, = adam_call(
        core_arr,
        [(q_mine, q_other_mine)],
        [(w_qkv, first_qkv, second_qkv)],
        [(D ** (-0.5), MATRIX_DECAY, moves)],
    )
    vec_grad = cut(vec_total[:vec_count].reshape(vec_count, -1, vec_here), 1, places["chip"])[:, 0]
    vec_new = adamw(vectors, vec_grad, first_vectors, second_vectors, VECTOR_RATE, 0.0)
    news = [qkv_new, out_new, up_new, down_new, vec_new]
    return (block_out, in_grad) + tuple(new[kind] for kind in range(3) for new in news)


def finish_group(grid, seats, own, other):
    rows, cols = own[0].shape[-2:]
    if rows % 16 == 0:
        return Pieces(own + other, rows)
    found = []
    for half, parts in enumerate((own, other)):
        here = seats[half * grid.chips : (half + 1) * grid.chips]
        order = jnp.zeros((grid.chips,), jnp.int32).at[here].set(jnp.arange(grid.chips, dtype=jnp.int32))
        blocks = jnp.concatenate(parts).reshape(grid.chips, rows, cols)
        found.append(jnp.take(blocks, order, axis=0).reshape(1, 1, grid.chips * rows, cols))
    return Pieces(found, grid.chips * rows, True)


def solution(mesh):
    weight = P("dp", None)
    vector = P(None, "dp")
    state = (weight, weight, weight, weight, vector)
    tokens = P("dp", "seq", None)
    return jax.shard_map(
        local,
        mesh=mesh,
        in_specs=(tokens, P("dp"), tokens) + state * 3,
        out_specs=(tokens, tokens) + state * 3,
        check_vma=False,
    )
```

profile of v0, /device:TPU:0, one launch (start us, length us, event | category | flops | bytes accessed | tf_op | source)
XLA Modules:
  0.0 286.8 jit_solution(15358232262964715590)
XLA Ops:
  3.2 4.1 %collective-permute-start.2 = (bf16[48,1280]{1,0:T(8,128)(2,1)S(1)}, bf16[48,1280]{1,0:T(8,128)(2,1)S(1)}, u32[]{:S(2)}, u32[]{:S(2)}) collective-permute-start(bf16[48,1280]{1,0:T(8,128)(2,1)S(1)} %get-tuple-element.263), channel_id=1, source_target_pairs={{0,16},{1,17},{2,18},{3,19},{4,20},{5,21},{6,22},{7,23},{8,24},{9,... | collective-permute-start | bytes 368648 | tf_op jit(solution)/shard_map/ppermute | solution.py:834
  13.0 3.8 %collective-permute-done.2 = bf16[48,1280]{1,0:T(8,128)(2,1)S(1)} collective-permute-done((bf16[48,1280]{1,0:T(8,128)(2,1)S(1)}, bf16[48,1280]{1,0:T(8,128)(2,1)S(1)}, u32[]{:S(2)}, u32[]{:S(2)}) %collective-permute-start.2) | collective-permute-done | bytes 122912 | tf_op jit(solution)/shard_map/ppermute | solution.py:834
  25.3 2.9 collective-permute-done.4
  32.6 14.7 %collective-permute-done.9 = bf16[2,48,1920]{2,1,0:T(8,128)(2,1)S(1)} collective-permute-done((bf16[2,48,1920]{2,1,0:T(8,128)(2,1)S(1)}, bf16[2,48,1920]{2,1,0:T(8,128)(2,1)S(1)}, u32[]{:S(2)}, u32[]{:S(2)}) %collective-permute-start.9) | collective-permute-done | bytes 368672 | tf_op jit(solution)/shard_map/ppermute | solution.py:834
  50.8 9.1 %qkv.1 = (bf16[1024,768]{1,0:T(8,128)(2,1)S(1)}, bf16[1024,2304]{1,0:T(8,128)(2,1)S(1)}, f32[16,768]{1,0:T(8,128)S(1)}, bf16[2304,768]{1,0:T(8,128)(2,1)S(1)}) custom-call(s32[1]{0:T(128)} %bitcast.64.core_ref, s32[32]{0:T(128)S(1)} %convert_element_type.410.seat_ref, bf16[1024,768]{1,0:T(8,128)(2,1)S(1)} %maximum_select_fusion.x_ref, ...), custom_call_target="tpu_custom_call" | custom-call | flops 14495514624 | bytes 40000000 | tf_op jit(solution)/shard_map/qkv/pallas_call | solution.py:161
  67.3 8.9 %attend.2 = (bf16[1024,768]{1,0:T(8,128)(2,1)S(1)}, f32[6,8,1024]{2,1,0:T(8,128)S(1)}) custom-call(s32[1]{0:T(128)} %bitcast.64.core_ref, s32[2]{0:T(128)S(1)} %copy-done.17, bf16[1024,2304]{1,0:T(8,128)(2,1)S(1)} %get-tuple-element.147.qkv_ref.q_ref.k_ref.v_ref), custom_call_target="tpu_custom_call" | custom-call | flops 48000000000 | bytes 19200000 | tf_op jit(solution)/shard_map/attend/pallas_call | solution.py:274
  78.0 6.4 %collective-permute-done.13.refs_1_ = bf16[2,4,48,1920]{3,2,1,0:T(8,128)(2,1)S(1)} collective-permute-done((bf16[2,4,48,1920]{3,2,1,0:T(8,128)(2,1)S(1)}, bf16[2,4,48,1920]{3,2,1,0:T(8,128)(2,1)S(1)}, u32[]{:S(2)}, u32[]{:S(2)}) %collective-permute-start.13) | collective-permute-done | bytes 1474592 | tf_op jit(solution)/shard_map/ppermute | solution.py:834
  85.1 4.8 %attend.3 = (bf16[1024,768]{1,0:T(8,128)(2,1)S(1)}, f32[6,8,1024]{2,1,0:T(8,128)S(1)}) custom-call(s32[1]{0:T(128)} %bitcast.64.core_ref, s32[2]{0:T(128)S(1)} %copy-done.17, bf16[1024,2304]{1,0:T(8,128)(2,1)S(1)} %get-tuple-element.147.qkv_ref.q_ref.k_ref.v_ref, ...), custom_call_target="tpu_custom_call", output_to_operand_aliasing={{0}: (3, {}), {1}: (4, {})} | custom-call | flops 24000000000 | bytes 9600000 | tf_op jit(solution)/shard_map/attend/pallas_call | solution.py:274
  89.9 4.3 %collective-permute-done.14 = bf16[4,192,384]{2,1,0:T(8,128)(2,1)S(1)} collective-permute-done((bf16[4,192,384]{2,1,0:T(8,128)(2,1)S(1)}, bf16[4,192,384]{2,1,0:T(8,128)(2,1)S(1)}, u32[]{:S(2)}, u32[]{:S(2)}) %collective-permute-start.14) | collective-permute-done | bytes 589856 | tf_op jit(solution)/shard_map/ppermute | solution.py:834
  97.2 21.2 %up.1 = (f32[1024,768]{1,0:T(8,128)}, bf16[1024,768]{1,0:T(8,128)(2,1)}, bf16[1024,3072]{1,0:T(8,128)(2,1)}, bf16[1024,3072]{1,0:T(8,128)(2,1)}, bf16[1024,768]{...) custom-call(s32[1]{0:T(128)} %bitcast.64.core_ref, s32[2]{0:T(128)S(1)} %copy-done.17, ...), custom_call_target="tpu_custom_call" | custom-call | flops 24000000000 | bytes 120000000 | tf_op jit(solution)/shard_map/up/pallas_call | solution.py:468
  119.9 9.5 %grad_down.1 = (bf16[3072,384]{1,0:T(8,128)(2,1)S(1)}, bf16[3072,384]{1,0:T(8,128)(2,1)}) custom-call(s32[1]{0:T(128)} %bitcast.64.core_ref, bf16[1024,3072]{1,0:T(8,128)(2,1)} %get-tuple-element.163.refs_0_.e_ref, bf16[1024,768]{1,0:T(8,128)(2,1)S(1)} %copy-done.24), custom_call_target="tpu_custom_call" | custom-call | flops 19327352832 | bytes 50331648 | tf_op jit(solution)/shard_map/grad_down/pallas_call | solution.py:636
  130.9 33.2 %down.1 = (bf16[512,768]{1,0:T(8,128)(2,1)S(1)}, bf16[2,512,768]{2,1,0:T(8,128)(2,1)}, bf16[1024,3072]{1,0:T(8,128)(2,1)}, bf16[1024,768]{1,0:T(8,128)(2,1)}, f3...) custom-call(s32[1]{0:T(128)} %bitcast.64.core_ref, s32[2]{0:T(128)S(1)} %copy-done.17, ...), custom_call_target="tpu_custom_call" | custom-call | flops 64000000000 | bytes 140000000 | tf_op jit(solution)/shard_map/down/pallas_call | solution.py:566
  167.4 11.8 %grad_up.1 = (bf16[768,1920]{1,0:T(8,128)(2,1)}, bf16[768,1920]{1,0:T(8,128)(2,1)}) custom-call(s32[1]{0:T(128)} %bitcast.64.core_ref, bf16[1024,768]{1,0:T(8,128)(2,1)S(1)} %copy-done.27, bf16[1024,768]{1,0:T(8,128)(2,1)S(1)} %copy-done.25, bf16[1024,768]{1,0:T(8,128)(2,1)S(1)} %copy-done.28, bf16[1024,3072]{1,0:T(8,128)(2,1)} %get-tuple-element.174.refs_3_), custom_call_target="tpu_custom_call" | custom-call | flops 24159191040 | bytes 61341696 | tf_op jit(solution)/shard_map/grad_up/pallas_call | solution.py:636
  179.3 2.6 collective-permute-done.23
  184.2 8.4 %attend_back.2 = (bf16[1024,768]{1,0:T(8,128)(2,1)S(1)}, bf16[1024,768]{1,0:T(8,128)(2,1)S(1)}, bf16[1024,768]{1,0:T(8,128)(2,1)S(1)}) custom-call(s32[1]{0:T(128)} %bitcast.64.core_ref, s32[2]{0:T(128)S(1)} %copy-done.17, bf16[1024,2304]{1,0:T(8,128)(2,1)S(1)} %bitcast.236, bf16[1024,2304]{1,0:T(8,128)(2,1)S(1)} %bitcast.236, ...), custom_call_target="tpu_custom_call" | custom-call | flops 48000000000 | bytes 16000000 | tf_op jit(solution)/shard_map/attend_back/pallas_call | solution.py:371
  199.2 15.4 %attend_back.3 = (bf16[1024,768]{1,0:T(8,128)(2,1)S(1)}, bf16[1024,768]{1,0:T(8,128)(2,1)S(1)}, bf16[1024,768]{1,0:T(8,128)(2,1)S(1)}) custom-call(s32[1]{0:T(128)} %bitcast.64.core_ref, s32[2]{0:T(128)S(1)} %copy-done.17, bf16[1024,2304]{1,0:T(8,128)(2,1)S(1)} %bitcast.236, ...), custom_call_target="tpu_custom_call", output_to_operand_aliasing={{0}: (8, {}), {1}: (9, {}), {2}: (10, {})} | custom-call | flops 96000000000 | bytes 32000000 | tf_op jit(solution)/shard_map/attend_back/pallas_call | solution.py:371
  218.7 4.9 %grad_qkv.1 = (bf16[768,1152]{1,0:T(8,128)(2,1)S(1)}, bf16[768,1152]{1,0:T(8,128)(2,1)S(1)}) custom-call(s32[1]{0:T(128)} %bitcast.64.core_ref, bf16[1024,768]{1,0:T(8,128)(2,1)S(1)} %copy-done.23, bf16[1024,768]{1,0:T(8,128)(2,1)S(1)} %get-tuple-element.202.refs_1_.dq_ref, bf16[1024,768]{1,0:T(8,128)(2,1)S(1)} %get-tuple-element.194.refs_2_.dk_ref, ...), custom_call_target="tpu_custom_call" | custom-call | flops 14495514624 | bytes 39321600 | tf_op jit(solution)/shard_map/grad_qkv/pallas_call | solution.py:636
  223.7 6.2 %collective-permute-done.39 = bf16[192,384]{1,0:T(8,128)(2,1)S(1)} collective-permute-done((bf16[192,384]{1,0:T(8,128)(2,1)S(1)}, bf16[192,384]{1,0:T(8,128)(2,1)S(1)}, u32[]{:S(2)}, u32[]{:S(2)}) %collective-permute-start.39) | collective-permute-done | bytes 147488 | tf_op jit(solution)/shard_map/ppermute | solution.py:834
  234.4 7.1 %last.1 = (f32[512,768]{1,0:T(8,128)S(1)}, f32[2,512,768]{2,1,0:T(8,128)}, f32[16,768]{1,0:T(8,128)S(1)}) custom-call(s32[1]{0:T(128)} %bitcast.64.core_ref, bf16[1024,768]{1,0:T(8,128)(2,1)S(1)} %copy-done.1, f32[1024,768]{1,0:T(8,128)S(1)} %copy-done.21, bf16[1024,768]{1,0:T(8,128)(2,1)S(1)} %get-tuple-element.202.refs_1_.dq_ref, ...), custom_call_target="tpu_custom_call" | custom-call | flops 14495514624 | bytes 64000000 | tf_op jit(solution)/shard_map/last/pallas_call | solution.py:700
  241.9 3.4 %collective-permute-done.29 = bf16[2,4,1,48,1152]{4,3,1,2,0:T(8,128)(2,1)S(1)} collective-permute-done((bf16[2,4,1,48,1152]{4,3,1,2,0:T(8,128)(2,1)S(1)}, bf16[2,4,1,48,1152]{4,3,1,2,0:T(8,128)(2,1)S(1)}, u32[]{:S(2)}, u32[]{:S(2)}) %collective-permute-start.29) | collective-permute-done | bytes 884768 | tf_op jit(solution)/shard_map/ppermute | solution.py:834
  247.0 4.0 %collective-permute-done.32 = bf16[2,48,1920]{2,1,0:T(8,128)(2,1)S(1)} collective-permute-done((bf16[2,48,1920]{2,1,0:T(8,128)(2,1)S(1)}, bf16[2,48,1920]{2,1,0:T(8,128)(2,1)S(1)}, u32[]{:S(2)}, u32[]{:S(2)}) %collective-permute-start.32) | collective-permute-done | bytes 368672 | tf_op jit(solution)/shard_map/ppermute | solution.py:834
  260.1 6.8 %collective-permute-done.33 = bf16[2,48,1152]{2,1,0:T(8,128)(2,1)S(1)} collective-permute-done((bf16[2,48,1152]{2,1,0:T(8,128)(2,1)S(1)}, bf16[2,48,1152]{2,1,0:T(8,128)(2,1)S(1)}, u32[]{:S(2)}, u32[]{:S(2)}) %collective-permute-start.33) | collective-permute-done | bytes 221216 | tf_op jit(solution)/shard_map/ppermute | solution.py:834
  274.7 4.5 %collective-permute-done.45 = f32[16,768]{1,0:T(8,128)S(1)} collective-permute-done((f32[16,768]{1,0:T(8,128)S(1)}, f32[16,768]{1,0:T(8,128)S(1)}, u32[]{:S(2)}, u32[]{:S(2)}) %collective-permute-start.45) | collective-permute-done | bytes 49184 | tf_op jit(solution)/shard_map/ppermute | solution.py:834
  280.1 2.8 bitcast_dynamic-update-slice_fusion
  (238 shorter events, 84.0 us)
Async XLA Ops:
  3.2 13.6 %collective-permute-start.2 = (bf16[48,1280]{1,0:T(8,128)(2,1)S(1)}, bf16[48,1280]{1,0:T(8,128)(2,1)S(1)}, u32[]{:S(2)}, u32[]{:S(2)}) collective-permute-start(bf16[48,1280]{1,0:T(8,128)(2,1)S(1)} %get-tuple-element.263), channel_id=1, source_target_pairs={{0,16},{1,17},{2,18},{3,19},{4,20},{5,21},{6,22},{7,23},{8,24},{9,... | collective-permute-start | bytes 368648 | tf_op jit(solution)/shard_map/ppermute | solution.py:834
  12.8 11.8 %collective-permute-start = (bf16[512,768]{1,0:T(8,128)(2,1)S(1)}, bf16[512,768]{1,0:T(8,128)(2,1)S(1)}, u32[]{:S(2)}, u32[]{:S(2)}) collective-permute-start(bf16[512,768]{1,0:T(8,128)(2,1)S(1)} %get-tuple-element.253), channel_id=1, source_target_pairs={{0,1},{1,0},{2,3},{3,2},{4,5},{5,4},{6,7},{7,6},{8,9},{9,8},{10,11... | collective-permute-start | bytes 2359304 | tf_op jit(solution)/shard_map/ppermute | solution.py:834
  28.3 19.8 %collective-permute-start.7 = (bf16[2,4,48,1280]{3,2,1,0:T(8,128)(2,1)S(1)}, bf16[2,4,48,1280]{3,2,1,0:T(8,128)(2,1)S(1)}, u32[]{:S(2)}, u32[]{:S(2)}) collective-permute-start(bf16[2,4,48,1280]{3,2,1,0:T(8,128)(2,1)S(1)} %pad_maximum_fusion.4.refs_0_), channel_id=1, source_target_pairs={{0,4},{1,3},{2,6},{3,1},{4,0},{5,7},{6,2},{7,5},{8,12},{9,11},{10,... | collective-permute-start | bytes 2949128 | tf_op jit(solution)/shard_map/ppermute | solution.py:834
  29.9 17.4 %collective-permute-start.9 = (bf16[2,48,1920]{2,1,0:T(8,128)(2,1)S(1)}, bf16[2,48,1920]{2,1,0:T(8,128)(2,1)S(1)}, u32[]{:S(2)}, u32[]{:S(2)}) collective-permute-start(bf16[2,48,1920]{2,1,0:T(8,128)(2,1)S(1)} %pad_maximum_fusion.7), channel_id=1, source_target_pairs={{0,16},{1,17},{2,18},{3,19},{4,20},{5,21},{6,22},{7,23},{8,24},{9,... | collective-permute-start | bytes 1105928 | tf_op jit(solution)/shard_map/ppermute | solution.py:834
  31.8 17.9 %collective-permute-start.8 = (bf16[2,4,48,1280]{3,2,1,0:T(8,128)(2,1)S(1)}, bf16[2,4,48,1280]{3,2,1,0:T(8,128)(2,1)}, u32[]{:S(2)}, u32[]{:S(2)}) collective-permute-start(bf16[2,4,48,1280]{3,2,1,0:T(8,128)(2,1)S(1)} %pad_maximum_fusion.4.refs_0_), channel_id=1, source_target_pairs={{0,1},{1,0},{2,3},{3,2},{4,5},{5,4},{6,7},{7,6},{8,9},{9,8},{10,11... | collective-permute-start | bytes 2949128 | tf_op jit(solution)/shard_map/ppermute | solution.py:834
  48.1 14.7 %collective-permute-start.12 = (bf16[4,48,1920]{2,1,0:T(8,128)(2,1)}, bf16[4,48,1920]{2,1,0:T(8,128)(2,1)S(1)}, u32[]{:S(2)}, u32[]{:S(2)}) collective-permute-start(bf16[4,48,1920]{2,1,0:T(8,128)(2,1)} %constant_dynamic-update-slice_fusion), channel_id=1, source_target_pairs={{0,2},{1,5},{2,0},{3,7},{4,6},{5,1},{6,4},{7,3},{8,10},{9,13},{10,... | collective-permute-start | bytes 2211848 | tf_op jit(solution)/shard_map/ppermute | solution.py:834
  48.7 17.8 %collective-permute-start.11 = (bf16[2,192,384]{2,1,0:T(8,128)(2,1)}, bf16[2,192,384]{2,1,0:T(8,128)(2,1)S(1)}, u32[]{:S(2)}, u32[]{:S(2)}) collective-permute-start(bf16[2,192,384]{2,1,0:T(8,128)(2,1)} %pad_maximum_fusion.9), channel_id=1, source_target_pairs={{0,16},{1,17},{2,18},{3,19},{4,20},{5,21},{6,22},{7,23},{8,24},{9,... | collective-permute-start | bytes 884744 | tf_op jit(solution)/shard_map/ppermute | solution.py:834
  64.8 20.3 %collective-permute-start.16 = (bf16[2,4,48,1920]{3,2,1,0:T(8,128)(2,1)S(1)}, bf16[2,4,48,1920]{3,2,1,0:T(8,128)(2,1)S(1)}, u32[]{:S(2)}, u32[]{:S(2)}) collective-permute-start(bf16[2,4,48,1920]{3,2,1,0:T(8,128)(2,1)S(1)} %pad_maximum_fusion.refs_0_), channel_id=1, source_target_pairs={{0,1},{1,0},{2,3},{3,2},{4,5},{5,4},{6,7},{7,6},{8,9},{9,8},{10,11... | collective-permute-start | bytes 4423688 | tf_op jit(solution)/shard_map/ppermute | solution.py:834
  65.0 19.4 %collective-permute-start.13 = (bf16[2,4,48,1920]{3,2,1,0:T(8,128)(2,1)S(1)}, bf16[2,4,48,1920]{3,2,1,0:T(8,128)(2,1)S(1)}, u32[]{:S(2)}, u32[]{:S(2)}) collective-permute-start(bf16[2,4,48,1920]{3,2,1,0:T(8,128)(2,1)S(1)} %pad_maximum_fusion.refs_0_), channel_id=1, source_target_pairs={{0,4},{1,3},{2,6},{3,1},{4,0},{5,7},{6,2},{7,5},{8,12},{9,11},{10,... | collective-permute-start | bytes 4423688 | tf_op jit(solution)/shard_map/ppermute | solution.py:834
  94.4 24.0 %collective-permute-start.19 = (bf16[2,4,192,384]{3,2,1,0:T(8,128)(2,1)S(1)}, bf16[2,4,192,384]{3,2,1,0:T(8,128)(2,1)S(1)}, u32[]{:S(2)}, u32[]{:S(2)}) collective-permute-start(bf16[2,4,192,384]{3,2,1,0:T(8,128)(2,1)S(1)} %pad_maximum_fusion.2.refs_0_), channel_id=1, source_target_pairs={{0,1},{1,0},{2,3},{3,2},{4,5},{5,4},{6,7},{7,6},{8,9},{9,8},{10,11... | collective-permute-start | bytes 3538952 | tf_op jit(solution)/shard_map/ppermute | solution.py:834
  94.5 23.9 %collective-permute-start.18 = (bf16[2,4,192,384]{3,2,1,0:T(8,128)(2,1)S(1)}, bf16[2,4,192,384]{3,2,1,0:T(8,128)(2,1)S(1)}, u32[]{:S(2)}, u32[]{:S(2)}) collective-permute-start(bf16[2,4,192,384]{3,2,1,0:T(8,128)(2,1)S(1)} %pad_maximum_fusion.2.refs_0_), channel_id=1, source_target_pairs={{0,4},{1,3},{2,6},{3,1},{4,0},{5,7},{6,2},{7,5},{8,12},{9,11},{10,... | collective-permute-start | bytes 3538952 | tf_op jit(solution)/shard_map/ppermute | solution.py:834
  118.4 11.5 %collective-permute-start.20 = (bf16[2,4,192,384]{3,2,1,0:T(8,128)(2,1)S(1)}, bf16[2,4,192,384]{3,2,1,0:T(8,128)(2,1)S(1)}, u32[]{:S(2)}, u32[]{:S(2)}) collective-permute-start(bf16[2,4,192,384]{3,2,1,0:T(8,128)(2,1)S(1)} %collective-permute-done.18.refs_1_), channel_id=1, source_target_pairs={{0,1},{1,0},{2,3},{3,2},{4,5},{5,4},{6,7},{7,6},{8,9},{9,8},{10,11... | collective-permute-start | bytes 3538952 | tf_op jit(solution)/shard_map/ppermute | solution.py:834
  129.4 34.7 %collective-permute-start.21 = (bf16[3072,384]{1,0:T(8,128)(2,1)}, bf16[3072,384]{1,0:T(8,128)(2,1)S(1)}, u32[]{:S(2)}, u32[]{:S(2)}) collective-permute-start(bf16[3072,384]{1,0:T(8,128)(2,1)} %get-tuple-element.172), channel_id=1, source_target_pairs={{0,1},{1,0},{2,3},{3,2},{4,5},{5,4},{6,7},{7,6},{8,9},{9,8},{10,11... | collective-permute-start | bytes 7077896 | tf_op jit(solution)/shard_map/ppermute | solution.py:834
  165.6 16.3 %collective-permute-start.23 = (bf16[2,4,1,192,384]{4,3,1,2,0:T(8,128)(2,1)S(1)}, bf16[2,4,1,192,384]{4,3,1,2,0:T(8,128)(2,1)S(1)}, u32[]{:S(2)}, u32[]{:S(2)}) collective-permute-start(bf16[2,4,1,192,384]{4,3,1,2,0:T(8,128)(2,1)S(1)} %pad_maximum_fusion.3), channel_id=1, source_target_pairs={{0,2},{1,5},{2,0},{3,7},{4,6},{5,1},{6,4},{7,3},{8,10},{9,13},{10,... | collective-permute-start | bytes 3538952 | tf_op jit(solution)/shard_map/ppermute | solution.py:834
  179.2 17.8 %collective-permute-start.22 = (bf16[768,1920]{1,0:T(8,128)(2,1)}, bf16[768,1920]{1,0:T(8,128)(2,1)S(1)}, u32[]{:S(2)}, u32[]{:S(2)}) collective-permute-start(bf16[768,1920]{1,0:T(8,128)(2,1)} %get-tuple-element.175), channel_id=1, source_target_pairs={{0,1},{1,0},{2,3},{3,2},{4,5},{5,4},{6,7},{7,6},{8,9},{9,8},{10,11... | collective-permute-start | bytes 8847368 | tf_op jit(solution)/shard_map/ppermute | solution.py:834
  195.1 19.4 %collective-permute-start.38 = (bf16[2,192,384]{2,1,0:T(8,128)(2,1)S(1)}, bf16[2,192,384]{2,1,0:T(8,128)(2,1)S(1)}, u32[]{:S(2)}, u32[]{:S(2)}) collective-permute-start(bf16[2,192,384]{2,1,0:T(8,128)(2,1)S(1)} %pad_maximum_fusion.10), channel_id=1, source_target_pairs={{0,16},{1,17},{2,18},{3,19},{4,20},{5,21},{6,22},{7,23},{8,24},{9,... | collective-permute-start | bytes 884744 | tf_op jit(solution)/shard_map/ppermute | solution.py:834
  197.6 19.4 %collective-permute-start.26 = (bf16[2,4,1,48,1920]{4,3,1,2,0:T(8,128)(2,1)S(1)}, bf16[2,4,1,48,1920]{4,3,1,2,0:T(8,128)(2,1)S(1)}, u32[]{:S(2)}, u32[]{:S(2)}) collective-permute-start(bf16[2,4,1,48,1920]{4,3,1,2,0:T(8,128)(2,1)S(1)} %pad_maximum_fusion.1), channel_id=1, source_target_pairs={{0,2},{1,5},{2,0},{3,7},{4,6},{5,1},{6,4},{7,3},{8,10},{9,13},{10,... | collective-permute-start | bytes 4423688 | tf_op jit(solution)/shard_map/ppermute | solution.py:834
  214.6 15.5 %collective-permute-start.25 = (bf16[512,768]{1,0:T(8,128)(2,1)S(1)}, bf16[512,768]{1,0:T(8,128)(2,1)S(1)}, u32[]{:S(2)}, u32[]{:S(2)}) collective-permute-start(bf16[512,768]{1,0:T(8,128)(2,1)S(1)} %get-tuple-element.190), channel_id=1, source_target_pairs={{0,1},{1,0},{2,3},{3,2},{4,5},{5,4},{6,7},{7,6},{8,9},{9,8},{10,11... | collective-permute-start | bytes 2359304 | tf_op jit(solution)/shard_map/ppermute | solution.py:834
  217.3 12.9 %collective-permute-start.28 = (bf16[4,1,48,1920]{3,2,1,0:T(8,128)(2,1)S(1)}, bf16[4,1,48,1920]{3,2,1,0:T(8,128)(2,1)S(1)}, u32[]{:S(2)}, u32[]{:S(2)}) collective-permute-start(bf16[4,1,48,1920]{3,2,1,0:T(8,128)(2,1)S(1)} %fusion.2), channel_id=1, source_target_pairs={{0,4},{1,3},{2,6},{3,1},{4,0},{5,7},{6,2},{7,5},{8,12},{9,11},{10,... | collective-permute-start | bytes 2211848 | tf_op jit(solution)/shard_map/ppermute | solution.py:834
  230.0 28.2 %collective-permute-start.40 = (f32[192,384]{1,0:T(8,128)S(1)}, f32[192,384]{1,0:T(8,128)S(1)}, u32[]{:S(2)}, u32[]{:S(2)}) collective-permute-start(f32[192,384]{1,0:T(8,128)S(1)} %fusion.16.refs_0_), channel_id=1, source_target_pairs={{0,1},{1,0},{2,3},{3,2},{4,5},{5,4},{6,7},{7,6},{8,9},{9,8},{10,11... | collective-permute-start | bytes 884744 | tf_op jit(solution)/shard_map/ppermute | solution.py:834
  231.4 19.6 %collective-permute-start.32 = (bf16[2,48,1920]{2,1,0:T(8,128)(2,1)S(1)}, bf16[2,48,1920]{2,1,0:T(8,128)(2,1)S(1)}, u32[]{:S(2)}, u32[]{:S(2)}) collective-permute-start(bf16[2,48,1920]{2,1,0:T(8,128)(2,1)S(1)} %pad_maximum_fusion.8), channel_id=1, source_target_pairs={{0,16},{1,17},{2,18},{3,19},{4,20},{5,21},{6,22},{7,23},{8,24},{9,... | collective-permute-start | bytes 1105928 | tf_op jit(solution)/shard_map/ppermute | solution.py:834
  232.2 13.1 %collective-permute-start.29 = (bf16[2,4,1,48,1152]{4,3,1,2,0:T(8,128)(2,1)S(1)}, bf16[2,4,1,48,1152]{4,3,1,2,0:T(8,128)(2,1)S(1)}, u32[]{:S(2)}, u32[]{:S(2)}) collective-permute-start(bf16[2,4,1,48,1152]{4,3,1,2,0:T(8,128)(2,1)S(1)} %pad_maximum_fusion.5), channel_id=1, source_target_pairs={{0,2},{1,5},{2,0},{3,7},{4,6},{5,1},{6,4},{7,3},{8,10},{9,13},{10,... | collective-permute-start | bytes 2654216 | tf_op jit(solution)/shard_map/ppermute | solution.py:834
  258.2 21.9 %collective-permute-start.30 = (f32[512,768]{1,0:T(8,128)S(1)}, f32[512,768]{1,0:T(8,128)}, u32[]{:S(2)}, u32[]{:S(2)}) collective-permute-start(f32[512,768]{1,0:T(8,128)S(1)} %get-tuple-element.208), channel_id=1, source_target_pairs={{0,1},{1,0},{2,3},{3,2},{4,5},{5,4},{6,7},{7,6},{8,9},{9,8},{10,11... | collective-permute-start | bytes 4718600 | tf_op jit(solution)/shard_map/ppermute | solution.py:834
  270.9 13.3 %collective-permute-start.37 = (f32[48,1920]{1,0:T(8,128)S(1)}, f32[48,1920]{1,0:T(8,128)S(1)}, u32[]{:S(2)}, u32[]{:S(2)}) collective-permute-start(f32[48,1920]{1,0:T(8,128)S(1)} %convert_add_fusion.8.refs_0_), channel_id=1, source_target_pairs={{0,1},{1,0},{2,3},{3,2},{4,5},{5,4},{6,7},{7,6},{8,9},{9,8},{10,11... | collective-permute-start | bytes 1105928 | tf_op jit(solution)/shard_map/ppermute | solution.py:834
  (68 other events, 516.6 us)
where the time goes:
time: 290 us; the launch traced here: 287 us
  Pallas kernels  139 us (48%)
  waiting for transfers between devices  77.3 us (27%)
  starting transfers between devices  35.5 us (12%)
  local copies, waits for them, and re-layouts  19.2 us (7%)
  other arithmetic  14.1 us (5%)
    ppermute x46, waiting for transfers between devices, permute(): return lax.ppermute(value, ('dp', 'seq'), pairs)  77.3 us
    ppermute x46, starting transfers between devices, permute(): return lax.ppermute(value, ('dp', 'seq'), pairs)  35.5 us
    pallas_call x1, Pallas kernels, down_call(): pl.pallas_call(functools.partial(down_kernel, group), name='down', grid_s...  33.2 us
    pallas_call x3, Pallas kernels, weight_grad_call(): pl.pallas_call(functools.partial(weight_grad_kernel, len(lefts), [len(gro...  26.2 us
    pallas_call x2, Pallas kernels, attend_back_call(): pl.pallas_call(attend_back_kernel, name='attend_back', grid_spec=pltpu.Pr...  23.8 us
    pallas_call x1, Pallas kernels, up_call(): pl.pallas_call(functools.partial(up_kernel, group), name='up', grid_spec=...  21.2 us
    pallas_call x2, Pallas kernels, attend_call(): pl.pallas_call(functools.partial(attend_kernel, first), name='attend', gr...  13.7 us
    unnamed x94, local copies, waits for them, and re-layouts  13.4 us
  transfers between devices with their start and end apart: 46, of which 22 were waited for; matrix products, arithmetic and copies ran while one was open for 7% of the time, Pallas kernels for 48%

commit v1 on v0

--- a/solution.py
+++ b/solution.py
@@ -412,9 +412,7 @@
 
 
 def up_kernel(group, core_ref, len_ref, seat_ref, x_ref, a_ref, og_ref, vec_ref, *refs):
-    refs, (
-        mid_ref, h_ref, e_ref, slope_ref, dy_ref, wo_back_ref, wu_back_ref, wo_ref, wu_ref, sems,
-    ) = refs[:-10], refs[-10:]
+    refs, (mid_ref, h_ref, e_ref, slope_ref, dy_ref, wo_ref, wu_ref, sems) = refs[:-8], refs[-8:]
     block = x_ref.shape[0]
 
     @pl.when(pl.program_id(0) == 0)
@@ -443,13 +441,6 @@
         slope = half + act * (1.0 - turned) * (GELU_ROOT + (3.0 * GELU_ROOT * GELU_CUBE) * squared)
         slope_ref[:, cols] = slope.astype(BF16)
 
-    quarter = at_rows(D)
-    wu_back_ref[...] = wu_ref[:, quarter].T
-
-    @pl.when(pl.program_id(0) == 0)
-    def _():
-        wo_back_ref[...] = wo_ref[...].T
-
     waiting = None
     for j in range(FF // D):
         z = mm(h, wu_ref[:, j * D : (j + 1) * D])
@@ -461,7 +452,6 @@
 
 def up_call(core, lengths, seats, x, a, og, vec, group, block=256):
     rows = x.shape[0]
-    assert rows // block == FF // D
     row_spec = pl.BlockSpec((block, D), lambda i, *s: (i, 0))
     wide_spec = pl.BlockSpec((block, FF), lambda i, *s: (i, 0))
     low, wide = [jax.ShapeDtypeStruct((rows, width), BF16) for width in (D, FF)]
@@ -472,11 +462,7 @@
             num_scalar_prefetch=3,
             grid=(rows // block,),
             in_specs=[row_spec, row_spec, row_spec, whole_spec(vec.shape)] + group.specs(),
-            out_specs=[
-                row_spec, row_spec, wide_spec, wide_spec, row_spec,
-                pl.BlockSpec((D, D), lambda i, *s: (0, 0)),
-                pl.BlockSpec((D, D), lambda i, *s: (i, 0)),
-            ],
+            out_specs=[row_spec, row_spec, wide_spec, wide_spec, row_spec],
             scratch_shapes=[
                 pltpu.VMEM((D, D), BF16),
                 pltpu.VMEM((D, FF), BF16),
@@ -489,31 +475,28 @@
             wide,
             wide,
             low,
-            jax.ShapeDtypeStruct((D, D), BF16),
-            jax.ShapeDtypeStruct((FF, D), BF16),
         ],
         compiler_params=params(48),
         cost_estimate=cost(6e9, 30e6, rows * FF),
     )(core, lengths, seats, x, a, og, vec, *group.arrays)
 
 
-def down_kernel(
-    group, core_ref, len_ref, seat_ref, mid_ref, e_ref, slope_ref, dy_ref, wo_back_ref, wu_back_ref, vec_ref, *refs
-):
-    refs, (
-        theirs_ref, mine_ref, dz_ref, dmb_ref, dm_ref, da_ref, acc_ref, wd_ref, wd_back_ref, sems,
-    ) = refs[:-10], refs[-10:]
+def down_kernel(up_group, down_group, core_ref, len_ref, seat_ref, mid_ref, e_ref, slope_ref, dy_ref, vec_ref, *refs):
+    count = len(up_group.arrays)
+    up_refs, down_refs = refs[:count], refs[count : count + len(down_group.arrays)]
+    (
+        theirs_ref, mine_ref, dz_ref, dmb_ref, dm_ref, da_ref, acc_ref, wo_ref, wu_ref, wd_ref, sems,
+    ) = refs[-11:]
     block = da_ref.shape[0]
     step, steps = pl.program_id(0), pl.num_programs(0)
 
     @pl.when(step == 0)
     def _():
-        group.start(refs, core_ref, seat_ref, 0, D // 2, wd_ref, sems.at[0])
+        down_group.start(down_refs, core_ref, seat_ref, 0, D // 2, wd_ref, sems.at[2])
+        up_group.start(up_refs, core_ref, seat_ref, D // 2, FF // 2, wu_ref, sems.at[1])
+        up_group.start(up_refs, core_ref, seat_ref, 0, D // 2, wo_ref, sems.at[0])
         acc_ref[...] = jnp.zeros_like(acc_ref)
-        wait_all(wd_ref, sems.at[0])
-        for j in range(FF // D):
-            cols = slice(j * D, (j + 1) * D)
-            wd_back_ref[:, cols] = wd_ref[cols, :].T
+        wait_all(wd_ref, sems.at[2])
 
     mid = mid_ref[...]
     down = vec_ref[7:8, :] + mid + mm(e_ref[...], wd_ref[...])
@@ -527,6 +510,11 @@
     @pl.when(step >= steps // 2)
     def _():
         mine_ref[0] = down
+
+    @pl.when(step == 0)
+    def _():
+        wait_all(wu_ref, sems.at[1])
+        wait_all(wo_ref, sems.at[0])
 
     dy = dy_ref[...]
     add_row(acc_ref, 7, dy.astype(F32))
@@ -535,14 +523,14 @@
     for j in range(FF // D + 1):
         later = None
         if j < FF // D:
-            later = (j, mm(dy, wd_back_ref[:, j * D : (j + 1) * D]))
+            later = (j, mm(dy, wd_ref[j * D : (j + 1) * D, :], NT))
         if waiting is not None:
             at, de = waiting
             cols = slice(at * D, (at + 1) * D)
             dz = (de * slope_ref[:, cols].astype(F32)).astype(BF16)
             dz_ref[:, cols] = dz
             add_row(acc_ref, 8 + at, dz.astype(F32))
-            part = mm(dz, wu_back_ref[cols, :])
+            part = mm(dz, wu_ref[:, cols], NT)
             dh = part if dh is None else dh + part
         waiting = later
     normed, scale = norm_parts(mid)
@@ -553,10 +541,10 @@
     dm_low = dm.astype(BF16)
     dmb_ref[...] = dm_low
     add_row(acc_ref, 4, dm_low.astype(F32))
-    da_ref[...] = mm(dm_low, wo_back_ref[...]).astype(BF16)
-
-
-def down_call(core, lengths, seats, mid, e, slope, dy, wo, wu, vec, group, block=256):
+    da_ref[...] = mm(dm_low, wo_ref[...], NT).astype(BF16)
+
+
+def down_call(core, lengths, seats, mid, e, slope, dy, vec, up_group, down_group, block=256):
     rows = mid.shape[0]
     steps = rows // block
     half = steps // 2
@@ -564,21 +552,26 @@
         pl.BlockSpec((block, width), lambda i, c, *s: (row_block(c[0], i, steps), 0)) for width in (D, FF)
     ]
     return pl.pallas_call(
-        functools.partial(down_kernel, group),
+        functools.partial(down_kernel, up_group, down_group),
         name="down",
         grid_spec=pltpu.PrefetchScalarGridSpec(
             num_scalar_prefetch=3,
             grid=(steps,),
-            in_specs=[row_spec, wide_spec, wide_spec, row_spec]
-            + [whole_spec(part.shape) for part in (wo, wu, vec)]
-            + group.specs(),
+            in_specs=[row_spec, wide_spec, wide_spec, row_spec, whole_spec(vec.shape)]
+            + up_group.specs()
+            + down_group.specs(),
             out_specs=[
                 pl.BlockSpec((block, D), lambda i, *s: (jnp.minimum(i, half - 1), 0)),
                 pl.BlockSpec((1, block, D), lambda i, c, *s: (c[0], jnp.maximum(i - half, 0), 0)),
                 wide_spec, row_spec, row_spec, row_spec,
                 pl.BlockSpec((16, D), lambda i, *s: (0, 0)),
             ],
-            scratch_shapes=[pltpu.VMEM((FF, D), BF16), pltpu.VMEM((D, FF), BF16), pltpu.SemaphoreType.DMA((1,))],
+            scratch_shapes=[
+                pltpu.VMEM((D, D), BF16),
+                pltpu.VMEM((D, FF), BF16),
+                pltpu.VMEM((FF, D), BF16),
+                pltpu.SemaphoreType.DMA((3,)),
+            ],
         ),
         out_shape=[
             jax.ShapeDtypeStruct((rows // 2, D), BF16),
@@ -591,7 +584,7 @@
         ],
         compiler_params=params(48),
         cost_estimate=cost(1.6e10, 35e6),
-    )(core, lengths, seats, mid, e, slope, dy, wo, wu, vec, *group.arrays)
+    )(core, lengths, seats, mid, e, slope, dy, vec, *up_group.arrays, *down_group.arrays)
 
 
 def pick(values, half, mode):
@@ -918,9 +911,9 @@
             return [parts[0] + got.astype(F32)], got
         return [part + got[at].astype(F32) for at, part in enumerate(parts[:half])], got
 
-    def scatter_z(self, parts):
+    def scatter_z(self, parts, *until):
         while len(parts) > 1:
-            parts, _ = self.scatter_bit(parts)
+            parts, _ = self.scatter_bit(parts, *until)
         return parts[0]
 
 
@@ -990,14 +983,14 @@
     u_rest_swap = [after(grid.swap(part), a) for part in u_rest]
     d_line = grid.gather_first(d_col, a)
     u_group = finish_group(grid, seats, [u_line] + u_rest, [u_line_swap] + u_rest_swap)
-    mid, h2, e, slope, dy, wo, wu = up_call(core_arr, lengths, seats, x, after(a, d_line), og, vec, u_group)
+    mid, h2, e, slope, dy = up_call(core_arr, lengths, seats, x, after(a, d_line), og, vec, u_group)
     d_line_swap = after(grid.swap(d_line), mid)
     d_rest = grid.gather_second(d_line, mid)
     d_own, d_other = weight_grad_call(core_arr, [(after(e, *d_rest), [dy])], 512, "grad_down")
     d_rest_swap = [after(grid.swap(part), d_own) for part in d_rest]
     d_group = finish_group(grid, seats, [d_line] + d_rest, [d_line_swap] + d_rest_swap)
     out_theirs, out_mine, dz, dmb, dm, da, acc_mid = down_call(
-        core_arr, lengths, seats, mid, e, slope, dy, wo, wu, vec, d_group
+        core_arr, lengths, seats, mid, e, slope, dy, vec, u_group, d_group
     )
 
     d_pair = after(grid.swap(d_other), dz)
@@ -1013,20 +1006,20 @@
     d_sum, d_here = grid.scatter_second(d_kept, *back)
     u_pair = after(grid.swap(u_other), *back)
     back = back_call(2, 4, back, u_pair, *d_here)
-    d_parts, _ = grid.scatter_bit(grid.order_z(d_sum), *back)
+    d_parts, d_got = grid.scatter_bit(grid.order_z(d_sum), *back)
     u_kept = grid.scatter_first(u_own, u_pair, *back)
     dq, dk, dv = back
     block_out = both_slots(out_mine, after(grid.swap(after(out_theirs, back[0])), dq))
     q_own, q_other = weight_grad_call(
-        core_arr, [(h1, [after(dq, *u_kept[1]), dk, dv])], 384, "grad_qkv", "turns"
+        core_arr, [(h1, [after(dq, d_got, *u_kept[1]), dk, dv])], 384, "grad_qkv", "turns"
     )
     u_sum, u_here = grid.scatter_second(u_kept, q_own)
-    d_mine = grid.scatter_z(d_parts)
-    d_other_mine = grid.swap(d_mine)
-    q_pair = after(grid.swap(q_other), *u_here)
+    q_pair = grid.swap(after(q_other, *u_here))
     in_theirs, in_mine, acc = last_call(
         core_arr, x, dm, after(dq, q_own, q_pair), dk, dv, w_back, vec, acc_mid
     )
+    d_mine = grid.scatter_z(d_parts, in_theirs)
+    d_other_mine = grid.swap(d_mine)
     q_kept = grid.scatter_first(q_own, q_pair, in_theirs)
     u_parts, u_got = grid.scatter_bit(grid.order_z(u_sum), *q_kept[1])
     q_sum, q_here = grid.scatter_second(q_kept, u_got)
@@ -1039,16 +1032,15 @@
     in_got = grid.swap(after(in_theirs, *q_kept[1]))
     u_mine = grid.scatter_z([after(part, *q_here) for part in u_parts])
     u_other_mine = grid.swap(u_mine)
-    q_parts = grid.order_z(q_sum)
-    q_gots = []
+    in_grad = both_slots(in_mine, after(in_got, *q_here))
+    q_parts, q_got = grid.scatter_bit(grid.order_z(q_sum), in_grad)
+    q_gots = [(q_got,)]
     while len(q_parts) > 1:
-        q_parts, got = grid.scatter_bit(q_parts)
-        q_gots.append((got,))
+        q_parts, q_got = grid.scatter_bit(q_parts)
+        q_gots.append((q_got,))
     q_mine = q_parts[0]
     q_other_mine = grid.swap(q_mine)
-    in_grad = both_slots(in_mine, after(in_got, *q_here))
-    w_qkv = after(w_qkv, in_grad)
-    vec_total = grid.total_small(acc, q_kept[1], q_here, *q_gots)
+    vec_total = grid.total_small(acc, (), q_kept[1], q_here, *q_gots)
 
     half, wide = D // 2, FF // 2
     out_new, up_new = adam_call(

time: 290 us -> 273 us (0.941)
  waiting for transfers between devices: 77.3 us -> 70.5 us
  local copies, waits for them, and re-layouts: 19.2 us -> 12.6 us
  Pallas kernels: 139 us -> 134 us
    ppermute x46, waiting for transfers between devices: 77.3 us -> 70.5 us  [permute(): return lax.ppermute(value, ('dp', 'seq'), pairs)]
    unnamed x94 -> x100, local copies, waits for them, and re-layouts: 13.4 us -> 9.38 us
    pallas_call x1, Pallas kernels: 33.2 us -> 29.6 us  [down_call(): pl.pallas_call(functools.partial(down_kernel, up_group, down_group), name...]
  transfers between devices with their start and end apart: 46 -> 46, of which waited for: 22 -> 22; matrix products, arithmetic and copies ran while one was open for 7% -> 6% of each run, Pallas kernels for 48% -> 49%
where the time goes in v1:
time: 273 us; the launch traced here: 270 us
  Pallas kernels  134 us (49%)
  waiting for transfers between devices  70.5 us (26%)
  starting transfers between devices  37.1 us (14%)
  other arithmetic  13.9 us (5%)
  local copies, waits for them, and re-layouts  12.6 us (5%)
    ppermute x46, waiting for transfers between devices, permute(): return lax.ppermute(value, ('dp', 'seq'), pairs)  70.5 us
    ppermute x46, starting transfers between devices, permute(): return lax.ppermute(value, ('dp', 'seq'), pairs)  37.1 us
    pallas_call x1, Pallas kernels, down_call(): pl.pallas_call(functools.partial(down_kernel, up_group, down_group), name...  29.6 us
    pallas_call x3, Pallas kernels, weight_grad_call(): pl.pallas_call(functools.partial(weight_grad_kernel, len(lefts), [len(gro...  26.3 us
    pallas_call x2, Pallas kernels, attend_back_call(): pl.pallas_call(attend_back_kernel, name='attend_back', grid_spec=pltpu.Pr...  23.8 us
    pallas_call x1, Pallas kernels, up_call(): pl.pallas_call(functools.partial(up_kernel, group), name='up', grid_spec=...  19.5 us
    pallas_call x2, Pallas kernels, attend_call(): pl.pallas_call(functools.partial(attend_kernel, first), name='attend', gr...  13.7 us
    unnamed x100, local copies, waits for them, and re-layouts  9.38 us
  transfers between devices with their start and end apart: 46, of which 22 were waited for; matrix products, arithmetic and copies ran while one was open for 6% of the time, Pallas kernels for 49%

profile of v1, /device:TPU:0, one launch (start us, length us, event | category | flops | bytes accessed | tf_op | source)
XLA Modules:
  0.0 269.7 jit_solution(1425308733604157978)
XLA Ops:
  3.2 4.1 %collective-permute-start.2 = (bf16[48,1280]{1,0:T(8,128)(2,1)S(1)}, bf16[48,1280]{1,0:T(8,128)(2,1)S(1)}, u32[]{:S(2)}, u32[]{:S(2)}) collective-permute-start(bf16[48,1280]{1,0:T(8,128)(2,1)S(1)} %get-tuple-element.261), channel_id=1, source_target_pairs={{0,16},{1,17},{2,18},{3,19},{4,20},{5,21},{6,22},{7,23},{8,24},{9,... | collective-permute-start | bytes 368648 | tf_op jit(solution)/shard_map/ppermute | solution.py:827
  13.0 3.8 %collective-permute-done.2 = bf16[48,1280]{1,0:T(8,128)(2,1)S(1)} collective-permute-done((bf16[48,1280]{1,0:T(8,128)(2,1)S(1)}, bf16[48,1280]{1,0:T(8,128)(2,1)S(1)}, u32[]{:S(2)}, u32[]{:S(2)}) %collective-permute-start.2) | collective-permute-done | bytes 122912 | tf_op jit(solution)/shard_map/ppermute | solution.py:827
  25.3 2.9 %collective-permute-done.4 = bf16[4,48,1280]{2,1,0:T(8,128)(2,1)S(1)} collective-permute-done((bf16[4,48,1280]{2,1,0:T(8,128)(2,1)S(1)}, bf16[4,48,1280]{2,1,0:T(8,128)(2,1)S(1)}, u32[]{:S(2)}, u32[]{:S(2)}) %collective-permute-start.4) | collective-permute-done | bytes 491552 | tf_op jit(solution)/shard_map/ppermute | solution.py:827
  32.6 14.7 %collective-permute-done.9 = bf16[2,48,1920]{2,1,0:T(8,128)(2,1)S(1)} collective-permute-done((bf16[2,48,1920]{2,1,0:T(8,128)(2,1)S(1)}, bf16[2,48,1920]{2,1,0:T(8,128)(2,1)S(1)}, u32[]{:S(2)}, u32[]{:S(2)}) %collective-permute-start.9) | collective-permute-done | bytes 368672 | tf_op jit(solution)/shard_map/ppermute | solution.py:827
  50.8 9.1 %qkv.1 = (bf16[1024,768]{1,0:T(8,128)(2,1)S(1)}, bf16[1024,2304]{1,0:T(8,128)(2,1)S(1)}, f32[16,768]{1,0:T(8,128)S(1)}, bf16[2304,768]{1,0:T(8,128)(2,1)S(1)}) custom-call(s32[1]{0:T(128)} %bitcast.64.core_ref, s32[32]{0:T(128)S(1)} %convert_element_type.410.seat_ref, bf16[1024,768]{1,0:T(8,128)(2,1)S(1)} %maximum_select_fusion.x_ref, ...), custom_call_target="tpu_custom_call" | custom-call | flops 14495514624 | bytes 40000000 | tf_op jit(solution)/shard_map/qkv/pallas_call | solution.py:161
  67.2 8.9 %attend.2 = (bf16[1024,768]{1,0:T(8,128)(2,1)S(1)}, f32[6,8,1024]{2,1,0:T(8,128)S(1)}) custom-call(s32[1]{0:T(128)} %bitcast.64.core_ref, s32[2]{0:T(128)S(1)} %copy-done.21, bf16[1024,2304]{1,0:T(8,128)(2,1)S(1)} %get-tuple-element.146.qkv_ref.q_ref.k_ref.v_ref), custom_call_target="tpu_custom_call" | custom-call | flops 48000000000 | bytes 19200000 | tf_op jit(solution)/shard_map/attend/pallas_call | solution.py:274
  78.0 6.3 %collective-permute-done.13.refs_1_ = bf16[2,4,48,1920]{3,2,1,0:T(8,128)(2,1)S(1)} collective-permute-done((bf16[2,4,48,1920]{3,2,1,0:T(8,128)(2,1)S(1)}, bf16[2,4,48,1920]{3,2,1,0:T(8,128)(2,1)S(1)}, u32[]{:S(2)}, u32[]{:S(2)}) %collective-permute-start.13) | collective-permute-done | bytes 1474592 | tf_op jit(solution)/shard_map/ppermute | solution.py:827
  85.1 4.8 %attend.3 = (bf16[1024,768]{1,0:T(8,128)(2,1)S(1)}, f32[6,8,1024]{2,1,0:T(8,128)S(1)}) custom-call(s32[1]{0:T(128)} %bitcast.64.core_ref, s32[2]{0:T(128)S(1)} %copy-done.21, bf16[1024,2304]{1,0:T(8,128)(2,1)S(1)} %get-tuple-element.146.qkv_ref.q_ref.k_ref.v_ref, ...), custom_call_target="tpu_custom_call", output_to_operand_aliasing={{0}: (3, {}), {1}: (4, {})} | custom-call | flops 24000000000 | bytes 9600000 | tf_op jit(solution)/shard_map/attend/pallas_call | solution.py:274
  89.9 4.3 %collective-permute-done.14 = bf16[4,192,384]{2,1,0:T(8,128)(2,1)S(1)} collective-permute-done((bf16[4,192,384]{2,1,0:T(8,128)(2,1)S(1)}, bf16[4,192,384]{2,1,0:T(8,128)(2,1)S(1)}, u32[]{:S(2)}, u32[]{:S(2)}) %collective-permute-start.14) | collective-permute-done | bytes 589856 | tf_op jit(solution)/shard_map/ppermute | solution.py:827
  96.0 19.5 %up.1 = (f32[1024,768]{1,0:T(8,128)}, bf16[1024,768]{1,0:T(8,128)(2,1)}, bf16[1024,3072]{1,0:T(8,128)(2,1)}, bf16[1024,3072]{1,0:T(8,128)(2,1)}, bf16[1024,768]{1,0:T(8,128)(2,1)}) custom-call(s32[1]{0:T(128)} %bitcast.64.core_ref, s32[2]{0:T(128)S(1)} %copy-done.21, s32[32]{0:T(128)S(1)} %convert_element_type.409.seat_ref, bf16[1024,768]{1,0:T(8,128)(2,1)} %copy-done, ...), custom_call_target="tpu_custom_call" | custom-call | flops 24000000000 | bytes 120000000 | tf_op jit(solution)/shard_map/up/pallas_call | solution.py:458
  117.1 9.5 %grad_down.1 = (bf16[3072,384]{1,0:T(8,128)(2,1)S(1)}, bf16[3072,384]{1,0:T(8,128)(2,1)}) custom-call(s32[1]{0:T(128)} %bitcast.64.core_ref, bf16[1024,3072]{1,0:T(8,128)(2,1)} %get-tuple-element.160.refs_0_.e_ref, bf16[1024,768]{1,0:T(8,128)(2,1)S(1)} %copy-done.28), custom_call_target="tpu_custom_call" | custom-call | flops 19327352832 | bytes 50331648 | tf_op jit(solution)/shard_map/grad_down/pallas_call | solution.py:629
  127.1 29.6 %down.1 = (bf16[512,768]{1,0:T(8,128)(2,1)S(1)}, bf16[2,512,768]{2,1,0:T(8,128)(2,1)}, bf16[1024,3072]{1,0:T(8,128)(2,1)}, bf16[1024,768]{1,0:T(8,128)(2,1)}, f3...) custom-call(s32[1]{0:T(128)} %bitcast.64.core_ref, s32[2]{0:T(128)S(1)} %copy-done.21, ...), custom_call_target="tpu_custom_call" | custom-call | flops 64000000000 | bytes 140000000 | tf_op jit(solution)/shard_map/down/pallas_call | solution.py:554
  160.4 12.0 %grad_up.1 = (bf16[768,1920]{1,0:T(8,128)(2,1)}, bf16[768,1920]{1,0:T(8,128)(2,1)}) custom-call(s32[1]{0:T(128)} %bitcast.64.core_ref, bf16[1024,768]{1,0:T(8,128)(2,1)S(1)} %copy-done.31, bf16[1024,768]{1,0:T(8,128)(2,1)S(1)} %copy-done.29, bf16[1024,768]{1,0:T(8,128)(2,1)S(1)} %copy-done.32, bf16[1024,3072]{1,0:T(8,128)(2,1)} %get-tuple-element.171.refs_3_), custom_call_target="tpu_custom_call" | custom-call | flops 24159191040 | bytes 61341696 | tf_op jit(solution)/shard_map/grad_up/pallas_call | solution.py:629
  172.4 2.3 collective-permute-done.23
  175.6 8.4 %attend_back.2 = (bf16[1024,768]{1,0:T(8,128)(2,1)S(1)}, bf16[1024,768]{1,0:T(8,128)(2,1)S(1)}, bf16[1024,768]{1,0:T(8,128)(2,1)S(1)}) custom-call(s32[1]{0:T(128)} %bitcast.64.core_ref, s32[2]{0:T(128)S(1)} %copy-done.21, bf16[1024,2304]{1,0:T(8,128)(2,1)S(1)} %bitcast.232, bf16[1024,2304]{1,0:T(8,128)(2,1)S(1)} %bitcast.232, ...), custom_call_target="tpu_custom_call" | custom-call | flops 48000000000 | bytes 16000000 | tf_op jit(solution)/shard_map/attend_back/pallas_call | solution.py:371
  190.7 15.4 %attend_back.3 = (bf16[1024,768]{1,0:T(8,128)(2,1)S(1)}, bf16[1024,768]{1,0:T(8,128)(2,1)S(1)}, bf16[1024,768]{1,0:T(8,128)(2,1)S(1)}) custom-call(s32[1]{0:T(128)} %bitcast.64.core_ref, s32[2]{0:T(128)S(1)} %copy-done.21, bf16[1024,2304]{1,0:T(8,128)(2,1)S(1)} %bitcast.232, ...), custom_call_target="tpu_custom_call", output_to_operand_aliasing={{0}: (8, {}), {1}: (9, {}), {2}: (10, {})} | custom-call | flops 96000000000 | bytes 32000000 | tf_op jit(solution)/shard_map/attend_back/pallas_call | solution.py:371
  206.2 2.3 collective-permute-done.27
  210.2 4.8 %grad_qkv.1 = (bf16[768,1152]{1,0:T(8,128)(2,1)S(1)}, bf16[768,1152]{1,0:T(8,128)(2,1)S(1)}) custom-call(s32[1]{0:T(128)} %bitcast.64.core_ref, bf16[1024,768]{1,0:T(8,128)(2,1)S(1)} %copy-done.27, bf16[1024,768]{1,0:T(8,128)(2,1)S(1)} %get-tuple-element.203.refs_1_.dq_ref, bf16[1024,768]{1,0:T(8,128)(2,1)S(1)} %get-tuple-element.194.refs_2_.dk_ref, ...), custom_call_target="tpu_custom_call" | custom-call | flops 14495514624 | bytes 39321600 | tf_op jit(solution)/shard_map/grad_qkv/pallas_call | solution.py:629
  215.1 5.3 %collective-permute-done.28 = bf16[4,1,48,1920]{3,2,1,0:T(8,128)(2,1)S(1)} collective-permute-done((bf16[4,1,48,1920]{3,2,1,0:T(8,128)(2,1)S(1)}, bf16[4,1,48,1920]{3,2,1,0:T(8,128)(2,1)S(1)}, u32[]{:S(2)}, u32[]{:S(2)}) %collective-permute-start.28) | collective-permute-done | bytes 737312 | tf_op jit(solution)/shard_map/ppermute | solution.py:827
  226.1 7.0 %last.1 = (f32[512,768]{1,0:T(8,128)S(1)}, f32[2,512,768]{2,1,0:T(8,128)}, f32[16,768]{1,0:T(8,128)S(1)}) custom-call(s32[1]{0:T(128)} %bitcast.64.core_ref, bf16[1024,768]{1,0:T(8,128)(2,1)S(1)} %copy-done.1, f32[1024,768]{1,0:T(8,128)S(1)} %copy-done.25, bf16[1024,768]{1,0:T(8,128)(2,1)S(1)} %get-tuple-element.203.refs_1_.dq_ref, ...), custom_call_target="tpu_custom_call" | custom-call | flops 14495514624 | bytes 64000000 | tf_op jit(solution)/shard_map/last/pallas_call | solution.py:693
  235.3 2.3 collective-permute-done.30
  242.4 3.7 %collective-permute-done.32 = bf16[4,1,48,1152]{3,2,1,0:T(8,128)(2,1)S(1)} collective-permute-done((bf16[4,1,48,1152]{3,2,1,0:T(8,128)(2,1)S(1)}, bf16[4,1,48,1152]{3,2,1,0:T(8,128)(2,1)S(1)}, u32[]{:S(2)}, u32[]{:S(2)}) %collective-permute-start.32) | collective-permute-done | bytes 442400 | tf_op jit(solution)/shard_map/ppermute | solution.py:827
  250.2 5.0 %collective-permute-done.37 = bf16[48,1920]{1,0:T(8,128)(2,1)S(1)} collective-permute-done((bf16[48,1920]{1,0:T(8,128)(2,1)S(1)}, bf16[48,1920]{1,0:T(8,128)(2,1)S(1)}, u32[]{:S(2)}, u32[]{:S(2)}) %collective-permute-start.37) | collective-permute-done | bytes 184352 | tf_op jit(solution)/shard_map/ppermute | solution.py:827
  255.5 4.4 %collective-permute-done.34 = bf16[2,48,1152]{2,1,0:T(8,128)(2,1)S(1)} collective-permute-done((bf16[2,48,1152]{2,1,0:T(8,128)(2,1)S(1)}, bf16[2,48,1152]{2,1,0:T(8,128)(2,1)S(1)}, u32[]{:S(2)}, u32[]{:S(2)}) %collective-permute-start.34) | collective-permute-done | bytes 221216 | tf_op jit(solution)/shard_map/ppermute | solution.py:827
  (244 shorter events, 77.0 us)
Async XLA Ops:
  3.2 13.6 %collective-permute-start.2 = (bf16[48,1280]{1,0:T(8,128)(2,1)S(1)}, bf16[48,1280]{1,0:T(8,128)(2,1)S(1)}, u32[]{:S(2)}, u32[]{:S(2)}) collective-permute-start(bf16[48,1280]{1,0:T(8,128)(2,1)S(1)} %get-tuple-element.261), channel_id=1, source_target_pairs={{0,16},{1,17},{2,18},{3,19},{4,20},{5,21},{6,22},{7,23},{8,24},{9,... | collective-permute-start | bytes 368648 | tf_op jit(solution)/shard_map/ppermute | solution.py:827
  12.8 11.8 %collective-permute-start = (bf16[512,768]{1,0:T(8,128)(2,1)S(1)}, bf16[512,768]{1,0:T(8,128)(2,1)S(1)}, u32[]{:S(2)}, u32[]{:S(2)}) collective-permute-start(bf16[512,768]{1,0:T(8,128)(2,1)S(1)} %get-tuple-element.251), channel_id=1, source_target_pairs={{0,1},{1,0},{2,3},{3,2},{4,5},{5,4},{6,7},{7,6},{8,9},{9,8},{10,11... | collective-permute-start | bytes 2359304 | tf_op jit(solution)/shard_map/ppermute | solution.py:827
  28.3 19.8 %collective-permute-start.7 = (bf16[2,4,48,1280]{3,2,1,0:T(8,128)(2,1)S(1)}, bf16[2,4,48,1280]{3,2,1,0:T(8,128)(2,1)S(1)}, u32[]{:S(2)}, u32[]{:S(2)}) collective-permute-start(bf16[2,4,48,1280]{3,2,1,0:T(8,128)(2,1)S(1)} %pad_maximum_fusion.4.refs_0_), channel_id=1, source_target_pairs={{0,4},{1,3},{2,6},{3,1},{4,0},{5,7},{6,2},{7,5},{8,12},{9,11},{10,... | collective-permute-start | bytes 2949128 | tf_op jit(solution)/shard_map/ppermute | solution.py:827
  29.9 17.4 %collective-permute-start.9 = (bf16[2,48,1920]{2,1,0:T(8,128)(2,1)S(1)}, bf16[2,48,1920]{2,1,0:T(8,128)(2,1)S(1)}, u32[]{:S(2)}, u32[]{:S(2)}) collective-permute-start(bf16[2,48,1920]{2,1,0:T(8,128)(2,1)S(1)} %pad_maximum_fusion.7), channel_id=1, source_target_pairs={{0,16},{1,17},{2,18},{3,19},{4,20},{5,21},{6,22},{7,23},{8,24},{9,... | collective-permute-start | bytes 1105928 | tf_op jit(solution)/shard_map/ppermute | solution.py:827
  31.8 17.9 %collective-permute-start.8 = (bf16[2,4,48,1280]{3,2,1,0:T(8,128)(2,1)S(1)}, bf16[2,4,48,1280]{3,2,1,0:T(8,128)(2,1)}, u32[]{:S(2)}, u32[]{:S(2)}) collective-permute-start(bf16[2,4,48,1280]{3,2,1,0:T(8,128)(2,1)S(1)} %pad_maximum_fusion.4.refs_0_), channel_id=1, source_target_pairs={{0,1},{1,0},{2,3},{3,2},{4,5},{5,4},{6,7},{7,6},{8,9},{9,8},{10,11... | collective-permute-start | bytes 2949128 | tf_op jit(solution)/shard_map/ppermute | solution.py:827
  48.1 14.7 %collective-permute-start.12 = (bf16[4,48,1920]{2,1,0:T(8,128)(2,1)}, bf16[4,48,1920]{2,1,0:T(8,128)(2,1)S(1)}, u32[]{:S(2)}, u32[]{:S(2)}) collective-permute-start(bf16[4,48,1920]{2,1,0:T(8,128)(2,1)} %constant_dynamic-update-slice_fusion), channel_id=1, source_target_pairs={{0,2},{1,5},{2,0},{3,7},{4,6},{5,1},{6,4},{7,3},{8,10},{9,13},{10,... | collective-permute-start | bytes 2211848 | tf_op jit(solution)/shard_map/ppermute | solution.py:827
  48.7 17.8 %collective-permute-start.11 = (bf16[2,192,384]{2,1,0:T(8,128)(2,1)}, bf16[2,192,384]{2,1,0:T(8,128)(2,1)S(1)}, u32[]{:S(2)}, u32[]{:S(2)}) collective-permute-start(bf16[2,192,384]{2,1,0:T(8,128)(2,1)} %pad_maximum_fusion.9), channel_id=1, source_target_pairs={{0,16},{1,17},{2,18},{3,19},{4,20},{5,21},{6,22},{7,23},{8,24},{9,... | collective-permute-start | bytes 884744 | tf_op jit(solution)/shard_map/ppermute | solution.py:827
  64.8 20.3 %collective-permute-start.16 = (bf16[2,4,48,1920]{3,2,1,0:T(8,128)(2,1)S(1)}, bf16[2,4,48,1920]{3,2,1,0:T(8,128)(2,1)S(1)}, u32[]{:S(2)}, u32[]{:S(2)}) collective-permute-start(bf16[2,4,48,1920]{3,2,1,0:T(8,128)(2,1)S(1)} %pad_maximum_fusion.refs_0_), channel_id=1, source_target_pairs={{0,1},{1,0},{2,3},{3,2},{4,5},{5,4},{6,7},{7,6},{8,9},{9,8},{10,11... | collective-permute-start | bytes 4423688 | tf_op jit(solution)/shard_map/ppermute | solution.py:827
  65.0 19.4 %collective-permute-start.13 = (bf16[2,4,48,1920]{3,2,1,0:T(8,128)(2,1)S(1)}, bf16[2,4,48,1920]{3,2,1,0:T(8,128)(2,1)S(1)}, u32[]{:S(2)}, u32[]{:S(2)}) collective-permute-start(bf16[2,4,48,1920]{3,2,1,0:T(8,128)(2,1)S(1)} %pad_maximum_fusion.refs_0_), channel_id=1, source_target_pairs={{0,4},{1,3},{2,6},{3,1},{4,0},{5,7},{6,2},{7,5},{8,12},{9,11},{10,... | collective-permute-start | bytes 4423688 | tf_op jit(solution)/shard_map/ppermute | solution.py:827
  94.3 21.2 %collective-permute-start.19 = (bf16[2,4,192,384]{3,2,1,0:T(8,128)(2,1)S(1)}, bf16[2,4,192,384]{3,2,1,0:T(8,128)(2,1)S(1)}, u32[]{:S(2)}, u32[]{:S(2)}) collective-permute-start(bf16[2,4,192,384]{3,2,1,0:T(8,128)(2,1)S(1)} %pad_maximum_fusion.2.refs_4_), channel_id=1, source_target_pairs={{0,1},{1,0},{2,3},{3,2},{4,5},{5,4},{6,7},{7,6},{8,9},{9,8},{10,11... | collective-permute-start | bytes 3538952 | tf_op jit(solution)/shard_map/ppermute | solution.py:827
  94.4 21.2 %collective-permute-start.18 = (bf16[2,4,192,384]{3,2,1,0:T(8,128)(2,1)S(1)}, bf16[2,4,192,384]{3,2,1,0:T(8,128)(2,1)S(1)}, u32[]{:S(2)}, u32[]{:S(2)}) collective-permute-start(bf16[2,4,192,384]{3,2,1,0:T(8,128)(2,1)S(1)} %pad_maximum_fusion.2.refs_4_), channel_id=1, source_target_pairs={{0,4},{1,3},{2,6},{3,1},{4,0},{5,7},{6,2},{7,5},{8,12},{9,11},{10,... | collective-permute-start | bytes 3538952 | tf_op jit(solution)/shard_map/ppermute | solution.py:827
  126.6 30.1 %collective-permute-start.21 = (bf16[3072,384]{1,0:T(8,128)(2,1)}, bf16[3072,384]{1,0:T(8,128)(2,1)S(1)}, u32[]{:S(2)}, u32[]{:S(2)}) collective-permute-start(bf16[3072,384]{1,0:T(8,128)(2,1)} %get-tuple-element.169), channel_id=1, source_target_pairs={{0,1},{1,0},{2,3},{3,2},{4,5},{5,4},{6,7},{7,6},{8,9},{9,8},{10,11... | collective-permute-start | bytes 7077896 | tf_op jit(solution)/shard_map/ppermute | solution.py:827
  158.3 16.4 %collective-permute-start.23 = (bf16[2,4,1,192,384]{4,3,1,2,0:T(8,128)(2,1)}, bf16[2,4,1,192,384]{4,3,1,2,0:T(8,128)(2,1)S(1)}, u32[]{:S(2)}, u32[]{:S(2)}) collective-permute-start(bf16[2,4,1,192,384]{4,3,1,2,0:T(8,128)(2,1)} %pad_maximum_fusion.3), channel_id=1, source_target_pairs={{0,2},{1,5},{2,0},{3,7},{4,6},{5,1},{6,4},{7,3},{8,10},{9,13},{10,... | collective-permute-start | bytes 3538952 | tf_op jit(solution)/shard_map/ppermute | solution.py:827
  172.4 16.3 %collective-permute-start.22 = (bf16[768,1920]{1,0:T(8,128)(2,1)}, bf16[768,1920]{1,0:T(8,128)(2,1)S(1)}, u32[]{:S(2)}, u32[]{:S(2)}) collective-permute-start(bf16[768,1920]{1,0:T(8,128)(2,1)} %get-tuple-element.172), channel_id=1, source_target_pairs={{0,1},{1,0},{2,3},{3,2},{4,5},{5,4},{6,7},{7,6},{8,9},{9,8},{10,11... | collective-permute-start | bytes 8847368 | tf_op jit(solution)/shard_map/ppermute | solution.py:827
  186.7 19.5 %collective-permute-start.26 = (bf16[2,192,384]{2,1,0:T(8,128)(2,1)S(1)}, bf16[2,192,384]{2,1,0:T(8,128)(2,1)S(1)}, u32[]{:S(2)}, u32[]{:S(2)}) collective-permute-start(bf16[2,192,384]{2,1,0:T(8,128)(2,1)S(1)} %pad_maximum_fusion.10), channel_id=1, source_target_pairs={{0,16},{1,17},{2,18},{3,19},{4,20},{5,21},{6,22},{7,23},{8,24},{9,... | collective-permute-start | bytes 884744 | tf_op jit(solution)/shard_map/ppermute | solution.py:827
  189.2 19.4 %collective-permute-start.27 = (bf16[2,4,1,48,1920]{4,3,1,2,0:T(8,128)(2,1)S(1)}, bf16[2,4,1,48,1920]{4,3,1,2,0:T(8,128)(2,1)S(1)}, u32[]{:S(2)}, u32[]{:S(2)}) collective-permute-start(bf16[2,4,1,48,1920]{4,3,1,2,0:T(8,128)(2,1)S(1)} %pad_maximum_fusion.1), channel_id=1, source_target_pairs={{0,2},{1,5},{2,0},{3,7},{4,6},{5,1},{6,4},{7,3},{8,10},{9,13},{10,... | collective-permute-start | bytes 4423688 | tf_op jit(solution)/shard_map/ppermute | solution.py:827
  206.2 14.4 %collective-permute-start.25 = (bf16[512,768]{1,0:T(8,128)(2,1)S(1)}, bf16[512,768]{1,0:T(8,128)(2,1)S(1)}, u32[]{:S(2)}, u32[]{:S(2)}) collective-permute-start(bf16[512,768]{1,0:T(8,128)(2,1)S(1)} %get-tuple-element.187), channel_id=1, source_target_pairs={{0,1},{1,0},{2,3},{3,2},{4,5},{5,4},{6,7},{7,6},{8,9},{9,8},{10,11... | collective-permute-start | bytes 2359304 | tf_op jit(solution)/shard_map/ppermute | solution.py:827
  208.9 11.5 %collective-permute-start.28 = (bf16[4,1,48,1920]{3,2,1,0:T(8,128)(2,1)S(1)}, bf16[4,1,48,1920]{3,2,1,0:T(8,128)(2,1)S(1)}, u32[]{:S(2)}, u32[]{:S(2)}) collective-permute-start(bf16[4,1,48,1920]{3,2,1,0:T(8,128)(2,1)S(1)} %fusion.2), channel_id=1, source_target_pairs={{0,4},{1,3},{2,6},{3,1},{4,0},{5,7},{6,2},{7,5},{8,12},{9,11},{10,... | collective-permute-start | bytes 2211848 | tf_op jit(solution)/shard_map/ppermute | solution.py:827
  220.5 12.6 %collective-permute-start.39 = (bf16[192,384]{1,0:T(8,128)(2,1)S(1)}, bf16[192,384]{1,0:T(8,128)(2,1)S(1)}, u32[]{:S(2)}, u32[]{:S(2)}) collective-permute-start(bf16[192,384]{1,0:T(8,128)(2,1)S(1)} %fusion.15), channel_id=1, source_target_pairs={{0,8},{1,9},{2,10},{3,11},{4,12},{5,13},{6,14},{7,15},{8,0},{9,1},... | collective-permute-start | bytes 442376 | tf_op jit(solution)/shard_map/ppermute | solution.py:827
  221.1 19.9 %collective-permute-start.33 = (bf16[2,48,1920]{2,1,0:T(8,128)(2,1)S(1)}, bf16[2,48,1920]{2,1,0:T(8,128)(2,1)S(1)}, u32[]{:S(2)}, u32[]{:S(2)}) collective-permute-start(bf16[2,48,1920]{2,1,0:T(8,128)(2,1)S(1)} %pad_maximum_fusion.8), channel_id=1, source_target_pairs={{0,16},{1,17},{2,18},{3,19},{4,20},{5,21},{6,22},{7,23},{8,24},{9,... | collective-permute-start | bytes 1105928 | tf_op jit(solution)/shard_map/ppermute | solution.py:827
  224.5 13.1 %collective-permute-start.30 = (bf16[2,4,1,48,1152]{4,3,1,2,0:T(8,128)(2,1)S(1)}, bf16[2,4,1,48,1152]{4,3,1,2,0:T(8,128)(2,1)S(1)}, u32[]{:S(2)}, u32[]{:S(2)}) collective-permute-start(bf16[2,4,1,48,1152]{4,3,1,2,0:T(8,128)(2,1)S(1)} %pad_maximum_fusion.5), channel_id=1, source_target_pairs={{0,2},{1,5},{2,0},{3,7},{4,6},{5,1},{6,4},{7,3},{8,10},{9,13},{10,... | collective-permute-start | bytes 2654216 | tf_op jit(solution)/shard_map/ppermute | solution.py:827
  233.1 29.0 %collective-permute-start.40 = (f32[192,384]{1,0:T(8,128)S(1)}, f32[192,384]{1,0:T(8,128)S(1)}, u32[]{:S(2)}, u32[]{:S(2)}) collective-permute-start(f32[192,384]{1,0:T(8,128)S(1)} %fusion.16.refs_0_), channel_id=1, source_target_pairs={{0,1},{1,0},{2,3},{3,2},{4,5},{5,4},{6,7},{7,6},{8,9},{9,8},{10,11... | collective-permute-start | bytes 884744 | tf_op jit(solution)/shard_map/ppermute | solution.py:827
  242.3 13.1 %collective-permute-start.31 = (f32[512,768]{1,0:T(8,128)S(1)}, f32[512,768]{1,0:T(8,128)S(1)}, u32[]{:S(2)}, u32[]{:S(2)}) collective-permute-start(f32[512,768]{1,0:T(8,128)S(1)} %get-tuple-element.209), channel_id=1, source_target_pairs={{0,1},{1,0},{2,3},{3,2},{4,5},{5,4},{6,7},{7,6},{8,9},{9,8},{10,11... | collective-permute-start | bytes 4718600 | tf_op jit(solution)/shard_map/ppermute | solution.py:827
  246.7 13.3 %collective-permute-start.44 = (f32[16,768]{1,0:T(8,128)S(1)}, f32[16,768]{1,0:T(8,128)S(1)}, u32[]{:S(2)}, u32[]{:S(2)}) collective-permute-start(f32[16,768]{1,0:T(8,128)S(1)} %add.658), channel_id=1, source_target_pairs={{0,8},{1,9},{2,10},{3,11},{4,12},{5,13},{6,14},{7,15},{8,0},{9,1},... | collective-permute-start | bytes 147464 | tf_op jit(solution)/shard_map/ppermute | solution.py:827
  (71 other events, 562.3 us)

commit v2 on v1

--- a/solution.py
+++ b/solution.py
@@ -476,7 +476,7 @@
             wide,
             low,
         ],
-        compiler_params=params(48),
+        compiler_params=params(40),
         cost_estimate=cost(6e9, 30e6, rows * FF),
     )(core, lengths, seats, x, a, og, vec, *group.arrays)
 
@@ -582,7 +582,7 @@
             jax.ShapeDtypeStruct((rows, D), BF16),
             jax.ShapeDtypeStruct((16, D), F32),
         ],
-        compiler_params=params(48),
+        compiler_params=params(40),
         cost_estimate=cost(1.6e10, 35e6),
     )(core, lengths, seats, mid, e, slope, dy, vec, *up_group.arrays, *down_group.arrays)
 
@@ -869,6 +869,15 @@
     def gather_bit(self, held, bit, *until):
         return jnp.concatenate([held, after(self.permute(held, "zx", bit), *until)])
 
+    def along(self, axis, column, *until):
+        return [after(self.permute(column, axis, s), *until) for s in range(1, self.n)]
+
+    def plane_parts(self, column, firsts, seconds, passed):
+        parts = [column] + firsts
+        for s2 in range(1, self.n):
+            parts += [seconds[s2 - 1]] + [passed[s1 - 1][s2 - 1] for s1 in range(1, self.n)]
+        return [part[None] for part in parts]
+
     def gather_first(self, column, *until):
         return jnp.stack([column] + [after(self.permute(column, "first", s), *until) for s in range(1, self.n)])
 
@@ -972,23 +981,38 @@
     q_group = finish_group(grid, q_seats, [q_line] + q_rest, [q_line_swap] + q_rest_swap)
 
     h1, qkv, vec, w_back = qkv_call(core_arr, q_seats, x, q_group)
-    u_line = grid.gather_first(u_col, qkv)
+    u_firsts = grid.along("first", u_col, qkv)
     d_col = grid.gather_bit(after(d_col, u_col), bits[-1], qkv)
     og = own_slot(after(out_grad, qkv))
-    att = attend_call(core_arr, lengths, after(qkv, u_line, d_col), 0, 4, ())
-    u_line_swap = after(grid.swap(u_line), *att)
-    u_rest = grid.gather_second(u_line, *att)
-    d_col = after(d_col, *u_rest)
+    att = attend_call(core_arr, lengths, after(qkv, d_col, *u_firsts), 0, 4, ())
+    u_seconds = grid.along("second", u_col, *att)
+    u_passed = [grid.along("second", part, *att) for part in u_firsts]
+    early = [after(grid.swap(part), *att) for part in [u_col] + u_firsts]
+    d_col = after(d_col, *u_seconds, *[part for parts in u_passed for part in parts])
     a, lse = attend_call(core_arr, lengths, after(qkv, d_col), 4, 2, att)
-    u_rest_swap = [after(grid.swap(part), a) for part in u_rest]
-    d_line = grid.gather_first(d_col, a)
-    u_group = finish_group(grid, seats, [u_line] + u_rest, [u_line_swap] + u_rest_swap)
-    mid, h2, e, slope, dy = up_call(core_arr, lengths, seats, x, after(a, d_line), og, vec, u_group)
-    d_line_swap = after(grid.swap(d_line), mid)
-    d_rest = grid.gather_second(d_line, mid)
-    d_own, d_other = weight_grad_call(core_arr, [(after(e, *d_rest), [dy])], 512, "grad_down")
-    d_rest_swap = [after(grid.swap(part), d_own) for part in d_rest]
-    d_group = finish_group(grid, seats, [d_line] + d_rest, [d_line_swap] + d_rest_swap)
+    late_seconds = [after(grid.swap(part), a) for part in u_seconds]
+    late_passed = [[after(grid.swap(part), a) for part in parts] for parts in u_passed]
+    u_group = finish_group(
+        grid,
+        seats,
+        grid.plane_parts(u_col, u_firsts, u_seconds, u_passed),
+        grid.plane_parts(early[0], early[1:], late_seconds, late_passed),
+    )
+    mid, h2, e, slope, dy = up_call(core_arr, lengths, seats, x, a, og, vec, u_group)
+    d_firsts = grid.along("first", d_col, mid)
+    d_seconds = grid.along("second", d_col, mid)
+    d_col_swap = after(grid.swap(d_col), mid)
+    d_own, d_other = weight_grad_call(
+        core_arr, [(after(e, *d_firsts, *d_seconds), [dy])], 512, "grad_down"
+    )
+    d_passed = [grid.along("second", part, d_own) for part in d_firsts]
+    early = [[after(grid.swap(part), d_own) for part in parts] for parts in (d_firsts, d_seconds)]
+    d_group = finish_group(
+        grid,
+        seats,
+        grid.plane_parts(d_col, d_firsts, d_seconds, d_passed),
+        grid.plane_parts(d_col_swap, *early, [[grid.swap(part) for part in parts] for parts in d_passed]),
+    )
     out_theirs, out_mine, dz, dmb, dm, da, acc_mid = down_call(
         core_arr, lengths, seats, mid, e, slope, dy, vec, u_group, d_group
     )

time: 273 us -> 273 us (level)
  waiting for transfers between devices: 70.5 us -> 63 us
  local copies, waits for them, and re-layouts: 12.6 us -> 18.2 us
  starting transfers between devices: 37.1 us -> 41.6 us
    ppermute x46 -> x52, waiting for transfers between devices: 70.5 us -> 63 us  [permute(): return lax.ppermute(value, ('dp', 'seq'), pairs)]
    unnamed x100 -> x102, local copies, waits for them, and re-layouts: 9.38 us -> 15.7 us
    ppermute x46 -> x52, starting transfers between devices: 37.1 us -> 41.6 us  [permute(): return lax.ppermute(value, ('dp', 'seq'), pairs)]
  transfers between devices with their start and end apart: 46 -> 52, of which waited for: 22 -> 20; matrix products, arithmetic and copies ran while one was open for 6% -> 4% of each run, Pallas kernels for 49% -> 49%
where the time goes in v2:
time: 273 us; the launch traced here: 270 us
  Pallas kernels  133 us (49%)
  waiting for transfers between devices  63 us (23%)
  starting transfers between devices  41.6 us (15%)
  local copies, waits for them, and re-layouts  18.2 us (7%)
  other arithmetic  11.9 us (4%)
    ppermute x52, waiting for transfers between devices, permute(): return lax.ppermute(value, ('dp', 'seq'), pairs)  63 us
    ppermute x52, starting transfers between devices, permute(): return lax.ppermute(value, ('dp', 'seq'), pairs)  41.6 us
    pallas_call x1, Pallas kernels, down_call(): pl.pallas_call(functools.partial(down_kernel, up_group, down_group), name...  30.5 us
    pallas_call x3, Pallas kernels, weight_grad_call(): pl.pallas_call(functools.partial(weight_grad_kernel, len(lefts), [len(gro...  26.3 us
    pallas_call x2, Pallas kernels, attend_back_call(): pl.pallas_call(attend_back_kernel, name='attend_back', grid_spec=pltpu.Pr...  23.8 us
    pallas_call x1, Pallas kernels, up_call(): pl.pallas_call(functools.partial(up_kernel, group), name='up', grid_spec=...  18.1 us
    unnamed x102, local copies, waits for them, and re-layouts  15.7 us
    pallas_call x2, Pallas kernels, attend_call(): pl.pallas_call(functools.partial(attend_kernel, first), name='attend', gr...  13.7 us
  transfers between devices with their start and end apart: 52, of which 20 were waited for; matrix products, arithmetic and copies ran while one was open for 4% of the time, Pallas kernels for 49%

profile of v2, /device:TPU:0, one launch (start us, length us, event | category | flops | bytes accessed | tf_op | source)
XLA Modules:
  0.0 269.7 jit_solution(12297862762817303562)
XLA Ops:
  3.2 4.1 %collective-permute-start.2 = (bf16[48,1280]{1,0:T(8,128)(2,1)S(1)}, bf16[48,1280]{1,0:T(8,128)(2,1)S(1)}, u32[]{:S(2)}, u32[]{:S(2)}) collective-permute-start(bf16[48,1280]{1,0:T(8,128)(2,1)S(1)} %get-tuple-element.269), channel_id=1, source_target_pairs={{0,16},{1,17},{2,18},{3,19},{4,20},{5,21},{6,22},{7,23},{8,24},{9,... | collective-permute-start | bytes 368648 | tf_op jit(solution)/shard_map/ppermute | solution.py:827
  13.0 3.8 %collective-permute-done.2 = bf16[48,1280]{1,0:T(8,128)(2,1)S(1)} collective-permute-done((bf16[48,1280]{1,0:T(8,128)(2,1)S(1)}, bf16[48,1280]{1,0:T(8,128)(2,1)S(1)}, u32[]{:S(2)}, u32[]{:S(2)}) %collective-permute-start.2) | collective-permute-done | bytes 122912 | tf_op jit(solution)/shard_map/ppermute | solution.py:827
  25.3 2.9 %collective-permute-done.4 = bf16[4,48,1280]{2,1,0:T(8,128)(2,1)S(1)} collective-permute-done((bf16[4,48,1280]{2,1,0:T(8,128)(2,1)S(1)}, bf16[4,48,1280]{2,1,0:T(8,128)(2,1)S(1)}, u32[]{:S(2)}, u32[]{:S(2)}) %collective-permute-start.4) | collective-permute-done | bytes 491552 | tf_op jit(solution)/shard_map/ppermute | solution.py:827
  31.9 15.5 %collective-permute-done.9 = bf16[2,48,1920]{2,1,0:T(8,128)(2,1)S(1)} collective-permute-done((bf16[2,48,1920]{2,1,0:T(8,128)(2,1)S(1)}, bf16[2,48,1920]{2,1,0:T(8,128)(2,1)S(1)}, u32[]{:S(2)}, u32[]{:S(2)}) %collective-permute-start.9) | collective-permute-done | bytes 368672 | tf_op jit(solution)/shard_map/ppermute | solution.py:827
  51.1 9.1 %qkv.1 = (bf16[1024,768]{1,0:T(8,128)(2,1)S(1)}, bf16[1024,2304]{1,0:T(8,128)(2,1)S(1)}, f32[16,768]{1,0:T(8,128)S(1)}, bf16[2304,768]{1,0:T(8,128)(2,1)S(1)}) custom-call(s32[1]{0:T(128)} %bitcast.64.core_ref, s32[32]{0:T(128)S(1)} %convert_element_type.410.seat_ref, bf16[1024,768]{1,0:T(8,128)(2,1)S(1)} %maximum_select_fusion.x_ref, ...), custom_call_target="tpu_custom_call" | custom-call | flops 14495514624 | bytes 40000000 | tf_op jit(solution)/shard_map/qkv/pallas_call | solution.py:161
  61.4 4.3 %collective-permute-done.13 = bf16[4,48,1920]{2,1,0:T(8,128)(2,1)S(1)} collective-permute-done((bf16[4,48,1920]{2,1,0:T(8,128)(2,1)S(1)}, bf16[4,48,1920]{2,1,0:T(8,128)(2,1)S(1)}, u32[]{:S(2)}, u32[]{:S(2)}) %collective-permute-start.13) | collective-permute-done | bytes 737312 | tf_op jit(solution)/shard_map/ppermute | solution.py:827
  65.8 2.7 collective-permute-start.14
  69.2 8.9 %attend.2 = (bf16[1024,768]{1,0:T(8,128)(2,1)S(1)}, f32[6,8,1024]{2,1,0:T(8,128)S(1)}) custom-call(s32[1]{0:T(128)} %bitcast.64.core_ref, s32[2]{0:T(128)S(1)} %copy-done.23, bf16[1024,2304]{1,0:T(8,128)(2,1)S(1)} %get-tuple-element.151.qkv_ref.q_ref.k_ref.v_ref), custom_call_target="tpu_custom_call" | custom-call | flops 48000000000 | bytes 19200000 | tf_op jit(solution)/shard_map/attend/pallas_call | solution.py:274
  79.9 4.8 %attend.3 = (bf16[1024,768]{1,0:T(8,128)(2,1)S(1)}, f32[6,8,1024]{2,1,0:T(8,128)S(1)}) custom-call(s32[1]{0:T(128)} %bitcast.64.core_ref, s32[2]{0:T(128)S(1)} %copy-done.23, bf16[1024,2304]{1,0:T(8,128)(2,1)S(1)} %get-tuple-element.151.qkv_ref.q_ref.k_ref.v_ref, ...), custom_call_target="tpu_custom_call", output_to_operand_aliasing={{0}: (3, {}), {1}: (4, {})} | custom-call | flops 24000000000 | bytes 9600000 | tf_op jit(solution)/shard_map/attend/pallas_call | solution.py:274
  86.1 18.1 %up.1 = (f32[1024,768]{1,0:T(8,128)}, bf16[1024,768]{1,0:T(8,128)(2,1)S(1)}, bf16[1024,3072]{1,0:T(8,128)(2,1)}, bf16[1024,3072]{1,0:T(8,128)(2,1)}, bf16[1024,768]{1,0:T(8,128)(2,1)S(1)}) custom-call(s32[1]{0:T(128)} %bitcast.64.core_ref, s32[2]{0:T(128)S(1)} %copy-done.23, s32[32]{0:T(128)S(1)} %convert_element_type.409.seat_ref, ...), custom_call_target="tpu_custom_call" | custom-call | flops 24000000000 | bytes 120000000 | tf_op jit(solution)/shard_map/up/pallas_call | solution.py:458
  107.2 9.6 %grad_down.1 = (bf16[3072,384]{1,0:T(8,128)(2,1)S(1)}, bf16[3072,384]{1,0:T(8,128)(2,1)}) custom-call(s32[1]{0:T(128)} %bitcast.64.core_ref, bf16[1024,3072]{1,0:T(8,128)(2,1)} %get-tuple-element.165.refs_0_.e_ref, bf16[1024,768]{1,0:T(8,128)(2,1)S(1)} %get-tuple-element.162.refs_1_.dy_ref), custom_call_target="tpu_custom_call" | custom-call | flops 19327352832 | bytes 50331648 | tf_op jit(solution)/shard_map/grad_down/pallas_call | solution.py:629
  124.1 30.5 %down.1 = (bf16[512,768]{1,0:T(8,128)(2,1)S(1)}, bf16[2,512,768]{2,1,0:T(8,128)(2,1)}, bf16[1024,3072]{1,0:T(8,128)(2,1)}, bf16[1024,768]{1,0:T(8,128)(2,1)S(1)}...) custom-call(s32[1]{0:T(128)} %bitcast.64.core_ref, s32[2]{0:T(128)S(1)} %copy-done.23, ...), custom_call_target="tpu_custom_call" | custom-call | flops 64000000000 | bytes 140000000 | tf_op jit(solution)/shard_map/down/pallas_call | solution.py:554
  159.3 11.9 %grad_up.1 = (bf16[768,1920]{1,0:T(8,128)(2,1)}, bf16[768,1920]{1,0:T(8,128)(2,1)}) custom-call(s32[1]{0:T(128)} %bitcast.64.core_ref, bf16[1024,768]{1,0:T(8,128)(2,1)S(1)} %copy-done.34, bf16[1024,768]{1,0:T(8,128)(2,1)S(1)} %copy-done.32, bf16[1024,768]{1,0:T(8,128)(2,1)S(1)} %copy-done.36, bf16[1024,3072]{1,0:T(8,128)(2,1)} %get-tuple-element.179.refs_3_), custom_call_target="tpu_custom_call" | custom-call | flops 24159191040 | bytes 61341696 | tf_op jit(solution)/shard_map/grad_up/pallas_call | solution.py:629
  176.0 8.4 %attend_back.2 = (bf16[1024,768]{1,0:T(8,128)(2,1)S(1)}, bf16[1024,768]{1,0:T(8,128)(2,1)S(1)}, bf16[1024,768]{1,0:T(8,128)(2,1)S(1)}) custom-call(s32[1]{0:T(128)} %bitcast.64.core_ref, s32[2]{0:T(128)S(1)} %copy-done.23, bf16[1024,2304]{1,0:T(8,128)(2,1)S(1)} %bitcast.267, bf16[1024,2304]{1,0:T(8,128)(2,1)S(1)} %bitcast.267, ...), custom_call_target="tpu_custom_call" | custom-call | flops 48000000000 | bytes 16000000 | tf_op jit(solution)/shard_map/attend_back/pallas_call | solution.py:371
  188.7 15.4 %attend_back.3 = (bf16[1024,768]{1,0:T(8,128)(2,1)S(1)}, bf16[1024,768]{1,0:T(8,128)(2,1)S(1)}, bf16[1024,768]{1,0:T(8,128)(2,1)S(1)}) custom-call(s32[1]{0:T(128)} %bitcast.64.core_ref, s32[2]{0:T(128)S(1)} %copy-done.23, bf16[1024,2304]{1,0:T(8,128)(2,1)S(1)} %bitcast.267, ...), custom_call_target="tpu_custom_call", output_to_operand_aliasing={{0}: (8, {}), {1}: (9, {}), {2}: (10, {})} | custom-call | flops 96000000000 | bytes 32000000 | tf_op jit(solution)/shard_map/attend_back/pallas_call | solution.py:371
  204.2 3.1 %collective-permute-done.33 = bf16[2,4,1,48,1920]{4,3,1,2,0:T(8,128)(2,1)S(1)} collective-permute-done((bf16[2,4,1,48,1920]{4,3,1,2,0:T(8,128)(2,1)S(1)}, bf16[2,4,1,48,1920]{4,3,1,2,0:T(8,128)(2,1)S(1)}, u32[]{:S(2)}, u32[]{:S(2)}) %collective-permute-start.33) | collective-permute-done | bytes 1474592 | tf_op jit(solution)/shard_map/ppermute | solution.py:827
  208.4 4.8 %grad_qkv.1 = (bf16[768,1152]{1,0:T(8,128)(2,1)S(1)}, bf16[768,1152]{1,0:T(8,128)(2,1)S(1)}) custom-call(s32[1]{0:T(128)} %bitcast.64.core_ref, bf16[1024,768]{1,0:T(8,128)(2,1)S(1)} %copy-done.29, bf16[1024,768]{1,0:T(8,128)(2,1)S(1)} %get-tuple-element.211.refs_1_.dq_ref, bf16[1024,768]{1,0:T(8,128)(2,1)S(1)} %get-tuple-element.202.refs_2_.dk_ref, ...), custom_call_target="tpu_custom_call" | custom-call | flops 14495514624 | bytes 39321600 | tf_op jit(solution)/shard_map/grad_qkv/pallas_call | solution.py:629
  213.3 5.9 %collective-permute-done.34 = bf16[4,1,48,1920]{3,2,1,0:T(8,128)(2,1)S(1)} collective-permute-done((bf16[4,1,48,1920]{3,2,1,0:T(8,128)(2,1)S(1)}, bf16[4,1,48,1920]{3,2,1,0:T(8,128)(2,1)S(1)}, u32[]{:S(2)}, u32[]{:S(2)}) %collective-permute-start.34) | collective-permute-done | bytes 737312 | tf_op jit(solution)/shard_map/ppermute | solution.py:827
  224.8 7.0 %last.1 = (f32[512,768]{1,0:T(8,128)S(1)}, f32[2,512,768]{2,1,0:T(8,128)}, f32[16,768]{1,0:T(8,128)S(1)}) custom-call(s32[1]{0:T(128)} %bitcast.64.core_ref, bf16[1024,768]{1,0:T(8,128)(2,1)S(1)} %maximum_select_fusion.x_ref, f32[1024,768]{1,0:T(8,128)S(1)} %copy-done.27, bf16[1024,768]{1,0:T(8,128)(2,1)S(1)} %get-tuple-element.211.refs_1_.dq_ref, ...), custom_call_target="tpu_custom_call" | custom-call | flops 14495514624 | bytes 64000000 | tf_op jit(solution)/shard_map/last/pallas_call | solution.py:693
  237.3 2.7 %collective-permute-done.39 = bf16[2,48,1920]{2,1,0:T(8,128)(2,1)S(1)} collective-permute-done((bf16[2,48,1920]{2,1,0:T(8,128)(2,1)S(1)}, bf16[2,48,1920]{2,1,0:T(8,128)(2,1)S(1)}, u32[]{:S(2)}, u32[]{:S(2)}) %collective-permute-start.39) | collective-permute-done | bytes 368672 | tf_op jit(solution)/shard_map/ppermute | solution.py:827
  241.0 3.9 %collective-permute-done.38 = bf16[4,1,48,1152]{3,2,1,0:T(8,128)(2,1)S(1)} collective-permute-done((bf16[4,1,48,1152]{3,2,1,0:T(8,128)(2,1)S(1)}, bf16[4,1,48,1152]{3,2,1,0:T(8,128)(2,1)S(1)}, u32[]{:S(2)}, u32[]{:S(2)}) %collective-permute-start.38) | collective-permute-done | bytes 442400 | tf_op jit(solution)/shard_map/ppermute | solution.py:827
  247.8 2.7 collective-permute-start.40
  250.4 5.8 %collective-permute-done.43 = bf16[48,1920]{1,0:T(8,128)(2,1)S(1)} collective-permute-done((bf16[48,1920]{1,0:T(8,128)(2,1)S(1)}, bf16[48,1920]{1,0:T(8,128)(2,1)S(1)}, u32[]{:S(2)}, u32[]{:S(2)}) %collective-permute-start.43) | collective-permute-done | bytes 184352 | tf_op jit(solution)/shard_map/ppermute | solution.py:827
  258.9 3.0 %collective-permute-start.41 = (bf16[48,1152]{1,0:T(8,128)(2,1)S(1)}, bf16[48,1152]{1,0:T(8,128)(2,1)S(1)}, u32[]{:S(2)}, u32[]{:S(2)}) collective-permute-start(bf16[48,1152]{1,0:T(8,128)(2,1)S(1)} %fusion.18), channel_id=1, source_target_pairs={{0,8},{1,9},{2,10},{3,11},{4,12},{5,13},{6,14},{7,15},{8,0},{9,1},... | collective-permute-start | bytes 331784 | tf_op jit(solution)/shard_map/ppermute | solution.py:827
  (256 shorter events, 78.7 us)
Async XLA Ops:
  3.2 13.6 %collective-permute-start.2 = (bf16[48,1280]{1,0:T(8,128)(2,1)S(1)}, bf16[48,1280]{1,0:T(8,128)(2,1)S(1)}, u32[]{:S(2)}, u32[]{:S(2)}) collective-permute-start(bf16[48,1280]{1,0:T(8,128)(2,1)S(1)} %get-tuple-element.269), channel_id=1, source_target_pairs={{0,16},{1,17},{2,18},{3,19},{4,20},{5,21},{6,22},{7,23},{8,24},{9,... | collective-permute-start | bytes 368648 | tf_op jit(solution)/shard_map/ppermute | solution.py:827
  28.3 19.1 %collective-permute-start.7 = (bf16[2,4,48,1280]{3,2,1,0:T(8,128)(2,1)S(1)}, bf16[2,4,48,1280]{3,2,1,0:T(8,128)(2,1)}, u32[]{:S(2)}, u32[]{:S(2)}) collective-permute-start(bf16[2,4,48,1280]{3,2,1,0:T(8,128)(2,1)S(1)} %pad_maximum_fusion.2.refs_0_), channel_id=1, source_target_pairs={{0,4},{1,3},{2,6},{3,1},{4,0},{5,7},{6,2},{7,5},{8,12},{9,11},{10,... | collective-permute-start | bytes 2949128 | tf_op jit(solution)/shard_map/ppermute | solution.py:827
  29.9 17.4 %collective-permute-start.9 = (bf16[2,48,1920]{2,1,0:T(8,128)(2,1)S(1)}, bf16[2,48,1920]{2,1,0:T(8,128)(2,1)S(1)}, u32[]{:S(2)}, u32[]{:S(2)}) collective-permute-start(bf16[2,48,1920]{2,1,0:T(8,128)(2,1)S(1)} %pad_maximum_fusion.5), channel_id=1, source_target_pairs={{0,16},{1,17},{2,18},{3,19},{4,20},{5,21},{6,22},{7,23},{8,24},{9,... | collective-permute-start | bytes 1105928 | tf_op jit(solution)/shard_map/ppermute | solution.py:827
  31.8 17.7 %collective-permute-start.8 = (bf16[2,4,48,1280]{3,2,1,0:T(8,128)(2,1)S(1)}, bf16[2,4,48,1280]{3,2,1,0:T(8,128)(2,1)}, u32[]{:S(2)}, u32[]{:S(2)}) collective-permute-start(bf16[2,4,48,1280]{3,2,1,0:T(8,128)(2,1)S(1)} %pad_maximum_fusion.2.refs_0_), channel_id=1, source_target_pairs={{0,1},{1,0},{2,3},{3,2},{4,5},{5,4},{6,7},{7,6},{8,9},{9,8},{10,11... | collective-permute-start | bytes 2949128 | tf_op jit(solution)/shard_map/ppermute | solution.py:827
  47.5 30.6 %collective-permute-start.16 = (bf16[4,48,1920]{2,1,0:T(8,128)(2,1)S(1)}, bf16[4,48,1920]{2,1,0:T(8,128)(2,1)S(1)}, u32[]{:S(2)}, u32[]{:S(2)}) collective-permute-start(bf16[4,48,1920]{2,1,0:T(8,128)(2,1)S(1)} %constant_dynamic-update-slice_fusion), channel_id=1, source_target_pairs={{0,1},{1,0},{2,3},{3,2},{4,5},{5,4},{6,7},{7,6},{8,9},{9,8},{10,11... | collective-permute-start | bytes 2211848 | tf_op jit(solution)/shard_map/ppermute | solution.py:827
  48.0 17.8 %collective-permute-start.13 = (bf16[4,48,1920]{2,1,0:T(8,128)(2,1)S(1)}, bf16[4,48,1920]{2,1,0:T(8,128)(2,1)S(1)}, u32[]{:S(2)}, u32[]{:S(2)}) collective-permute-start(bf16[4,48,1920]{2,1,0:T(8,128)(2,1)S(1)} %constant_dynamic-update-slice_fusion), channel_id=1, source_target_pairs={{0,2},{1,5},{2,0},{3,7},{4,6},{5,1},{6,4},{7,3},{8,10},{9,13},{10,... | collective-permute-start | bytes 2211848 | tf_op jit(solution)/shard_map/ppermute | solution.py:827
  48.5 20.0 %collective-permute-start.11 = (bf16[2,192,384]{2,1,0:T(8,128)(2,1)}, bf16[2,192,384]{2,1,0:T(8,128)(2,1)S(1)}, u32[]{:S(2)}, u32[]{:S(2)}) collective-permute-start(bf16[2,192,384]{2,1,0:T(8,128)(2,1)} %pad_maximum_fusion.7), channel_id=1, source_target_pairs={{0,16},{1,17},{2,18},{3,19},{4,20},{5,21},{6,22},{7,23},{8,24},{9,... | collective-permute-start | bytes 884744 | tf_op jit(solution)/shard_map/ppermute | solution.py:827
  49.5 28.6 %collective-permute-start.12 = (bf16[4,48,1920]{2,1,0:T(8,128)(2,1)S(1)}, bf16[4,48,1920]{2,1,0:T(8,128)(2,1)S(1)}, u32[]{:S(2)}, u32[]{:S(2)}) collective-permute-start(bf16[4,48,1920]{2,1,0:T(8,128)(2,1)S(1)} %constant_dynamic-update-slice_fusion), channel_id=1, source_target_pairs={{0,4},{1,3},{2,6},{3,1},{4,0},{5,7},{6,2},{7,5},{8,12},{9,11},{10,... | collective-permute-start | bytes 2211848 | tf_op jit(solution)/shard_map/ppermute | solution.py:827
  65.8 14.2 %collective-permute-start.17 = (bf16[4,48,1920]{2,1,0:T(8,128)(2,1)S(1)}, bf16[4,48,1920]{2,1,0:T(8,128)(2,1)S(1)}, u32[]{:S(2)}, u32[]{:S(2)}) collective-permute-start(bf16[4,48,1920]{2,1,0:T(8,128)(2,1)S(1)} %collective-permute-done.13), channel_id=1, source_target_pairs={{0,1},{1,0},{2,3},{3,2},{4,5},{5,4},{6,7},{7,6},{8,9},{9,8},{10,11... | collective-permute-start | bytes 2211848 | tf_op jit(solution)/shard_map/ppermute | solution.py:827
  68.7 16.7 %collective-permute-start.15 = (bf16[512,768]{1,0:T(8,128)(2,1)S(1)}, bf16[512,768]{1,0:T(8,128)(2,1)S(1)}, u32[]{:S(2)}, u32[]{:S(2)}) collective-permute-start(bf16[512,768]{1,0:T(8,128)(2,1)S(1)} %get-tuple-element.257), channel_id=1, source_target_pairs={{0,1},{1,0},{2,3},{3,2},{4,5},{5,4},{6,7},{7,6},{8,9},{9,8},{10,11... | collective-permute-start | bytes 2359304 | tf_op jit(solution)/shard_map/ppermute | solution.py:827
  78.3 39.9 %collective-permute-start.23 = (bf16[4,192,384]{2,1,0:T(8,128)(2,1)S(1)}, bf16[4,192,384]{2,1,0:T(8,128)(2,1)S(1)}, u32[]{:S(2)}, u32[]{:S(2)}) collective-permute-start(bf16[4,192,384]{2,1,0:T(8,128)(2,1)S(1)} %constant_dynamic-update-slice_fusion.2), channel_id=1, source_target_pairs={{0,1},{1,0},{2,3},{3,2},{4,5},{5,4},{6,7},{7,6},{8,9},{9,8},{10,11... | collective-permute-start | bytes 1769480 | tf_op jit(solution)/shard_map/ppermute | solution.py:827
  78.7 28.5 %collective-permute-start.21 = (bf16[4,192,384]{2,1,0:T(8,128)(2,1)S(1)}, bf16[4,192,384]{2,1,0:T(8,128)(2,1)S(1)}, u32[]{:S(2)}, u32[]{:S(2)}) collective-permute-start(bf16[4,192,384]{2,1,0:T(8,128)(2,1)S(1)} %constant_dynamic-update-slice_fusion.2), channel_id=1, source_target_pairs={{0,4},{1,3},{2,6},{3,1},{4,0},{5,7},{6,2},{7,5},{8,12},{9,11},{10,... | collective-permute-start | bytes 1769480 | tf_op jit(solution)/shard_map/ppermute | solution.py:827
  84.7 20.7 %collective-permute-start.20 = (bf16[4,192,384]{2,1,0:T(8,128)(2,1)S(1)}, bf16[4,192,384]{2,1,0:T(8,128)(2,1)}, u32[]{:S(2)}, u32[]{:S(2)}) collective-permute-start(bf16[4,192,384]{2,1,0:T(8,128)(2,1)S(1)} %constant_dynamic-update-slice_fusion.2), channel_id=1, source_target_pairs={{0,2},{1,5},{2,0},{3,7},{4,6},{5,1},{6,4},{7,3},{8,10},{9,13},{10,... | collective-permute-start | bytes 1769480 | tf_op jit(solution)/shard_map/ppermute | solution.py:827
  105.5 14.3 %collective-permute-start.24 = (bf16[4,192,384]{2,1,0:T(8,128)(2,1)}, bf16[4,192,384]{2,1,0:T(8,128)(2,1)S(1)}, u32[]{:S(2)}, u32[]{:S(2)}) collective-permute-start(bf16[4,192,384]{2,1,0:T(8,128)(2,1)} %collective-permute-done.20), channel_id=1, source_target_pairs={{0,1},{1,0},{2,3},{3,2},{4,5},{5,4},{6,7},{7,6},{8,9},{9,8},{10,11... | collective-permute-start | bytes 1769480 | tf_op jit(solution)/shard_map/ppermute | solution.py:827
  118.9 36.7 %collective-permute-start.27 = (bf16[3072,384]{1,0:T(8,128)(2,1)}, bf16[3072,384]{1,0:T(8,128)(2,1)S(1)}, u32[]{:S(2)}, u32[]{:S(2)}) collective-permute-start(bf16[3072,384]{1,0:T(8,128)(2,1)} %get-tuple-element.177), channel_id=1, source_target_pairs={{0,1},{1,0},{2,3},{3,2},{4,5},{5,4},{6,7},{7,6},{8,9},{9,8},{10,11... | collective-permute-start | bytes 7077896 | tf_op jit(solution)/shard_map/ppermute | solution.py:827
  157.2 16.5 %collective-permute-start.29 = (bf16[2,4,1,192,384]{4,3,1,2,0:T(8,128)(2,1)}, bf16[2,4,1,192,384]{4,3,1,2,0:T(8,128)(2,1)}, u32[]{:S(2)}, u32[]{:S(2)}) collective-permute-start(bf16[2,4,1,192,384]{4,3,1,2,0:T(8,128)(2,1)} %pad_maximum_fusion.1), channel_id=1, source_target_pairs={{0,2},{1,5},{2,0},{3,7},{4,6},{5,1},{6,4},{7,3},{8,10},{9,13},{10,... | collective-permute-start | bytes 3538952 | tf_op jit(solution)/shard_map/ppermute | solution.py:827
  171.3 15.8 %collective-permute-start.28 = (bf16[768,1920]{1,0:T(8,128)(2,1)}, bf16[768,1920]{1,0:T(8,128)(2,1)S(1)}, u32[]{:S(2)}, u32[]{:S(2)}) collective-permute-start(bf16[768,1920]{1,0:T(8,128)(2,1)} %get-tuple-element.180), channel_id=1, source_target_pairs={{0,1},{1,0},{2,3},{3,2},{4,5},{5,4},{6,7},{7,6},{8,9},{9,8},{10,11... | collective-permute-start | bytes 8847368 | tf_op jit(solution)/shard_map/ppermute | solution.py:827
  186.9 17.1 %collective-permute-start.32 = (bf16[2,192,384]{2,1,0:T(8,128)(2,1)S(1)}, bf16[2,192,384]{2,1,0:T(8,128)(2,1)S(1)}, u32[]{:S(2)}, u32[]{:S(2)}) collective-permute-start(bf16[2,192,384]{2,1,0:T(8,128)(2,1)S(1)} %pad_maximum_fusion.8), channel_id=1, source_target_pairs={{0,16},{1,17},{2,18},{3,19},{4,20},{5,21},{6,22},{7,23},{8,24},{9,... | collective-permute-start | bytes 884744 | tf_op jit(solution)/shard_map/ppermute | solution.py:827
  187.9 19.4 %collective-permute-start.33 = (bf16[2,4,1,48,1920]{4,3,1,2,0:T(8,128)(2,1)S(1)}, bf16[2,4,1,48,1920]{4,3,1,2,0:T(8,128)(2,1)S(1)}, u32[]{:S(2)}, u32[]{:S(2)}) collective-permute-start(bf16[2,4,1,48,1920]{4,3,1,2,0:T(8,128)(2,1)S(1)} %pad_maximum_fusion), channel_id=1, source_target_pairs={{0,2},{1,5},{2,0},{3,7},{4,6},{5,1},{6,4},{7,3},{8,10},{9,13},{10,... | collective-permute-start | bytes 4423688 | tf_op jit(solution)/shard_map/ppermute | solution.py:827
  204.1 15.8 %collective-permute-start.31 = (bf16[512,768]{1,0:T(8,128)(2,1)S(1)}, bf16[512,768]{1,0:T(8,128)(2,1)S(1)}, u32[]{:S(2)}, u32[]{:S(2)}) collective-permute-start(bf16[512,768]{1,0:T(8,128)(2,1)S(1)} %get-tuple-element.195), channel_id=1, source_target_pairs={{0,1},{1,0},{2,3},{3,2},{4,5},{5,4},{6,7},{7,6},{8,9},{9,8},{10,11... | collective-permute-start | bytes 2359304 | tf_op jit(solution)/shard_map/ppermute | solution.py:827
  220.4 19.6 %collective-permute-start.39 = (bf16[2,48,1920]{2,1,0:T(8,128)(2,1)S(1)}, bf16[2,48,1920]{2,1,0:T(8,128)(2,1)S(1)}, u32[]{:S(2)}, u32[]{:S(2)}) collective-permute-start(bf16[2,48,1920]{2,1,0:T(8,128)(2,1)S(1)} %pad_maximum_fusion.6), channel_id=1, source_target_pairs={{0,16},{1,17},{2,18},{3,19},{4,20},{5,21},{6,22},{7,23},{8,24},{9,... | collective-permute-start | bytes 1105928 | tf_op jit(solution)/shard_map/ppermute | solution.py:827
  232.0 30.0 %collective-permute-start.46 = (f32[192,384]{1,0:T(8,128)S(1)}, f32[192,384]{1,0:T(8,128)S(1)}, u32[]{:S(2)}, u32[]{:S(2)}) collective-permute-start(f32[192,384]{1,0:T(8,128)S(1)} %fusion.16.refs_0_), channel_id=1, source_target_pairs={{0,1},{1,0},{2,3},{3,2},{4,5},{5,4},{6,7},{7,6},{8,9},{9,8},{10,11... | collective-permute-start | bytes 884744 | tf_op jit(solution)/shard_map/ppermute | solution.py:827
  240.9 15.6 %collective-permute-start.37 = (f32[512,768]{1,0:T(8,128)S(1)}, f32[512,768]{1,0:T(8,128)S(1)}, u32[]{:S(2)}, u32[]{:S(2)}) collective-permute-start(f32[512,768]{1,0:T(8,128)S(1)} %get-tuple-element.217), channel_id=1, source_target_pairs={{0,1},{1,0},{2,3},{3,2},{4,5},{5,4},{6,7},{7,6},{8,9},{9,8},{10,11... | collective-permute-start | bytes 4718600 | tf_op jit(solution)/shard_map/ppermute | solution.py:827
  245.4 13.4 %collective-permute-start.50 = (f32[16,768]{1,0:T(8,128)S(1)}, f32[16,768]{1,0:T(8,128)S(1)}, u32[]{:S(2)}, u32[]{:S(2)}) collective-permute-start(f32[16,768]{1,0:T(8,128)S(1)} %add.658), channel_id=1, source_target_pairs={{0,8},{1,9},{2,10},{3,11},{4,12},{5,13},{6,14},{7,15},{8,0},{9,1},... | collective-permute-start | bytes 147464 | tf_op jit(solution)/shard_map/ppermute | solution.py:827
  (78 other events, 464.5 us)

commit v3 on v2

--- a/solution.py
+++ b/solution.py
@@ -476,7 +476,7 @@
             wide,
             low,
         ],
-        compiler_params=params(40),
+        compiler_params=params(48),
         cost_estimate=cost(6e9, 30e6, rows * FF),
     )(core, lengths, seats, x, a, og, vec, *group.arrays)
 
@@ -582,7 +582,7 @@
             jax.ShapeDtypeStruct((rows, D), BF16),
             jax.ShapeDtypeStruct((16, D), F32),
         ],
-        compiler_params=params(40),
+        compiler_params=params(48),
         cost_estimate=cost(1.6e10, 35e6),
     )(core, lengths, seats, mid, e, slope, dy, vec, *up_group.arrays, *down_group.arrays)
 
@@ -642,6 +642,38 @@
         compiler_params=params(16 if mode == "turns" else 48),
         cost_estimate=cost(2 * rows * height * width, rows * (height + width) * 2 + height * width * 2),
     )(core, *lefts, *rights)
+
+
+def half_grad_kernel(lefts, core_ref, *refs):
+    out_ref = refs[-1]
+    parts = [mm(refs[at][...], refs[lefts + at][...], TN).astype(BF16) for at in range(lefts)]
+    out_ref[...] = parts[0] if lefts == 1 else jnp.concatenate(parts, axis=1)
+
+
+def half_grad_call(core, products, block, name, other):
+    rows, height = products[0][0].shape
+    widths = [right.shape[1] // 2 for _, right in products]
+
+    def half(c):
+        return 1 - c[0] if other else c[0]
+
+    return pl.pallas_call(
+        functools.partial(half_grad_kernel, len(products)),
+        name=name,
+        grid_spec=pltpu.PrefetchScalarGridSpec(
+            num_scalar_prefetch=1,
+            grid=(height // block,),
+            in_specs=[pl.BlockSpec((rows, block), lambda i, c: (0, i))] * len(products)
+            + [
+                pl.BlockSpec((rows, width), lambda i, c: (0, half(c)), pipeline_mode=pl.Buffered(1))
+                for width in widths
+            ],
+            out_specs=pl.BlockSpec((block, sum(widths)), lambda i, c: (i, 0)),
+        ),
+        out_shape=jax.ShapeDtypeStruct((height, sum(widths)), BF16),
+        compiler_params=params(48),
+        cost_estimate=cost(2 * rows * height * sum(widths), rows * (height + sum(widths)) * 2 + height * sum(widths) * 2),
+    )(core, *[left for left, _ in products], *[right for _, right in products])
 
 
 def last_kernel(
@@ -1018,27 +1050,27 @@
     )
 
     d_pair = after(grid.swap(d_other), dz)
-    u_own, u_other = weight_grad_call(
-        core_arr, [(a, [dmb]), (h2, [after(dz, d_pair)])], 384, "grad_up"
-    )
+    u_other = half_grad_call(core_arr, [(a, dmb), (h2, after(dz, d_pair))], 384, "grad_up", True)
+    u_own = half_grad_call(core_arr, [(a, dmb), (h2, after(dz, u_other))], 384, "grad_up", False)
     d_kept = grid.scatter_first(d_own, d_pair, u_own)
 
     def back_call(start, count, before, *needs):
         return attend_back_call(core_arr, lengths, qkv, a, after(da, *needs), lse, start, count, before)
 
-    back = back_call(0, 2, (), u_own, *d_kept[1])
+    back = back_call(0, 1, (), u_own, *d_kept[1])
+    u_pair = after(grid.swap(u_other), *back)
     d_sum, d_here = grid.scatter_second(d_kept, *back)
-    u_pair = after(grid.swap(u_other), *back)
-    back = back_call(2, 4, back, u_pair, *d_here)
+    back = back_call(1, 3, back, u_pair, *d_here)
+    u_kept = grid.scatter_first(u_own, u_pair, *back)
     d_parts, d_got = grid.scatter_bit(grid.order_z(d_sum), *back)
-    u_kept = grid.scatter_first(u_own, u_pair, *back)
+    back = back_call(4, 2, back, d_got, *u_kept[1])
+    u_sum, u_here = grid.scatter_second(u_kept, *back)
     dq, dk, dv = back
     block_out = both_slots(out_mine, after(grid.swap(after(out_theirs, back[0])), dq))
     q_own, q_other = weight_grad_call(
-        core_arr, [(h1, [after(dq, d_got, *u_kept[1]), dk, dv])], 384, "grad_qkv", "turns"
+        core_arr, [(h1, [after(dq, *u_here), dk, dv])], 384, "grad_qkv", "turns"
     )
-    u_sum, u_here = grid.scatter_second(u_kept, q_own)
-    q_pair = grid.swap(after(q_other, *u_here))
+    q_pair = grid.swap(q_other)
     in_theirs, in_mine, acc = last_call(
         core_arr, x, dm, after(dq, q_own, q_pair), dk, dv, w_back, vec, acc_mid
     )

time: 273 us -> 278 us (1.018)
  local copies, waits for them, and re-layouts: 18.2 us -> 12.3 us
  other arithmetic: 11.9 us -> 15.5 us
  Pallas kernels: 133 us -> 136 us
    pallas_call x0 -> x2, Pallas kernels: none -> 14.4 us  [half_grad_call(): pl.pallas_call(functools.partial(half_grad_kernel, len(products)), name=n...]
    pallas_call x3 -> x2, Pallas kernels: 26.3 us -> 14.2 us  [weight_grad_call(): pl.pallas_call(functools.partial(weight_grad_kernel, len(lefts), [len(gro...]
    unnamed x102, local copies, waits for them, and re-layouts: 15.7 us -> 9.77 us
    pallas_call x2 -> x3, Pallas kernels: 23.8 us -> 24 us  [attend_back_call(): pl.pallas_call(attend_back_kernel, name='attend_back', grid_spec=pltpu.Pr...]
  transfers between devices with their start and end apart: 52 -> 52, of which waited for: 20 -> 19; matrix products, arithmetic and copies ran while one was open for 4% -> 5% of each run, Pallas kernels for 49% -> 48%
where the time goes in v3:
time: 278 us; the launch traced here: 274 us
  Pallas kernels  136 us (49%)
  waiting for transfers between devices  65.6 us (24%)
  starting transfers between devices  42.3 us (15%)
  other arithmetic  15.5 us (6%)
  local copies, waits for them, and re-layouts  12.3 us (4%)
    ppermute x52, waiting for transfers between devices, permute(): return lax.ppermute(value, ('dp', 'seq'), pairs)  65.6 us
    ppermute x52, starting transfers between devices, permute(): return lax.ppermute(value, ('dp', 'seq'), pairs)  42.3 us
    pallas_call x1, Pallas kernels, down_call(): pl.pallas_call(functools.partial(down_kernel, up_group, down_group), name...  29.7 us
    pallas_call x3, Pallas kernels, attend_back_call(): pl.pallas_call(attend_back_kernel, name='attend_back', grid_spec=pltpu.Pr...  24 us
    pallas_call x1, Pallas kernels, up_call(): pl.pallas_call(functools.partial(up_kernel, group), name='up', grid_spec=...  19.6 us
    pallas_call x2, Pallas kernels, half_grad_call(): pl.pallas_call(functools.partial(half_grad_kernel, len(products)), name=n...  14.4 us
    pallas_call x2, Pallas kernels, weight_grad_call(): pl.pallas_call(functools.partial(weight_grad_kernel, len(lefts), [len(gro...  14.2 us
    pallas_call x2, Pallas kernels, attend_call(): pl.pallas_call(functools.partial(attend_kernel, first), name='attend', gr...  13.7 us
  transfers between devices with their start and end apart: 52, of which 19 were waited for; matrix products, arithmetic and copies ran while one was open for 5% of the time, Pallas kernels for 48%

profile of v3, /device:TPU:0, one launch (start us, length us, event | category | flops | bytes accessed | tf_op | source)
XLA Modules:
  0.0 274.1 jit_solution(13398696393727600335)
XLA Ops:
  3.2 4.1 %collective-permute-start.2 = (bf16[48,1280]{1,0:T(8,128)(2,1)S(1)}, bf16[48,1280]{1,0:T(8,128)(2,1)S(1)}, u32[]{:S(2)}, u32[]{:S(2)}) collective-permute-start(bf16[48,1280]{1,0:T(8,128)(2,1)S(1)} %get-tuple-element.273), channel_id=1, source_target_pairs={{0,16},{1,17},{2,18},{3,19},{4,20},{5,21},{6,22},{7,23},{8,24},{9,... | collective-permute-start | bytes 368648 | tf_op jit(solution)/shard_map/ppermute | solution.py:859
  13.0 3.8 %collective-permute-done.2 = bf16[48,1280]{1,0:T(8,128)(2,1)S(1)} collective-permute-done((bf16[48,1280]{1,0:T(8,128)(2,1)S(1)}, bf16[48,1280]{1,0:T(8,128)(2,1)S(1)}, u32[]{:S(2)}, u32[]{:S(2)}) %collective-permute-start.2) | collective-permute-done | bytes 122912 | tf_op jit(solution)/shard_map/ppermute | solution.py:859
  25.3 2.9 %collective-permute-done.4 = bf16[4,48,1280]{2,1,0:T(8,128)(2,1)S(1)} collective-permute-done((bf16[4,48,1280]{2,1,0:T(8,128)(2,1)S(1)}, bf16[4,48,1280]{2,1,0:T(8,128)(2,1)S(1)}, u32[]{:S(2)}, u32[]{:S(2)}) %collective-permute-start.4) | collective-permute-done | bytes 491552 | tf_op jit(solution)/shard_map/ppermute | solution.py:859
  31.9 15.5 %collective-permute-done.9 = bf16[2,48,1920]{2,1,0:T(8,128)(2,1)S(1)} collective-permute-done((bf16[2,48,1920]{2,1,0:T(8,128)(2,1)S(1)}, bf16[2,48,1920]{2,1,0:T(8,128)(2,1)S(1)}, u32[]{:S(2)}, u32[]{:S(2)}) %collective-permute-start.9) | collective-permute-done | bytes 368672 | tf_op jit(solution)/shard_map/ppermute | solution.py:859
  51.1 9.1 %qkv.1 = (bf16[1024,768]{1,0:T(8,128)(2,1)S(1)}, bf16[1024,2304]{1,0:T(8,128)(2,1)S(1)}, f32[16,768]{1,0:T(8,128)S(1)}, bf16[2304,768]{1,0:T(8,128)(2,1)S(1)}) custom-call(s32[1]{0:T(128)} %bitcast.64.core_ref, s32[32]{0:T(128)S(1)} %convert_element_type.410.seat_ref, bf16[1024,768]{1,0:T(8,128)(2,1)S(1)} %maximum_select_fusion.x_ref, ...), custom_call_target="tpu_custom_call" | custom-call | flops 14495514624 | bytes 40000000 | tf_op jit(solution)/shard_map/qkv/pallas_call | solution.py:161
  69.2 8.9 %attend.2 = (bf16[1024,768]{1,0:T(8,128)(2,1)S(1)}, f32[6,8,1024]{2,1,0:T(8,128)S(1)}) custom-call(s32[1]{0:T(128)} %bitcast.64.core_ref, s32[2]{0:T(128)S(1)} %copy-done.24, bf16[1024,2304]{1,0:T(8,128)(2,1)S(1)} %get-tuple-element.153.qkv_ref.q_ref.k_ref.v_ref), custom_call_target="tpu_custom_call" | custom-call | flops 48000000000 | bytes 19200000 | tf_op jit(solution)/shard_map/attend/pallas_call | solution.py:274
  80.0 4.8 %attend.3 = (bf16[1024,768]{1,0:T(8,128)(2,1)S(1)}, f32[6,8,1024]{2,1,0:T(8,128)S(1)}) custom-call(s32[1]{0:T(128)} %bitcast.64.core_ref, s32[2]{0:T(128)S(1)} %copy-done.24, bf16[1024,2304]{1,0:T(8,128)(2,1)S(1)} %get-tuple-element.153.qkv_ref.q_ref.k_ref.v_ref, ...), custom_call_target="tpu_custom_call", output_to_operand_aliasing={{0}: (3, {}), {1}: (4, {})} | custom-call | flops 24000000000 | bytes 9600000 | tf_op jit(solution)/shard_map/attend/pallas_call | solution.py:274
  87.3 19.6 %up.1 = (f32[1024,768]{1,0:T(8,128)}, bf16[1024,768]{1,0:T(8,128)(2,1)}, bf16[1024,3072]{1,0:T(8,128)(2,1)}, bf16[1024,3072]{1,0:T(8,128)(2,1)}, bf16[1024,768]{1,0:T(8,128)(2,1)}) custom-call(s32[1]{0:T(128)} %bitcast.64.core_ref, s32[2]{0:T(128)S(1)} %copy-done.24, s32[32]{0:T(128)S(1)} %convert_element_type.409.seat_ref, bf16[1024,768]{1,0:T(8,128)(2,1)} %copy-done, ...), custom_call_target="tpu_custom_call" | custom-call | flops 24000000000 | bytes 120000000 | tf_op jit(solution)/shard_map/up/pallas_call | solution.py:458
  110.2 9.5 %grad_down.1 = (bf16[3072,384]{1,0:T(8,128)(2,1)S(1)}, bf16[3072,384]{1,0:T(8,128)(2,1)}) custom-call(s32[1]{0:T(128)} %bitcast.64.core_ref, bf16[1024,3072]{1,0:T(8,128)(2,1)} %get-tuple-element.167.refs_0_.e_ref, bf16[1024,768]{1,0:T(8,128)(2,1)S(1)} %copy-done.35), custom_call_target="tpu_custom_call" | custom-call | flops 19327352832 | bytes 50331648 | tf_op jit(solution)/shard_map/grad_down/pallas_call | solution.py:629
  121.9 29.7 %down.1 = (bf16[512,768]{1,0:T(8,128)(2,1)}, bf16[2,512,768]{2,1,0:T(8,128)(2,1)}, bf16[1024,3072]{1,0:T(8,128)(2,1)}, bf16[1024,768]{1,0:T(8,128)(2,1)}, f32[10...) custom-call(s32[1]{0:T(128)} %bitcast.64.core_ref, s32[2]{0:T(128)S(1)} %copy-done.24, ...), custom_call_target="tpu_custom_call" | custom-call | flops 64000000000 | bytes 140000000 | tf_op jit(solution)/shard_map/down/pallas_call | solution.py:554
  154.9 7.1 %grad_up.2 = bf16[768,1920]{1,0:T(8,128)(2,1)} custom-call(s32[1]{0:T(128)} %bitcast.64.core_ref, bf16[1024,768]{1,0:T(8,128)(2,1)S(1)} %copy-done.32, bf16[1024,768]{1,0:T(8,128)(2,1)S(1)} %copy-done.29, bf16[1024,768]{1,0:T(8,128)(2,1)S(1)} %copy-done.30, bf16[1024,3072]{1,0:T(8,128)(2,1)} %get-tuple-element.185.refs_3_), custom_call_target="tpu_custom_call" | custom-call | flops 12079595520 | bytes 33816576 | tf_op jit(solution)/shard_map/grad_up/pallas_call | solution.py:660
  162.4 7.4 %grad_up.3 = bf16[768,1920]{1,0:T(8,128)(2,1)} custom-call(s32[1]{0:T(128)} %bitcast.64.core_ref, bf16[1024,768]{1,0:T(8,128)(2,1)S(1)} %copy-done.32, bf16[1024,768]{1,0:T(8,128)(2,1)S(1)} %copy-done.29, bf16[1024,768]{1,0:T(8,128)(2,1)S(1)} %copy-done.30, bf16[1024,3072]{1,0:T(8,128)(2,1)} %get-tuple-element.185.refs_3_), custom_call_target="tpu_custom_call" | custom-call | flops 12079595520 | bytes 33816576 | tf_op jit(solution)/shard_map/grad_up/pallas_call | solution.py:660
  172.0 4.2 %attend_back.3 = (bf16[1024,768]{1,0:T(8,128)(2,1)S(1)}, bf16[1024,768]{1,0:T(8,128)(2,1)S(1)}, bf16[1024,768]{1,0:T(8,128)(2,1)S(1)}) custom-call(s32[1]{0:T(128)} %bitcast.64.core_ref, s32[2]{0:T(128)S(1)} %copy-done.24, bf16[1024,2304]{1,0:T(8,128)(2,1)S(1)} %bitcast.268, bf16[1024,2304]{1,0:T(8,128)(2,1)S(1)} %bitcast.268, ...), custom_call_target="tpu_custom_call" | custom-call | flops 24000000000 | bytes 8000000 | tf_op jit(solution)/shard_map/attend_back/pallas_call | solution.py:371
  176.2 4.9 %collective-permute-done.29 = bf16[4,1,192,384]{3,2,1,0:T(8,128)(2,1)S(1)} collective-permute-done((bf16[4,1,192,384]{3,2,1,0:T(8,128)(2,1)S(1)}, bf16[4,1,192,384]{3,2,1,0:T(8,128)(2,1)S(1)}, u32[]{:S(2)}, u32[]{:S(2)}) %collective-permute-start.29) | collective-permute-done | bytes 589856 | tf_op jit(solution)/shard_map/ppermute | solution.py:859
  185.7 11.7 %attend_back.4 = (bf16[1024,768]{1,0:T(8,128)(2,1)S(1)}, bf16[1024,768]{1,0:T(8,128)(2,1)S(1)}, bf16[1024,768]{1,0:T(8,128)(2,1)S(1)}) custom-call(s32[1]{0:T(128)} %bitcast.64.core_ref, s32[2]{0:T(128)S(1)} %copy-done.24, bf16[1024,2304]{1,0:T(8,128)(2,1)S(1)} %bitcast.268, ...), custom_call_target="tpu_custom_call", output_to_operand_aliasing={{0}: (8, {}), {1}: (9, {}), {2}: (10, {})} | custom-call | flops 71999995904 | bytes 24000000 | tf_op jit(solution)/shard_map/attend_back/pallas_call | solution.py:371
  197.4 7.0 %collective-permute-done.32 = bf16[2,4,1,48,1920]{4,3,1,2,0:T(8,128)(2,1)S(1)} collective-permute-done((bf16[2,4,1,48,1920]{4,3,1,2,0:T(8,128)(2,1)S(1)}, bf16[2,4,1,48,1920]{4,3,1,2,0:T(8,128)(2,1)S(1)}, u32[]{:S(2)}, u32[]{:S(2)}) %collective-permute-start.32) | collective-permute-done | bytes 1474592 | tf_op jit(solution)/shard_map/ppermute | solution.py:859
  206.7 8.2 %attend_back.5 = (bf16[1024,768]{1,0:T(8,128)(2,1)S(1)}, bf16[1024,768]{1,0:T(8,128)(2,1)S(1)}, bf16[1024,768]{1,0:T(8,128)(2,1)S(1)}) custom-call(s32[1]{0:T(128)} %bitcast.64.core_ref, s32[2]{0:T(128)S(1)} %copy-done.24, bf16[1024,2304]{1,0:T(8,128)(2,1)S(1)} %bitcast.268, ...), custom_call_target="tpu_custom_call", output_to_operand_aliasing={{0}: (8, {}), {1}: (9, {}), {2}: (10, {})} | custom-call | flops 48000000000 | bytes 16000000 | tf_op jit(solution)/shard_map/attend_back/pallas_call | solution.py:371
  217.4 4.7 %grad_qkv.1 = (bf16[768,1152]{1,0:T(8,128)(2,1)S(1)}, bf16[768,1152]{1,0:T(8,128)(2,1)S(1)}) custom-call(s32[1]{0:T(128)} %bitcast.64.core_ref, bf16[1024,768]{1,0:T(8,128)(2,1)S(1)} %copy-done.34, bf16[1024,768]{1,0:T(8,128)(2,1)S(1)} %get-tuple-element.215.refs_1_.dq_ref, bf16[1024,768]{1,0:T(8,128)(2,1)S(1)} %get-tuple-element.209.refs_2_.dk_ref, ...), custom_call_target="tpu_custom_call" | custom-call | flops 14495514624 | bytes 39321600 | tf_op jit(solution)/shard_map/grad_qkv/pallas_call | solution.py:629
  228.7 6.9 %last.1 = (f32[512,768]{1,0:T(8,128)S(1)}, f32[2,512,768]{2,1,0:T(8,128)}, f32[16,768]{1,0:T(8,128)S(1)}) custom-call(s32[1]{0:T(128)} %bitcast.64.core_ref, bf16[1024,768]{1,0:T(8,128)(2,1)S(1)} %copy-done.1, f32[1024,768]{1,0:T(8,128)S(1)} %copy-done.28, bf16[1024,768]{1,0:T(8,128)(2,1)S(1)} %get-tuple-element.215.refs_1_.dq_ref, ...), custom_call_target="tpu_custom_call" | custom-call | flops 14495514624 | bytes 64000000 | tf_op jit(solution)/shard_map/last/pallas_call | solution.py:725
  238.0 2.7 collective-permute-done.36
  241.8 2.8 %collective-permute-done.39 = bf16[2,48,1920]{2,1,0:T(8,128)(2,1)S(1)} collective-permute-done((bf16[2,48,1920]{2,1,0:T(8,128)(2,1)S(1)}, bf16[2,48,1920]{2,1,0:T(8,128)(2,1)S(1)}, u32[]{:S(2)}, u32[]{:S(2)}) %collective-permute-start.39) | collective-permute-done | bytes 368672 | tf_op jit(solution)/shard_map/ppermute | solution.py:859
  245.5 3.8 %collective-permute-done.38 = bf16[4,1,48,1152]{3,2,1,0:T(8,128)(2,1)S(1)} collective-permute-done((bf16[4,1,48,1152]{3,2,1,0:T(8,128)(2,1)S(1)}, bf16[4,1,48,1152]{3,2,1,0:T(8,128)(2,1)S(1)}, u32[]{:S(2)}, u32[]{:S(2)}) %collective-permute-start.38) | collective-permute-done | bytes 442400 | tf_op jit(solution)/shard_map/ppermute | solution.py:859
  254.6 6.1 %collective-permute-done.43 = bf16[48,1920]{1,0:T(8,128)(2,1)S(1)} collective-permute-done((bf16[48,1920]{1,0:T(8,128)(2,1)S(1)}, bf16[48,1920]{1,0:T(8,128)(2,1)S(1)}, u32[]{:S(2)}, u32[]{:S(2)}) %collective-permute-start.43) | collective-permute-done | bytes 184352 | tf_op jit(solution)/shard_map/ppermute | solution.py:859
  263.3 3.0 %collective-permute-start.41 = (bf16[48,1152]{1,0:T(8,128)(2,1)S(1)}, bf16[48,1152]{1,0:T(8,128)(2,1)S(1)}, u32[]{:S(2)}, u32[]{:S(2)}) collective-permute-start(bf16[48,1152]{1,0:T(8,128)(2,1)S(1)} %fusion.18), channel_id=1, source_target_pairs={{0,8},{1,9},{2,10},{3,11},{4,12},{5,13},{6,14},{7,15},{8,0},{9,1},... | collective-permute-start | bytes 331784 | tf_op jit(solution)/shard_map/ppermute | solution.py:859
  (258 shorter events, 83.5 us)
Async XLA Ops:
  3.2 13.6 %collective-permute-start.2 = (bf16[48,1280]{1,0:T(8,128)(2,1)S(1)}, bf16[48,1280]{1,0:T(8,128)(2,1)S(1)}, u32[]{:S(2)}, u32[]{:S(2)}) collective-permute-start(bf16[48,1280]{1,0:T(8,128)(2,1)S(1)} %get-tuple-element.273), channel_id=1, source_target_pairs={{0,16},{1,17},{2,18},{3,19},{4,20},{5,21},{6,22},{7,23},{8,24},{9,... | collective-permute-start | bytes 368648 | tf_op jit(solution)/shard_map/ppermute | solution.py:859
  28.3 19.1 %collective-permute-start.7 = (bf16[2,4,48,1280]{3,2,1,0:T(8,128)(2,1)S(1)}, bf16[2,4,48,1280]{3,2,1,0:T(8,128)(2,1)}, u32[]{:S(2)}, u32[]{:S(2)}) collective-permute-start(bf16[2,4,48,1280]{3,2,1,0:T(8,128)(2,1)S(1)} %pad_maximum_fusion.2.refs_0_), channel_id=1, source_target_pairs={{0,4},{1,3},{2,6},{3,1},{4,0},{5,7},{6,2},{7,5},{8,12},{9,11},{10,... | collective-permute-start | bytes 2949128 | tf_op jit(solution)/shard_map/ppermute | solution.py:859
  29.9 17.4 %collective-permute-start.9 = (bf16[2,48,1920]{2,1,0:T(8,128)(2,1)S(1)}, bf16[2,48,1920]{2,1,0:T(8,128)(2,1)S(1)}, u32[]{:S(2)}, u32[]{:S(2)}) collective-permute-start(bf16[2,48,1920]{2,1,0:T(8,128)(2,1)S(1)} %pad_maximum_fusion.5), channel_id=1, source_target_pairs={{0,16},{1,17},{2,18},{3,19},{4,20},{5,21},{6,22},{7,23},{8,24},{9,... | collective-permute-start | bytes 1105928 | tf_op jit(solution)/shard_map/ppermute | solution.py:859
  31.8 17.7 %collective-permute-start.8 = (bf16[2,4,48,1280]{3,2,1,0:T(8,128)(2,1)S(1)}, bf16[2,4,48,1280]{3,2,1,0:T(8,128)(2,1)}, u32[]{:S(2)}, u32[]{:S(2)}) collective-permute-start(bf16[2,4,48,1280]{3,2,1,0:T(8,128)(2,1)S(1)} %pad_maximum_fusion.2.refs_0_), channel_id=1, source_target_pairs={{0,1},{1,0},{2,3},{3,2},{4,5},{5,4},{6,7},{7,6},{8,9},{9,8},{10,11... | collective-permute-start | bytes 2949128 | tf_op jit(solution)/shard_map/ppermute | solution.py:859
  47.5 30.6 %collective-permute-start.16 = (bf16[4,48,1920]{2,1,0:T(8,128)(2,1)S(1)}, bf16[4,48,1920]{2,1,0:T(8,128)(2,1)S(1)}, u32[]{:S(2)}, u32[]{:S(2)}) collective-permute-start(bf16[4,48,1920]{2,1,0:T(8,128)(2,1)S(1)} %constant_dynamic-update-slice_fusion), channel_id=1, source_target_pairs={{0,1},{1,0},{2,3},{3,2},{4,5},{5,4},{6,7},{7,6},{8,9},{9,8},{10,11... | collective-permute-start | bytes 2211848 | tf_op jit(solution)/shard_map/ppermute | solution.py:859
  48.0 17.8 %collective-permute-start.13 = (bf16[4,48,1920]{2,1,0:T(8,128)(2,1)S(1)}, bf16[4,48,1920]{2,1,0:T(8,128)(2,1)S(1)}, u32[]{:S(2)}, u32[]{:S(2)}) collective-permute-start(bf16[4,48,1920]{2,1,0:T(8,128)(2,1)S(1)} %constant_dynamic-update-slice_fusion), channel_id=1, source_target_pairs={{0,2},{1,5},{2,0},{3,7},{4,6},{5,1},{6,4},{7,3},{8,10},{9,13},{10,... | collective-permute-start | bytes 2211848 | tf_op jit(solution)/shard_map/ppermute | solution.py:859
  48.5 20.0 %collective-permute-start.11 = (bf16[2,192,384]{2,1,0:T(8,128)(2,1)}, bf16[2,192,384]{2,1,0:T(8,128)(2,1)S(1)}, u32[]{:S(2)}, u32[]{:S(2)}) collective-permute-start(bf16[2,192,384]{2,1,0:T(8,128)(2,1)} %pad_maximum_fusion.7), channel_id=1, source_target_pairs={{0,16},{1,17},{2,18},{3,19},{4,20},{5,21},{6,22},{7,23},{8,24},{9,... | collective-permute-start | bytes 884744 | tf_op jit(solution)/shard_map/ppermute | solution.py:859
  49.5 28.6 %collective-permute-start.12 = (bf16[4,48,1920]{2,1,0:T(8,128)(2,1)S(1)}, bf16[4,48,1920]{2,1,0:T(8,128)(2,1)S(1)}, u32[]{:S(2)}, u32[]{:S(2)}) collective-permute-start(bf16[4,48,1920]{2,1,0:T(8,128)(2,1)S(1)} %constant_dynamic-update-slice_fusion), channel_id=1, source_target_pairs={{0,4},{1,3},{2,6},{3,1},{4,0},{5,7},{6,2},{7,5},{8,12},{9,11},{10,... | collective-permute-start | bytes 2211848 | tf_op jit(solution)/shard_map/ppermute | solution.py:859
  65.8 14.2 %collective-permute-start.17 = (bf16[4,48,1920]{2,1,0:T(8,128)(2,1)S(1)}, bf16[4,48,1920]{2,1,0:T(8,128)(2,1)S(1)}, u32[]{:S(2)}, u32[]{:S(2)}) collective-permute-start(bf16[4,48,1920]{2,1,0:T(8,128)(2,1)S(1)} %collective-permute-done.13), channel_id=1, source_target_pairs={{0,1},{1,0},{2,3},{3,2},{4,5},{5,4},{6,7},{7,6},{8,9},{9,8},{10,11... | collective-permute-start | bytes 2211848 | tf_op jit(solution)/shard_map/ppermute | solution.py:859
  68.7 16.8 %collective-permute-start.15 = (bf16[512,768]{1,0:T(8,128)(2,1)S(1)}, bf16[512,768]{1,0:T(8,128)(2,1)S(1)}, u32[]{:S(2)}, u32[]{:S(2)}) collective-permute-start(bf16[512,768]{1,0:T(8,128)(2,1)S(1)} %get-tuple-element.261), channel_id=1, source_target_pairs={{0,1},{1,0},{2,3},{3,2},{4,5},{5,4},{6,7},{7,6},{8,9},{9,8},{10,11... | collective-permute-start | bytes 2359304 | tf_op jit(solution)/shard_map/ppermute | solution.py:859
  78.3 41.9 %collective-permute-start.23 = (bf16[4,192,384]{2,1,0:T(8,128)(2,1)S(1)}, bf16[4,192,384]{2,1,0:T(8,128)(2,1)S(1)}, u32[]{:S(2)}, u32[]{:S(2)}) collective-permute-start(bf16[4,192,384]{2,1,0:T(8,128)(2,1)S(1)} %constant_dynamic-update-slice_fusion.2), channel_id=1, source_target_pairs={{0,1},{1,0},{2,3},{3,2},{4,5},{5,4},{6,7},{7,6},{8,9},{9,8},{10,11... | collective-permute-start | bytes 1769480 | tf_op jit(solution)/shard_map/ppermute | solution.py:859
  78.7 30.0 %collective-permute-start.21 = (bf16[4,192,384]{2,1,0:T(8,128)(2,1)S(1)}, bf16[4,192,384]{2,1,0:T(8,128)(2,1)S(1)}, u32[]{:S(2)}, u32[]{:S(2)}) collective-permute-start(bf16[4,192,384]{2,1,0:T(8,128)(2,1)S(1)} %constant_dynamic-update-slice_fusion.2), channel_id=1, source_target_pairs={{0,4},{1,3},{2,6},{3,1},{4,0},{5,7},{6,2},{7,5},{8,12},{9,11},{10,... | collective-permute-start | bytes 1769480 | tf_op jit(solution)/shard_map/ppermute | solution.py:859
  84.8 22.2 %collective-permute-start.20 = (bf16[4,192,384]{2,1,0:T(8,128)(2,1)S(1)}, bf16[4,192,384]{2,1,0:T(8,128)(2,1)S(1)}, u32[]{:S(2)}, u32[]{:S(2)}) collective-permute-start(bf16[4,192,384]{2,1,0:T(8,128)(2,1)S(1)} %constant_dynamic-update-slice_fusion.2), channel_id=1, source_target_pairs={{0,2},{1,5},{2,0},{3,7},{4,6},{5,1},{6,4},{7,3},{8,10},{9,13},{10,... | collective-permute-start | bytes 1769480 | tf_op jit(solution)/shard_map/ppermute | solution.py:859
  107.0 13.3 %collective-permute-start.24 = (bf16[4,192,384]{2,1,0:T(8,128)(2,1)S(1)}, bf16[4,192,384]{2,1,0:T(8,128)(2,1)S(1)}, u32[]{:S(2)}, u32[]{:S(2)}) collective-permute-start(bf16[4,192,384]{2,1,0:T(8,128)(2,1)S(1)} %collective-permute-done.20), channel_id=1, source_target_pairs={{0,1},{1,0},{2,3},{3,2},{4,5},{5,4},{6,7},{7,6},{8,9},{9,8},{10,11... | collective-permute-start | bytes 1769480 | tf_op jit(solution)/shard_map/ppermute | solution.py:859
  120.2 31.5 %collective-permute-start.27 = (bf16[3072,384]{1,0:T(8,128)(2,1)}, bf16[3072,384]{1,0:T(8,128)(2,1)S(1)}, u32[]{:S(2)}, u32[]{:S(2)}) collective-permute-start(bf16[3072,384]{1,0:T(8,128)(2,1)} %get-tuple-element.177), channel_id=1, source_target_pairs={{0,1},{1,0},{2,3},{3,2},{4,5},{5,4},{6,7},{7,6},{8,9},{9,8},{10,11... | collective-permute-start | bytes 7077896 | tf_op jit(solution)/shard_map/ppermute | solution.py:859
  152.2 17.6 %collective-permute-start.28 = (bf16[2,4,1,192,384]{4,3,1,2,0:T(8,128)(2,1)S(1)}, bf16[2,4,1,192,384]{4,3,1,2,0:T(8,128)(2,1)S(1)}, u32[]{:S(2)}, u32[]{:S(2)}) collective-permute-start(bf16[2,4,1,192,384]{4,3,1,2,0:T(8,128)(2,1)S(1)} %pad_maximum_fusion.1), channel_id=1, source_target_pairs={{0,2},{1,5},{2,0},{3,7},{4,6},{5,1},{6,4},{7,3},{8,10},{9,13},{10,... | collective-permute-start | bytes 3538952 | tf_op jit(solution)/shard_map/ppermute | solution.py:859
  162.0 20.8 %collective-permute-start.31 = (bf16[768,1920]{1,0:T(8,128)(2,1)}, bf16[768,1920]{1,0:T(8,128)(2,1)}, u32[]{:S(2)}, u32[]{:S(2)}) collective-permute-start(bf16[768,1920]{1,0:T(8,128)(2,1)} %grad_up.2), channel_id=1, source_target_pairs={{0,1},{1,0},{2,3},{3,2},{4,5},{5,4},{6,7},{7,6},{8,9},{9,8},{10,11... | collective-permute-start | bytes 8847368 | tf_op jit(solution)/shard_map/ppermute | solution.py:859
  182.7 14.7 %collective-permute-start.30 = (bf16[2,192,384]{2,1,0:T(8,128)(2,1)S(1)}, bf16[2,192,384]{2,1,0:T(8,128)(2,1)S(1)}, u32[]{:S(2)}, u32[]{:S(2)}) collective-permute-start(bf16[2,192,384]{2,1,0:T(8,128)(2,1)S(1)} %pad_maximum_fusion.8), channel_id=1, source_target_pairs={{0,16},{1,17},{2,18},{3,19},{4,20},{5,21},{6,22},{7,23},{8,24},{9,... | collective-permute-start | bytes 884744 | tf_op jit(solution)/shard_map/ppermute | solution.py:859
  185.0 19.4 %collective-permute-start.32 = (bf16[2,4,1,48,1920]{4,3,1,2,0:T(8,128)(2,1)S(1)}, bf16[2,4,1,48,1920]{4,3,1,2,0:T(8,128)(2,1)S(1)}, u32[]{:S(2)}, u32[]{:S(2)}) collective-permute-start(bf16[2,4,1,48,1920]{4,3,1,2,0:T(8,128)(2,1)S(1)} %pad_maximum_fusion), channel_id=1, source_target_pairs={{0,2},{1,5},{2,0},{3,7},{4,6},{5,1},{6,4},{7,3},{8,10},{9,13},{10,... | collective-permute-start | bytes 4423688 | tf_op jit(solution)/shard_map/ppermute | solution.py:859
  222.2 13.4 %collective-permute-start.45 = (bf16[192,384]{1,0:T(8,128)(2,1)S(1)}, bf16[192,384]{1,0:T(8,128)(2,1)S(1)}, u32[]{:S(2)}, u32[]{:S(2)}) collective-permute-start(bf16[192,384]{1,0:T(8,128)(2,1)S(1)} %fusion.15), channel_id=1, source_target_pairs={{0,8},{1,9},{2,10},{3,11},{4,12},{5,13},{6,14},{7,15},{8,0},{9,1},... | collective-permute-start | bytes 442376 | tf_op jit(solution)/shard_map/ppermute | solution.py:859
  224.9 19.7 %collective-permute-start.39 = (bf16[2,48,1920]{2,1,0:T(8,128)(2,1)S(1)}, bf16[2,48,1920]{2,1,0:T(8,128)(2,1)S(1)}, u32[]{:S(2)}, u32[]{:S(2)}) collective-permute-start(bf16[2,48,1920]{2,1,0:T(8,128)(2,1)S(1)} %pad_maximum_fusion.6), channel_id=1, source_target_pairs={{0,16},{1,17},{2,18},{3,19},{4,20},{5,21},{6,22},{7,23},{8,24},{9,... | collective-permute-start | bytes 1105928 | tf_op jit(solution)/shard_map/ppermute | solution.py:859
  235.7 30.8 %collective-permute-start.46 = (f32[192,384]{1,0:T(8,128)S(1)}, f32[192,384]{1,0:T(8,128)S(1)}, u32[]{:S(2)}, u32[]{:S(2)}) collective-permute-start(f32[192,384]{1,0:T(8,128)S(1)} %fusion.16.refs_0_), channel_id=1, source_target_pairs={{0,1},{1,0},{2,3},{3,2},{4,5},{5,4},{6,7},{7,6},{8,9},{9,8},{10,11... | collective-permute-start | bytes 884744 | tf_op jit(solution)/shard_map/ppermute | solution.py:859
  245.4 15.5 %collective-permute-start.37 = (f32[512,768]{1,0:T(8,128)S(1)}, f32[512,768]{1,0:T(8,128)S(1)}, u32[]{:S(2)}, u32[]{:S(2)}) collective-permute-start(f32[512,768]{1,0:T(8,128)S(1)} %get-tuple-element.221), channel_id=1, source_target_pairs={{0,1},{1,0},{2,3},{3,2},{4,5},{5,4},{6,7},{7,6},{8,9},{9,8},{10,11... | collective-permute-start | bytes 4718600 | tf_op jit(solution)/shard_map/ppermute | solution.py:859
  249.8 13.3 %collective-permute-start.50 = (f32[16,768]{1,0:T(8,128)S(1)}, f32[16,768]{1,0:T(8,128)S(1)}, u32[]{:S(2)}, u32[]{:S(2)}) collective-permute-start(f32[16,768]{1,0:T(8,128)S(1)} %add.658), channel_id=1, source_target_pairs={{0,8},{1,9},{2,10},{3,11},{4,12},{5,13},{6,14},{7,15},{8,0},{9,1},... | collective-permute-start | bytes 147464 | tf_op jit(solution)/shard_map/ppermute | solution.py:859
  (78 other events, 535.3 us)

commit v4 on v2

--- a/solution.py
+++ b/solution.py
@@ -476,19 +476,16 @@
             wide,
             low,
         ],
-        compiler_params=params(40),
+        compiler_params=params(48),
         cost_estimate=cost(6e9, 30e6, rows * FF),
     )(core, lengths, seats, x, a, og, vec, *group.arrays)
 
 
-def down_kernel(up_group, down_group, core_ref, len_ref, seat_ref, mid_ref, e_ref, slope_ref, dy_ref, vec_ref, *refs):
+def down_kernel(up_group, down_group, core_ref, seat_ref, mid_ref, slope_ref, dy_ref, vec_ref, *refs):
     count = len(up_group.arrays)
     up_refs, down_refs = refs[:count], refs[count : count + len(down_group.arrays)]
-    (
-        theirs_ref, mine_ref, dz_ref, dmb_ref, dm_ref, da_ref, acc_ref, wo_ref, wu_ref, wd_ref, sems,
-    ) = refs[-11:]
-    block = da_ref.shape[0]
-    step, steps = pl.program_id(0), pl.num_programs(0)
+    dz_ref, dmb_ref, dm_ref, da_ref, acc_ref, wo_ref, wu_ref, wd_ref, sems = refs[-9:]
+    step = pl.program_id(0)
 
     @pl.when(step == 0)
     def _():
@@ -499,18 +496,6 @@
         wait_all(wd_ref, sems.at[2])
 
     mid = mid_ref[...]
-    down = vec_ref[7:8, :] + mid + mm(e_ref[...], wd_ref[...])
-    pos = row_block(core_ref[0], step, steps) * block + lax.broadcasted_iota(jnp.int32, (block, 1), 0)
-    down = jnp.where(pos < len_ref[core_ref[0]], down, 0.0).astype(BF16)
-
-    @pl.when(step < steps // 2)
-    def _():
-        theirs_ref[...] = down
-
-    @pl.when(step >= steps // 2)
-    def _():
-        mine_ref[0] = down
-
     @pl.when(step == 0)
     def _():
         wait_all(wu_ref, sems.at[1])
@@ -544,25 +529,21 @@
     da_ref[...] = mm(dm_low, wo_ref[...], NT).astype(BF16)
 
 
-def down_call(core, lengths, seats, mid, e, slope, dy, vec, up_group, down_group, block=256):
+def down_call(core, seats, mid, slope, dy, vec, up_group, down_group, block=256):
     rows = mid.shape[0]
-    steps = rows // block
-    half = steps // 2
     row_spec, wide_spec = [
-        pl.BlockSpec((block, width), lambda i, c, *s: (row_block(c[0], i, steps), 0)) for width in (D, FF)
+        pl.BlockSpec((block, width), lambda i, *s: (i, 0)) for width in (D, FF)
     ]
     return pl.pallas_call(
         functools.partial(down_kernel, up_group, down_group),
         name="down",
         grid_spec=pltpu.PrefetchScalarGridSpec(
-            num_scalar_prefetch=3,
-            grid=(steps,),
-            in_specs=[row_spec, wide_spec, wide_spec, row_spec, whole_spec(vec.shape)]
+            num_scalar_prefetch=2,
+            grid=(rows // block,),
+            in_specs=[row_spec, wide_spec, row_spec, whole_spec(vec.shape)]
             + up_group.specs()
             + down_group.specs(),
             out_specs=[
-                pl.BlockSpec((block, D), lambda i, *s: (jnp.minimum(i, half - 1), 0)),
-                pl.BlockSpec((1, block, D), lambda i, c, *s: (c[0], jnp.maximum(i - half, 0), 0)),
                 wide_spec, row_spec, row_spec, row_spec,
                 pl.BlockSpec((16, D), lambda i, *s: (0, 0)),
             ],
@@ -574,17 +555,67 @@
             ],
         ),
         out_shape=[
-            jax.ShapeDtypeStruct((rows // 2, D), BF16),
-            jax.ShapeDtypeStruct((2, rows // 2, D), BF16),
             jax.ShapeDtypeStruct((rows, FF), BF16),
             jax.ShapeDtypeStruct((rows, D), BF16),
             jax.ShapeDtypeStruct((rows, D), F32),
             jax.ShapeDtypeStruct((rows, D), BF16),
             jax.ShapeDtypeStruct((16, D), F32),
         ],
-        compiler_params=params(40),
-        cost_estimate=cost(1.6e10, 35e6),
-    )(core, lengths, seats, mid, e, slope, dy, vec, *up_group.arrays, *down_group.arrays)
+        compiler_params=params(48),
+        cost_estimate=cost(1.1e10, 28e6),
+    )(core, seats, mid, slope, dy, vec, *up_group.arrays, *down_group.arrays)
+
+
+def out_kernel(group, core_ref, len_ref, seat_ref, mid_ref, e_ref, vec_ref, *refs):
+    refs, (theirs_ref, mine_ref, wd_ref, sems) = refs[:-4], refs[-4:]
+    block = mid_ref.shape[0]
+    step, steps = pl.program_id(0), pl.num_programs(0)
+
+    @pl.when(step == 0)
+    def _():
+        group.start(refs, core_ref, seat_ref, 0, D // 2, wd_ref, sems.at[0])
+        wait_all(wd_ref, sems.at[0])
+
+    down = vec_ref[7:8, :] + mid_ref[...] + mm(e_ref[...], wd_ref[...])
+    pos = row_block(core_ref[0], step, steps) * block + lax.broadcasted_iota(jnp.int32, (block, 1), 0)
+    down = jnp.where(pos < len_ref[core_ref[0]], down, 0.0).astype(BF16)
+
+    @pl.when(step < steps // 2)
+    def _():
+        theirs_ref[...] = down
+
+    @pl.when(step >= steps // 2)
+    def _():
+        mine_ref[0] = down
+
+
+def out_call(core, lengths, seats, mid, e, vec, group, block=256):
+    rows = mid.shape[0]
+    steps = rows // block
+    half = steps // 2
+    row_spec, wide_spec = [
+        pl.BlockSpec((block, width), lambda i, c, *s: (row_block(c[0], i, steps), 0)) for width in (D, FF)
+    ]
+    return pl.pallas_call(
+        functools.partial(out_kernel, group),
+        name="out",
+        grid_spec=pltpu.PrefetchScalarGridSpec(
+            num_scalar_prefetch=3,
+            grid=(steps,),
+            in_specs=[row_spec, wide_spec, whole_spec(vec.shape)] + group.specs(),
+            out_specs=[
+                pl.BlockSpec((block, D), lambda i, *s: (jnp.minimum(i, half - 1), 0)),
+                pl.BlockSpec((1, block, D), lambda i, c, *s: (c[0], jnp.maximum(i - half, 0), 0)),
+            ],
+            scratch_shapes=[pltpu.VMEM((FF, D), BF16), pltpu.SemaphoreType.DMA((1,))],
+        ),
+        out_shape=[
+            jax.ShapeDtypeStruct((rows // 2, D), BF16),
+            jax.ShapeDtypeStruct((2, rows // 2, D), BF16),
+        ],
+        compiler_params=params(20),
+        cost_estimate=cost(4.9e9, 16e6),
+    )(core, lengths, seats, mid, e, vec, *group.arrays)
 
 
 def pick(values, half, mode):
@@ -1013,9 +1044,7 @@
         grid.plane_parts(d_col, d_firsts, d_seconds, d_passed),
         grid.plane_parts(d_col_swap, *early, [[grid.swap(part) for part in parts] for parts in d_passed]),
     )
-    out_theirs, out_mine, dz, dmb, dm, da, acc_mid = down_call(
-        core_arr, lengths, seats, mid, e, slope, dy, vec, u_group, d_group
-    )
+    dz, dmb, dm, da, acc_mid = down_call(core_arr, seats, mid, slope, dy, vec, u_group, d_group)
 
     d_pair = after(grid.swap(d_other), dz)
     u_own, u_other = weight_grad_call(
@@ -1033,7 +1062,6 @@
     d_parts, d_got = grid.scatter_bit(grid.order_z(d_sum), *back)
     u_kept = grid.scatter_first(u_own, u_pair, *back)
     dq, dk, dv = back
-    block_out = both_slots(out_mine, after(grid.swap(after(out_theirs, back[0])), dq))
     q_own, q_other = weight_grad_call(
         core_arr, [(h1, [after(dq, d_got, *u_kept[1]), dk, dv])], 384, "grad_qkv", "turns"
     )
@@ -1057,7 +1085,9 @@
     u_mine = grid.scatter_z([after(part, *q_here) for part in u_parts])
     u_other_mine = grid.swap(u_mine)
     in_grad = both_slots(in_mine, after(in_got, *q_here))
-    q_parts, q_got = grid.scatter_bit(grid.order_z(q_sum), in_grad)
+    out_theirs, out_mine = out_call(core_arr, lengths, seats, after(mid, in_grad, *q_here), e, vec, d_group)
+    q_parts, q_got = grid.scatter_bit(grid.order_z(q_sum), out_theirs)
+    block_out = both_slots(out_mine, grid.swap(out_theirs))
     q_gots = [(q_got,)]
     while len(q_parts) > 1:
         q_parts, q_got = grid.scatter_bit(q_parts)

time: 273 us -> 272 us (level)
  local copies, waits for them, and re-layouts: 18.2 us -> 14.1 us
    pallas_call x1, Pallas kernels: 30.5 us -> 22.1 us  [down_call(): pl.pallas_call(functools.partial(down_kernel, up_group, down_group), name...]
    pallas_call x0 -> x1, Pallas kernels: none -> 8.03 us  [out_call(): pl.pallas_call(functools.partial(out_kernel, group), name='out', grid_spe...]
    unnamed x102 -> x130, local copies, waits for them, and re-layouts: 15.7 us -> 9.33 us
  transfers between devices with their start and end apart: 52 -> 52, of which waited for: 20 -> 21; matrix products, arithmetic and copies ran while one was open for 4% -> 5% of each run, Pallas kernels for 49% -> 50%
where the time goes in v4:
time: 272 us; the launch traced here: 269 us
  Pallas kernels  134 us (49%)
  waiting for transfers between devices  65.2 us (24%)
  starting transfers between devices  40.6 us (15%)
  local copies, waits for them, and re-layouts  14.1 us (5%)
  other arithmetic  12 us (4%)
    ppermute x52, waiting for transfers between devices, permute(): return lax.ppermute(value, ('dp', 'seq'), pairs)  65.2 us
    ppermute x52, starting transfers between devices, permute(): return lax.ppermute(value, ('dp', 'seq'), pairs)  40.6 us
    pallas_call x3, Pallas kernels, weight_grad_call(): pl.pallas_call(functools.partial(weight_grad_kernel, len(lefts), [len(gro...  26.3 us
    pallas_call x2, Pallas kernels, attend_back_call(): pl.pallas_call(attend_back_kernel, name='attend_back', grid_spec=pltpu.Pr...  23.6 us
    pallas_call x1, Pallas kernels, down_call(): pl.pallas_call(functools.partial(down_kernel, up_group, down_group), name...  22.1 us
    pallas_call x1, Pallas kernels, up_call(): pl.pallas_call(functools.partial(up_kernel, group), name='up', grid_spec=...  19.7 us
    pallas_call x2, Pallas kernels, attend_call(): pl.pallas_call(functools.partial(attend_kernel, first), name='attend', gr...  13.7 us
    pallas_call x1, Pallas kernels, qkv_call(): pl.pallas_call(functools.partial(qkv_kernel, group), name='qkv', grid_spe...  9.49 us
  transfers between devices with their start and end apart: 52, of which 21 were waited for; matrix products, arithmetic and copies ran while one was open for 5% of the time, Pallas kernels for 50%

profile of v4, /device:TPU:0, one launch (start us, length us, event | category | flops | bytes accessed | tf_op | source)
XLA Modules:
  0.0 268.6 jit_solution(1891369958343411114)
XLA Ops:
  3.2 4.1 %collective-permute-start.2 = (bf16[48,1280]{1,0:T(8,128)(2,1)S(1)}, bf16[48,1280]{1,0:T(8,128)(2,1)S(1)}, u32[]{:S(2)}, u32[]{:S(2)}) collective-permute-start(bf16[48,1280]{1,0:T(8,128)(2,1)S(1)} %get-tuple-element.267), channel_id=1, source_target_pairs={{0,16},{1,17},{2,18},{3,19},{4,20},{5,21},{6,22},{7,23},{8,24},{9,... | collective-permute-start | bytes 368648 | tf_op jit(solution)/shard_map/ppermute | solution.py:858
  13.0 3.8 %collective-permute-done.2 = bf16[48,1280]{1,0:T(8,128)(2,1)S(1)} collective-permute-done((bf16[48,1280]{1,0:T(8,128)(2,1)S(1)}, bf16[48,1280]{1,0:T(8,128)(2,1)S(1)}, u32[]{:S(2)}, u32[]{:S(2)}) %collective-permute-start.2) | collective-permute-done | bytes 122912 | tf_op jit(solution)/shard_map/ppermute | solution.py:858
  25.3 2.9 %collective-permute-done.4 = bf16[4,48,1280]{2,1,0:T(8,128)(2,1)S(1)} collective-permute-done((bf16[4,48,1280]{2,1,0:T(8,128)(2,1)S(1)}, bf16[4,48,1280]{2,1,0:T(8,128)(2,1)S(1)}, u32[]{:S(2)}, u32[]{:S(2)}) %collective-permute-start.4) | collective-permute-done | bytes 491552 | tf_op jit(solution)/shard_map/ppermute | solution.py:858
  31.9 15.5 %collective-permute-done.9 = bf16[2,48,1920]{2,1,0:T(8,128)(2,1)S(1)} collective-permute-done((bf16[2,48,1920]{2,1,0:T(8,128)(2,1)S(1)}, bf16[2,48,1920]{2,1,0:T(8,128)(2,1)S(1)}, u32[]{:S(2)}, u32[]{:S(2)}) %collective-permute-start.9) | collective-permute-done | bytes 368672 | tf_op jit(solution)/shard_map/ppermute | solution.py:858
  51.1 9.5 %qkv.1 = (bf16[1024,768]{1,0:T(8,128)(2,1)S(1)}, bf16[1024,2304]{1,0:T(8,128)(2,1)S(1)}, f32[16,768]{1,0:T(8,128)S(1)}, bf16[2304,768]{1,0:T(8,128)(2,1)S(1)}) custom-call(s32[1]{0:T(128)} %bitcast.64.core_ref, s32[32]{0:T(128)S(1)} %convert_element_type.410.seat_ref, bf16[1024,768]{1,0:T(8,128)(2,1)S(1)} %maximum_select_fusion.x_ref, ...), custom_call_target="tpu_custom_call" | custom-call | flops 14495514624 | bytes 40000000 | tf_op jit(solution)/shard_map/qkv/pallas_call | solution.py:161
  61.8 4.0 %collective-permute-done.13 = bf16[4,48,1920]{2,1,0:T(8,128)(2,1)S(1)} collective-permute-done((bf16[4,48,1920]{2,1,0:T(8,128)(2,1)S(1)}, bf16[4,48,1920]{2,1,0:T(8,128)(2,1)S(1)}, u32[]{:S(2)}, u32[]{:S(2)}) %collective-permute-start.13) | collective-permute-done | bytes 737312 | tf_op jit(solution)/shard_map/ppermute | solution.py:858
  65.8 2.7 collective-permute-start.14
  69.2 8.9 %attend.2 = (bf16[1024,768]{1,0:T(8,128)(2,1)S(1)}, f32[6,8,1024]{2,1,0:T(8,128)S(1)}) custom-call(s32[1]{0:T(128)} %bitcast.64.core_ref, s32[2]{0:T(128)S(1)} %copy-done.36, bf16[1024,2304]{1,0:T(8,128)(2,1)S(1)} %get-tuple-element.150.qkv_ref.q_ref.k_ref.v_ref), custom_call_target="tpu_custom_call" | custom-call | flops 48000000000 | bytes 19200000 | tf_op jit(solution)/shard_map/attend/pallas_call | solution.py:274
  80.0 4.8 %attend.3 = (bf16[1024,768]{1,0:T(8,128)(2,1)S(1)}, f32[6,8,1024]{2,1,0:T(8,128)S(1)}) custom-call(s32[1]{0:T(128)} %bitcast.64.core_ref, s32[2]{0:T(128)S(1)} %copy-done.36, bf16[1024,2304]{1,0:T(8,128)(2,1)S(1)} %get-tuple-element.150.qkv_ref.q_ref.k_ref.v_ref, ...), custom_call_target="tpu_custom_call", output_to_operand_aliasing={{0}: (3, {}), {1}: (4, {})} | custom-call | flops 24000000000 | bytes 9600000 | tf_op jit(solution)/shard_map/attend/pallas_call | solution.py:274
  87.4 19.7 %up.1 = (f32[1024,768]{1,0:T(8,128)}, bf16[1024,768]{1,0:T(8,128)(2,1)}, bf16[1024,3072]{1,0:T(8,128)(2,1)}, bf16[1024,3072]{1,0:T(8,128)(2,1)}, bf16[1024,768]{1,0:T(8,128)(2,1)}) custom-call(s32[1]{0:T(128)} %bitcast.64.core_ref, s32[2]{0:T(128)S(1)} %copy-done.36, s32[32]{0:T(128)S(1)} %convert_element_type.409.seat_ref, bf16[1024,768]{1,0:T(8,128)(2,1)} %copy-done, ...), custom_call_target="tpu_custom_call" | custom-call | flops 24000000000 | bytes 120000000 | tf_op jit(solution)/shard_map/up/pallas_call | solution.py:458
  110.4 9.5 %grad_down.1 = (bf16[3072,384]{1,0:T(8,128)(2,1)S(1)}, bf16[3072,384]{1,0:T(8,128)(2,1)}) custom-call(s32[1]{0:T(128)} %bitcast.64.core_ref, bf16[1024,3072]{1,0:T(8,128)(2,1)} %get-tuple-element.164.refs_0_.e_ref, bf16[1024,768]{1,0:T(8,128)(2,1)S(1)} %copy-done.46), custom_call_target="tpu_custom_call" | custom-call | flops 19327352832 | bytes 50331648 | tf_op jit(solution)/shard_map/grad_down/pallas_call | solution.py:660
  121.9 22.1 %down.1 = (bf16[1024,3072]{1,0:T(8,128)(2,1)}, bf16[1024,768]{1,0:T(8,128)(2,1)}, f32[1024,768]{1,0:T(8,128)}, bf16[1024,768]{1,0:T(8,128)(2,1)}, f32[16,768]{1,0:T(8,128)S(1)}) custom-call(s32[1]{0:T(128)} %bitcast.64.core_ref, s32[32]{0:T(128)S(1)} %convert_element_type.409.seat_ref, f32[1024,768]{1,0:T(8,128)} %get-tuple-element.216.mid_ref, ...), custom_call_target="tpu_custom_call" | custom-call | flops 44000002048 | bytes 112000000 | tf_op jit(solution)/shard_map/down/pallas_call | solution.py:537
  147.3 11.9 %grad_up.1 = (bf16[768,1920]{1,0:T(8,128)(2,1)}, bf16[768,1920]{1,0:T(8,128)(2,1)}) custom-call(s32[1]{0:T(128)} %bitcast.64.core_ref, bf16[1024,768]{1,0:T(8,128)(2,1)S(1)} %copy-done.49, bf16[1024,768]{1,0:T(8,128)(2,1)S(1)} %copy-done.47, bf16[1024,768]{1,0:T(8,128)(2,1)S(1)} %copy-done.50, bf16[1024,3072]{1,0:T(8,128)(2,1)} %get-tuple-element.177.refs_3_), custom_call_target="tpu_custom_call" | custom-call | flops 24159191040 | bytes 61341696 | tf_op jit(solution)/shard_map/grad_up/pallas_call | solution.py:660
  163.3 8.2 %attend_back.2 = (bf16[1024,768]{1,0:T(8,128)(2,1)S(1)}, bf16[1024,768]{1,0:T(8,128)(2,1)S(1)}, bf16[1024,768]{1,0:T(8,128)(2,1)S(1)}) custom-call(s32[1]{0:T(128)} %bitcast.64.core_ref, s32[2]{0:T(128)S(1)} %copy-done.36, bf16[1024,2304]{1,0:T(8,128)(2,1)S(1)} %bitcast.276, bf16[1024,2304]{1,0:T(8,128)(2,1)S(1)} %bitcast.276, ...), custom_call_target="tpu_custom_call" | custom-call | flops 48000000000 | bytes 16000000 | tf_op jit(solution)/shard_map/attend_back/pallas_call | solution.py:371
  175.8 15.4 %attend_back.3 = (bf16[1024,768]{1,0:T(8,128)(2,1)S(1)}, bf16[1024,768]{1,0:T(8,128)(2,1)S(1)}, bf16[1024,768]{1,0:T(8,128)(2,1)S(1)}) custom-call(s32[1]{0:T(128)} %bitcast.64.core_ref, s32[2]{0:T(128)S(1)} %copy-done.36, bf16[1024,2304]{1,0:T(8,128)(2,1)S(1)} %bitcast.276, ...), custom_call_target="tpu_custom_call", output_to_operand_aliasing={{0}: (8, {}), {1}: (9, {}), {2}: (10, {})} | custom-call | flops 96000000000 | bytes 32000000 | tf_op jit(solution)/shard_map/attend_back/pallas_call | solution.py:371
  191.2 3.3 %collective-permute-done.32 = bf16[2,4,1,48,1920]{4,3,1,2,0:T(8,128)(2,1)S(1)} collective-permute-done((bf16[2,4,1,48,1920]{4,3,1,2,0:T(8,128)(2,1)S(1)}, bf16[2,4,1,48,1920]{4,3,1,2,0:T(8,128)(2,1)S(1)}, u32[]{:S(2)}, u32[]{:S(2)}) %collective-permute-start.32) | collective-permute-done | bytes 1474592 | tf_op jit(solution)/shard_map/ppermute | solution.py:858
  195.7 4.9 %grad_qkv.1 = (bf16[768,1152]{1,0:T(8,128)(2,1)S(1)}, bf16[768,1152]{1,0:T(8,128)(2,1)S(1)}) custom-call(s32[1]{0:T(128)} %bitcast.64.core_ref, bf16[1024,768]{1,0:T(8,128)(2,1)S(1)} %copy-done.45, bf16[1024,768]{1,0:T(8,128)(2,1)S(1)} %get-tuple-element.206.refs_1_.dq_ref, bf16[1024,768]{1,0:T(8,128)(2,1)S(1)} %get-tuple-element.197.refs_2_.dk_ref, ...), custom_call_target="tpu_custom_call" | custom-call | flops 14495514624 | bytes 39321600 | tf_op jit(solution)/shard_map/grad_qkv/pallas_call | solution.py:660
  200.6 5.7 %collective-permute-done.33 = bf16[4,1,48,1920]{3,2,1,0:T(8,128)(2,1)S(1)} collective-permute-done((bf16[4,1,48,1920]{3,2,1,0:T(8,128)(2,1)S(1)}, bf16[4,1,48,1920]{3,2,1,0:T(8,128)(2,1)S(1)}, u32[]{:S(2)}, u32[]{:S(2)}) %collective-permute-start.33) | collective-permute-done | bytes 737312 | tf_op jit(solution)/shard_map/ppermute | solution.py:858
  211.5 7.1 %last.1 = (f32[512,768]{1,0:T(8,128)S(1)}, f32[2,512,768]{2,1,0:T(8,128)}, f32[16,768]{1,0:T(8,128)S(1)}) custom-call(s32[1]{0:T(128)} %bitcast.64.core_ref, bf16[1024,768]{1,0:T(8,128)(2,1)S(1)} %copy-done.1, f32[1024,768]{1,0:T(8,128)S(1)} %copy-done.42, bf16[1024,768]{1,0:T(8,128)(2,1)S(1)} %get-tuple-element.206.refs_1_.dq_ref, ...), custom_call_target="tpu_custom_call" | custom-call | flops 14495514624 | bytes 64000000 | tf_op jit(solution)/shard_map/last/pallas_call | solution.py:724
  224.5 2.8 %collective-permute-done.38 = bf16[2,48,1920]{2,1,0:T(8,128)(2,1)S(1)} collective-permute-done((bf16[2,48,1920]{2,1,0:T(8,128)(2,1)S(1)}, bf16[2,48,1920]{2,1,0:T(8,128)(2,1)S(1)}, u32[]{:S(2)}, u32[]{:S(2)}) %collective-permute-start.38) | collective-permute-done | bytes 368672 | tf_op jit(solution)/shard_map/ppermute | solution.py:858
  228.3 3.8 %collective-permute-done.37 = bf16[4,1,48,1152]{3,2,1,0:T(8,128)(2,1)S(1)} collective-permute-done((bf16[4,1,48,1152]{3,2,1,0:T(8,128)(2,1)S(1)}, bf16[4,1,48,1152]{3,2,1,0:T(8,128)(2,1)S(1)}, u32[]{:S(2)}, u32[]{:S(2)}) %collective-permute-start.37) | collective-permute-done | bytes 442400 | tf_op jit(solution)/shard_map/ppermute | solution.py:858
  235.0 5.4 %collective-permute-done.43 = bf16[48,1920]{1,0:T(8,128)(2,1)S(1)} collective-permute-done((bf16[48,1920]{1,0:T(8,128)(2,1)S(1)}, bf16[48,1920]{1,0:T(8,128)(2,1)S(1)}, u32[]{:S(2)}, u32[]{:S(2)}) %collective-permute-start.43) | collective-permute-done | bytes 184352 | tf_op jit(solution)/shard_map/ppermute | solution.py:858
  242.9 8.0 %out.1 = (bf16[512,768]{1,0:T(8,128)(2,1)S(1)}, bf16[2,512,768]{2,1,0:T(8,128)(2,1)}) custom-call(s32[1]{0:T(128)} %bitcast.64.core_ref, s32[2]{0:T(128)S(1)} %copy-done.36, s32[32]{0:T(128)S(1)} %copy-done.38, f32[1024,768]{1,0:T(8,128)S(1)} %copy-done.43, bf16[1024,3072]{1,0:T(8,128)(2,1)S(1)} %bitcast.278, f32[16,768]{1,0:T(8,128)S(1)} %get-tuple-element.153.vec_ref, ...), custom_call_target="tpu_custom_call" | custom-call | flops 19599998976 | bytes 64000000 | tf_op jit(solution)/shard_map/out/pallas_call | solution.py:599
  253.2 4.4 %collective-permute-done.50 = f32[16,768]{1,0:T(8,128)S(1)} collective-permute-done((f32[16,768]{1,0:T(8,128)S(1)}, f32[16,768]{1,0:T(8,128)S(1)}, u32[]{:S(2)}, u32[]{:S(2)}) %collective-permute-start.50) | collective-permute-done | bytes 49184 | tf_op jit(solution)/shard_map/ppermute | solution.py:858
  (286 shorter events, 78.1 us)
Async XLA Ops:
  3.2 13.6 %collective-permute-start.2 = (bf16[48,1280]{1,0:T(8,128)(2,1)S(1)}, bf16[48,1280]{1,0:T(8,128)(2,1)S(1)}, u32[]{:S(2)}, u32[]{:S(2)}) collective-permute-start(bf16[48,1280]{1,0:T(8,128)(2,1)S(1)} %get-tuple-element.267), channel_id=1, source_target_pairs={{0,16},{1,17},{2,18},{3,19},{4,20},{5,21},{6,22},{7,23},{8,24},{9,... | collective-permute-start | bytes 368648 | tf_op jit(solution)/shard_map/ppermute | solution.py:858
  28.3 19.1 %collective-permute-start.7 = (bf16[2,4,48,1280]{3,2,1,0:T(8,128)(2,1)S(1)}, bf16[2,4,48,1280]{3,2,1,0:T(8,128)(2,1)}, u32[]{:S(2)}, u32[]{:S(2)}) collective-permute-start(bf16[2,4,48,1280]{3,2,1,0:T(8,128)(2,1)S(1)} %pad_maximum_fusion.2.refs_0_), channel_id=1, source_target_pairs={{0,4},{1,3},{2,6},{3,1},{4,0},{5,7},{6,2},{7,5},{8,12},{9,11},{10,... | collective-permute-start | bytes 2949128 | tf_op jit(solution)/shard_map/ppermute | solution.py:858
  29.9 17.4 %collective-permute-start.9 = (bf16[2,48,1920]{2,1,0:T(8,128)(2,1)S(1)}, bf16[2,48,1920]{2,1,0:T(8,128)(2,1)S(1)}, u32[]{:S(2)}, u32[]{:S(2)}) collective-permute-start(bf16[2,48,1920]{2,1,0:T(8,128)(2,1)S(1)} %pad_maximum_fusion.5), channel_id=1, source_target_pairs={{0,16},{1,17},{2,18},{3,19},{4,20},{5,21},{6,22},{7,23},{8,24},{9,... | collective-permute-start | bytes 1105928 | tf_op jit(solution)/shard_map/ppermute | solution.py:858
  31.8 17.7 %collective-permute-start.8 = (bf16[2,4,48,1280]{3,2,1,0:T(8,128)(2,1)S(1)}, bf16[2,4,48,1280]{3,2,1,0:T(8,128)(2,1)}, u32[]{:S(2)}, u32[]{:S(2)}) collective-permute-start(bf16[2,4,48,1280]{3,2,1,0:T(8,128)(2,1)S(1)} %pad_maximum_fusion.2.refs_0_), channel_id=1, source_target_pairs={{0,1},{1,0},{2,3},{3,2},{4,5},{5,4},{6,7},{7,6},{8,9},{9,8},{10,11... | collective-permute-start | bytes 2949128 | tf_op jit(solution)/shard_map/ppermute | solution.py:858
  47.5 30.6 %collective-permute-start.16 = (bf16[4,48,1920]{2,1,0:T(8,128)(2,1)S(1)}, bf16[4,48,1920]{2,1,0:T(8,128)(2,1)S(1)}, u32[]{:S(2)}, u32[]{:S(2)}) collective-permute-start(bf16[4,48,1920]{2,1,0:T(8,128)(2,1)S(1)} %constant_dynamic-update-slice_fusion), channel_id=1, source_target_pairs={{0,1},{1,0},{2,3},{3,2},{4,5},{5,4},{6,7},{7,6},{8,9},{9,8},{10,11... | collective-permute-start | bytes 2211848 | tf_op jit(solution)/shard_map/ppermute | solution.py:858
  48.0 17.8 %collective-permute-start.13 = (bf16[4,48,1920]{2,1,0:T(8,128)(2,1)S(1)}, bf16[4,48,1920]{2,1,0:T(8,128)(2,1)S(1)}, u32[]{:S(2)}, u32[]{:S(2)}) collective-permute-start(bf16[4,48,1920]{2,1,0:T(8,128)(2,1)S(1)} %constant_dynamic-update-slice_fusion), channel_id=1, source_target_pairs={{0,2},{1,5},{2,0},{3,7},{4,6},{5,1},{6,4},{7,3},{8,10},{9,13},{10,... | collective-permute-start | bytes 2211848 | tf_op jit(solution)/shard_map/ppermute | solution.py:858
  48.5 20.0 %collective-permute-start.11 = (bf16[2,192,384]{2,1,0:T(8,128)(2,1)}, bf16[2,192,384]{2,1,0:T(8,128)(2,1)S(1)}, u32[]{:S(2)}, u32[]{:S(2)}) collective-permute-start(bf16[2,192,384]{2,1,0:T(8,128)(2,1)} %pad_maximum_fusion.7), channel_id=1, source_target_pairs={{0,16},{1,17},{2,18},{3,19},{4,20},{5,21},{6,22},{7,23},{8,24},{9,... | collective-permute-start | bytes 884744 | tf_op jit(solution)/shard_map/ppermute | solution.py:858
  49.5 28.6 %collective-permute-start.12 = (bf16[4,48,1920]{2,1,0:T(8,128)(2,1)S(1)}, bf16[4,48,1920]{2,1,0:T(8,128)(2,1)S(1)}, u32[]{:S(2)}, u32[]{:S(2)}) collective-permute-start(bf16[4,48,1920]{2,1,0:T(8,128)(2,1)S(1)} %constant_dynamic-update-slice_fusion), channel_id=1, source_target_pairs={{0,4},{1,3},{2,6},{3,1},{4,0},{5,7},{6,2},{7,5},{8,12},{9,11},{10,... | collective-permute-start | bytes 2211848 | tf_op jit(solution)/shard_map/ppermute | solution.py:858
  65.8 14.2 %collective-permute-start.17 = (bf16[4,48,1920]{2,1,0:T(8,128)(2,1)S(1)}, bf16[4,48,1920]{2,1,0:T(8,128)(2,1)S(1)}, u32[]{:S(2)}, u32[]{:S(2)}) collective-permute-start(bf16[4,48,1920]{2,1,0:T(8,128)(2,1)S(1)} %collective-permute-done.13), channel_id=1, source_target_pairs={{0,1},{1,0},{2,3},{3,2},{4,5},{5,4},{6,7},{7,6},{8,9},{9,8},{10,11... | collective-permute-start | bytes 2211848 | tf_op jit(solution)/shard_map/ppermute | solution.py:858
  68.7 16.8 %collective-permute-start.15 = (bf16[512,768]{1,0:T(8,128)(2,1)S(1)}, bf16[512,768]{1,0:T(8,128)(2,1)S(1)}, u32[]{:S(2)}, u32[]{:S(2)}) collective-permute-start(bf16[512,768]{1,0:T(8,128)(2,1)S(1)} %get-tuple-element.255), channel_id=1, source_target_pairs={{0,1},{1,0},{2,3},{3,2},{4,5},{5,4},{6,7},{7,6},{8,9},{9,8},{10,11... | collective-permute-start | bytes 2359304 | tf_op jit(solution)/shard_map/ppermute | solution.py:858
  78.3 41.9 %collective-permute-start.23 = (bf16[4,192,384]{2,1,0:T(8,128)(2,1)S(1)}, bf16[4,192,384]{2,1,0:T(8,128)(2,1)S(1)}, u32[]{:S(2)}, u32[]{:S(2)}) collective-permute-start(bf16[4,192,384]{2,1,0:T(8,128)(2,1)S(1)} %constant_dynamic-update-slice_fusion.2), channel_id=1, source_target_pairs={{0,1},{1,0},{2,3},{3,2},{4,5},{5,4},{6,7},{7,6},{8,9},{9,8},{10,11... | collective-permute-start | bytes 1769480 | tf_op jit(solution)/shard_map/ppermute | solution.py:858
  78.7 30.1 %collective-permute-start.21 = (bf16[4,192,384]{2,1,0:T(8,128)(2,1)S(1)}, bf16[4,192,384]{2,1,0:T(8,128)(2,1)S(1)}, u32[]{:S(2)}, u32[]{:S(2)}) collective-permute-start(bf16[4,192,384]{2,1,0:T(8,128)(2,1)S(1)} %constant_dynamic-update-slice_fusion.2), channel_id=1, source_target_pairs={{0,4},{1,3},{2,6},{3,1},{4,0},{5,7},{6,2},{7,5},{8,12},{9,11},{10,... | collective-permute-start | bytes 1769480 | tf_op jit(solution)/shard_map/ppermute | solution.py:858
  84.7 22.3 %collective-permute-start.20 = (bf16[4,192,384]{2,1,0:T(8,128)(2,1)S(1)}, bf16[4,192,384]{2,1,0:T(8,128)(2,1)S(1)}, u32[]{:S(2)}, u32[]{:S(2)}) collective-permute-start(bf16[4,192,384]{2,1,0:T(8,128)(2,1)S(1)} %constant_dynamic-update-slice_fusion.2), channel_id=1, source_target_pairs={{0,2},{1,5},{2,0},{3,7},{4,6},{5,1},{6,4},{7,3},{8,10},{9,13},{10,... | collective-permute-start | bytes 1769480 | tf_op jit(solution)/shard_map/ppermute | solution.py:858
  107.1 13.4 %collective-permute-start.24 = (bf16[4,192,384]{2,1,0:T(8,128)(2,1)S(1)}, bf16[4,192,384]{2,1,0:T(8,128)(2,1)S(1)}, u32[]{:S(2)}, u32[]{:S(2)}) collective-permute-start(bf16[4,192,384]{2,1,0:T(8,128)(2,1)S(1)} %collective-permute-done.20), channel_id=1, source_target_pairs={{0,1},{1,0},{2,3},{3,2},{4,5},{5,4},{6,7},{7,6},{8,9},{9,8},{10,11... | collective-permute-start | bytes 1769480 | tf_op jit(solution)/shard_map/ppermute | solution.py:858
  120.2 23.9 %collective-permute-start.27 = (bf16[3072,384]{1,0:T(8,128)(2,1)}, bf16[3072,384]{1,0:T(8,128)(2,1)S(1)}, u32[]{:S(2)}, u32[]{:S(2)}) collective-permute-start(bf16[3072,384]{1,0:T(8,128)(2,1)} %get-tuple-element.175), channel_id=1, source_target_pairs={{0,1},{1,0},{2,3},{3,2},{4,5},{5,4},{6,7},{7,6},{8,9},{9,8},{10,11... | collective-permute-start | bytes 7077896 | tf_op jit(solution)/shard_map/ppermute | solution.py:858
  144.6 16.4 %collective-permute-start.29 = (bf16[2,4,1,192,384]{4,3,1,2,0:T(8,128)(2,1)S(1)}, bf16[2,4,1,192,384]{4,3,1,2,0:T(8,128)(2,1)}, u32[]{:S(2)}, u32[]{:S(2)}) collective-permute-start(bf16[2,4,1,192,384]{4,3,1,2,0:T(8,128)(2,1)S(1)} %pad_maximum_fusion.1), channel_id=1, source_target_pairs={{0,2},{1,5},{2,0},{3,7},{4,6},{5,1},{6,4},{7,3},{8,10},{9,13},{10,... | collective-permute-start | bytes 3538952 | tf_op jit(solution)/shard_map/ppermute | solution.py:858
  159.3 15.0 %collective-permute-start.28 = (bf16[768,1920]{1,0:T(8,128)(2,1)}, bf16[768,1920]{1,0:T(8,128)(2,1)S(1)}, u32[]{:S(2)}, u32[]{:S(2)}) collective-permute-start(bf16[768,1920]{1,0:T(8,128)(2,1)} %get-tuple-element.178), channel_id=1, source_target_pairs={{0,1},{1,0},{2,3},{3,2},{4,5},{5,4},{6,7},{7,6},{8,9},{9,8},{10,11... | collective-permute-start | bytes 8847368 | tf_op jit(solution)/shard_map/ppermute | solution.py:858
  174.2 17.0 %collective-permute-start.31 = (bf16[2,192,384]{2,1,0:T(8,128)(2,1)S(1)}, bf16[2,192,384]{2,1,0:T(8,128)(2,1)S(1)}, u32[]{:S(2)}, u32[]{:S(2)}) collective-permute-start(bf16[2,192,384]{2,1,0:T(8,128)(2,1)S(1)} %pad_maximum_fusion.8), channel_id=1, source_target_pairs={{0,16},{1,17},{2,18},{3,19},{4,20},{5,21},{6,22},{7,23},{8,24},{9,... | collective-permute-start | bytes 884744 | tf_op jit(solution)/shard_map/ppermute | solution.py:858
  175.1 19.4 %collective-permute-start.32 = (bf16[2,4,1,48,1920]{4,3,1,2,0:T(8,128)(2,1)S(1)}, bf16[2,4,1,48,1920]{4,3,1,2,0:T(8,128)(2,1)S(1)}, u32[]{:S(2)}, u32[]{:S(2)}) collective-permute-start(bf16[2,4,1,48,1920]{4,3,1,2,0:T(8,128)(2,1)S(1)} %pad_maximum_fusion), channel_id=1, source_target_pairs={{0,2},{1,5},{2,0},{3,7},{4,6},{5,1},{6,4},{7,3},{8,10},{9,13},{10,... | collective-permute-start | bytes 4423688 | tf_op jit(solution)/shard_map/ppermute | solution.py:858
  207.6 19.6 %collective-permute-start.38 = (bf16[2,48,1920]{2,1,0:T(8,128)(2,1)S(1)}, bf16[2,48,1920]{2,1,0:T(8,128)(2,1)S(1)}, u32[]{:S(2)}, u32[]{:S(2)}) collective-permute-start(bf16[2,48,1920]{2,1,0:T(8,128)(2,1)S(1)} %pad_maximum_fusion.6), channel_id=1, source_target_pairs={{0,16},{1,17},{2,18},{3,19},{4,20},{5,21},{6,22},{7,23},{8,24},{9,... | collective-permute-start | bytes 1105928 | tf_op jit(solution)/shard_map/ppermute | solution.py:858
  218.8 40.5 %collective-permute-start.46 = (f32[192,384]{1,0:T(8,128)S(1)}, f32[192,384]{1,0:T(8,128)S(1)}, u32[]{:S(2)}, u32[]{:S(2)}) collective-permute-start(f32[192,384]{1,0:T(8,128)S(1)} %fusion.16.refs_0_), channel_id=1, source_target_pairs={{0,1},{1,0},{2,3},{3,2},{4,5},{5,4},{6,7},{7,6},{8,9},{9,8},{10,11... | collective-permute-start | bytes 884744 | tf_op jit(solution)/shard_map/ppermute | solution.py:858
  227.5 24.0 %collective-permute-start.49 = (f32[16,768]{1,0:T(8,128)S(1)}, f32[16,768]{1,0:T(8,128)S(1)}, u32[]{:S(2)}, u32[]{:S(2)}) collective-permute-start(f32[16,768]{1,0:T(8,128)S(1)} %add.657), channel_id=1, source_target_pairs={{0,4},{1,3},{2,6},{3,1},{4,0},{5,7},{6,2},{7,5},{8,12},{9,11},{10,... | collective-permute-start | bytes 147464 | tf_op jit(solution)/shard_map/ppermute | solution.py:858
  234.0 17.0 %collective-permute-start.40 = (bf16[2,48,1152]{2,1,0:T(8,128)(2,1)S(1)}, bf16[2,48,1152]{2,1,0:T(8,128)(2,1)S(1)}, u32[]{:S(2)}, u32[]{:S(2)}) collective-permute-start(bf16[2,48,1152]{2,1,0:T(8,128)(2,1)S(1)} %pad_maximum_fusion.9), channel_id=1, source_target_pairs={{0,16},{1,17},{2,18},{3,19},{4,20},{5,21},{6,22},{7,23},{8,24},{9,... | collective-permute-start | bytes 663560 | tf_op jit(solution)/shard_map/ppermute | solution.py:858
  240.4 20.5 %collective-permute-start.44 = (f32[48,1920]{1,0:T(8,128)S(1)}, f32[48,1920]{1,0:T(8,128)S(1)}, u32[]{:S(2)}, u32[]{:S(2)}) collective-permute-start(f32[48,1920]{1,0:T(8,128)S(1)} %convert_add_fusion.8.refs_0_), channel_id=1, source_target_pairs={{0,1},{1,0},{2,3},{3,2},{4,5},{5,4},{6,7},{7,6},{8,9},{9,8},{10,11... | collective-permute-start | bytes 1105928 | tf_op jit(solution)/shard_map/ppermute | solution.py:858
  (92 other events, 911.0 us)

commit v5 on v4

--- a/solution.py
+++ b/solution.py
@@ -880,19 +880,9 @@
                         found.append(z * self.n * self.n + flat)
         return jnp.stack(found).astype(jnp.int32)
 
-    def total_small(self, value, *untils):
-        steps = [("core", 0), ("first", 1), ("second", 1)] if self.n == 2 else [("core", 0)]
-        if self.n != 2:
-            for axis in ("first", "second"):
-                value = value + sum(self.permute(value, axis, s) for s in range(1, self.n))
-        bit = 1
-        while bit < self.nz:
-            steps.append(("zx", bit))
-            bit *= 2
-        for at, (axis, shift) in enumerate(steps):
-            until = untils[at] if at < len(untils) else ()
-            value = value + after(self.permute(value, axis, shift), *until)
-        return value
+    def small(self, value, axis, shifts, *until):
+        got = [after(self.permute(value, axis, s), *until) for s in shifts]
+        return value + sum(got), got
 
     def gather_z(self, block, *until):
         return jnp.stack([block] + [after(self.permute(block, "z", s), *until) for s in range(1, self.nz)])
@@ -1082,19 +1072,27 @@
         [(FF ** (-0.5), MATRIX_DECAY, [(0, 0, D // 2, 0, D // 2)])],
     )
     in_got = grid.swap(after(in_theirs, *q_kept[1]))
-    u_mine = grid.scatter_z([after(part, *q_here) for part in u_parts])
+    in_grad = both_slots(in_mine, after(in_got, *q_here))
+    w_qkv = after(w_qkv, in_grad)
+    shifts = range(1, grid.n)
+    vec_total, _ = grid.small(acc, "core", [0])
+    vec_total, _ = grid.small(vec_total, "first", shifts, *q_kept[1])
+    vec_total, vec_here_got = grid.small(vec_total, "second", shifts, *q_here)
+    out_theirs, out_mine = out_call(
+        core_arr, lengths, seats, after(mid, *q_here, *vec_here_got), e, vec, d_group
+    )
+    u_mine = grid.scatter_z([after(part, *q_here) for part in u_parts], out_theirs)
     u_other_mine = grid.swap(u_mine)
-    in_grad = both_slots(in_mine, after(in_got, *q_here))
-    out_theirs, out_mine = out_call(core_arr, lengths, seats, after(mid, in_grad, *q_here), e, vec, d_group)
     q_parts, q_got = grid.scatter_bit(grid.order_z(q_sum), out_theirs)
     block_out = both_slots(out_mine, grid.swap(out_theirs))
-    q_gots = [(q_got,)]
+    until = (out_theirs,)
+    for bit in bits[:-1]:
+        vec_total, _ = grid.small(vec_total, "zx", [bit], *until)
     while len(q_parts) > 1:
         q_parts, q_got = grid.scatter_bit(q_parts)
-        q_gots.append((q_got,))
+    vec_total, _ = grid.small(vec_total, "zx", [bits[-1]], q_got)
     q_mine = q_parts[0]
     q_other_mine = grid.swap(q_mine)
-    vec_total = grid.total_small(acc, (), q_kept[1], q_here, *q_gots)
 
     half, wide = D // 2, FF // 2
     out_new, up_new = adam_call(

time: 272 us -> 267 us (0.982)
  waiting for transfers between devices: 65.2 us -> 55.9 us
    ppermute x52, waiting for transfers between devices: 65.2 us -> 55.9 us  [permute(): return lax.ppermute(value, ('dp', 'seq'), pairs)]
    unnamed x130 -> x134, local copies, waits for them, and re-layouts: 9.33 us -> 9.51 us
  transfers between devices with their start and end apart: 52 -> 52, of which waited for: 21 -> 20; matrix products, arithmetic and copies ran while one was open for 5% -> 7% of each run, Pallas kernels for 50% -> 50%
where the time goes in v5:
time: 267 us; the launch traced here: 263 us
  Pallas kernels  135 us (51%)
  waiting for transfers between devices  55.9 us (21%)
  starting transfers between devices  40.7 us (15%)
  local copies, waits for them, and re-layouts  16.7 us (6%)
  other arithmetic  12.9 us (5%)
    ppermute x52, waiting for transfers between devices, permute(): return lax.ppermute(value, ('dp', 'seq'), pairs)  55.9 us
    ppermute x52, starting transfers between devices, permute(): return lax.ppermute(value, ('dp', 'seq'), pairs)  40.7 us
    pallas_call x3, Pallas kernels, weight_grad_call(): pl.pallas_call(functools.partial(weight_grad_kernel, len(lefts), [len(gro...  26.3 us
    pallas_call x2, Pallas kernels, attend_back_call(): pl.pallas_call(attend_back_kernel, name='attend_back', grid_spec=pltpu.Pr...  23.6 us
    pallas_call x1, Pallas kernels, down_call(): pl.pallas_call(functools.partial(down_kernel, up_group, down_group), name...  22.1 us
    pallas_call x1, Pallas kernels, up_call(): pl.pallas_call(functools.partial(up_kernel, group), name='up', grid_spec=...  19.7 us
    pallas_call x2, Pallas kernels, attend_call(): pl.pallas_call(functools.partial(attend_kernel, first), name='attend', gr...  13.7 us
    unnamed x134, local copies, waits for them, and re-layouts  9.51 us
  transfers between devices with their start and end apart: 52, of which 20 were waited for; matrix products, arithmetic and copies ran while one was open for 7% of the time, Pallas kernels for 50%

profile of v5, /device:TPU:0, one launch (start us, length us, event | category | flops | bytes accessed | tf_op | source)
XLA Modules:
  0.0 263.1 jit_solution(11286315106729196382)
XLA Ops:
  3.2 4.1 %collective-permute-start.2 = (bf16[48,1280]{1,0:T(8,128)(2,1)S(1)}, bf16[48,1280]{1,0:T(8,128)(2,1)S(1)}, u32[]{:S(2)}, u32[]{:S(2)}) collective-permute-start(bf16[48,1280]{1,0:T(8,128)(2,1)S(1)} %get-tuple-element.271), channel_id=1, source_target_pairs={{0,16},{1,17},{2,18},{3,19},{4,20},{5,21},{6,22},{7,23},{8,24},{9,... | collective-permute-start | bytes 368648 | tf_op jit(solution)/shard_map/ppermute | solution.py:858
  13.0 3.8 %collective-permute-done.2 = bf16[48,1280]{1,0:T(8,128)(2,1)S(1)} collective-permute-done((bf16[48,1280]{1,0:T(8,128)(2,1)S(1)}, bf16[48,1280]{1,0:T(8,128)(2,1)S(1)}, u32[]{:S(2)}, u32[]{:S(2)}) %collective-permute-start.2) | collective-permute-done | bytes 122912 | tf_op jit(solution)/shard_map/ppermute | solution.py:858
  25.3 2.9 %collective-permute-done.4 = bf16[4,48,1280]{2,1,0:T(8,128)(2,1)S(1)} collective-permute-done((bf16[4,48,1280]{2,1,0:T(8,128)(2,1)S(1)}, bf16[4,48,1280]{2,1,0:T(8,128)(2,1)S(1)}, u32[]{:S(2)}, u32[]{:S(2)}) %collective-permute-start.4) | collective-permute-done | bytes 491552 | tf_op jit(solution)/shard_map/ppermute | solution.py:858
  31.9 15.5 %collective-permute-done.9 = bf16[2,48,1920]{2,1,0:T(8,128)(2,1)S(1)} collective-permute-done((bf16[2,48,1920]{2,1,0:T(8,128)(2,1)S(1)}, bf16[2,48,1920]{2,1,0:T(8,128)(2,1)S(1)}, u32[]{:S(2)}, u32[]{:S(2)}) %collective-permute-start.9) | collective-permute-done | bytes 368672 | tf_op jit(solution)/shard_map/ppermute | solution.py:858
  51.1 9.5 %qkv.1 = (bf16[1024,768]{1,0:T(8,128)(2,1)S(1)}, bf16[1024,2304]{1,0:T(8,128)(2,1)S(1)}, f32[16,768]{1,0:T(8,128)S(1)}, bf16[2304,768]{1,0:T(8,128)(2,1)S(1)}) custom-call(s32[1]{0:T(128)} %bitcast.64.core_ref, s32[32]{0:T(128)S(1)} %convert_element_type.410.seat_ref, bf16[1024,768]{1,0:T(8,128)(2,1)S(1)} %maximum_select_fusion.x_ref, ...), custom_call_target="tpu_custom_call" | custom-call | flops 14495514624 | bytes 40000000 | tf_op jit(solution)/shard_map/qkv/pallas_call | solution.py:161
  65.8 2.7 %collective-permute-start.14 = (bf16[4,48,1920]{2,1,0:T(8,128)(2,1)S(1)}, bf16[4,48,1920]{2,1,0:T(8,128)(2,1)S(1)}, u32[]{:S(2)}, u32[]{:S(2)}) collective-permute-start(bf16[4,48,1920]{2,1,0:T(8,128)(2,1)S(1)} %collective-permute-done.13), channel_id=1, source_target_pairs={{0,4},{1,3},{2,6},{3,1},{4,0},{5,7},{6,2},{7,5},{8,12},{9,11},{10,... | collective-permute-start | bytes 2211848 | tf_op jit(solution)/shard_map/ppermute | solution.py:858
  69.2 8.9 %attend.2 = (bf16[1024,768]{1,0:T(8,128)(2,1)S(1)}, f32[6,8,1024]{2,1,0:T(8,128)S(1)}) custom-call(s32[1]{0:T(128)} %bitcast.64.core_ref, s32[2]{0:T(128)S(1)} %copy-done.38, bf16[1024,2304]{1,0:T(8,128)(2,1)S(1)} %get-tuple-element.152.qkv_ref.q_ref.k_ref.v_ref), custom_call_target="tpu_custom_call" | custom-call | flops 48000000000 | bytes 19200000 | tf_op jit(solution)/shard_map/attend/pallas_call | solution.py:274
  80.0 4.8 %attend.3 = (bf16[1024,768]{1,0:T(8,128)(2,1)S(1)}, f32[6,8,1024]{2,1,0:T(8,128)S(1)}) custom-call(s32[1]{0:T(128)} %bitcast.64.core_ref, s32[2]{0:T(128)S(1)} %copy-done.38, bf16[1024,2304]{1,0:T(8,128)(2,1)S(1)} %get-tuple-element.152.qkv_ref.q_ref.k_ref.v_ref, ...), custom_call_target="tpu_custom_call", output_to_operand_aliasing={{0}: (3, {}), {1}: (4, {})} | custom-call | flops 24000000000 | bytes 9600000 | tf_op jit(solution)/shard_map/attend/pallas_call | solution.py:274
  87.4 19.7 %up.1 = (f32[1024,768]{1,0:T(8,128)}, bf16[1024,768]{1,0:T(8,128)(2,1)}, bf16[1024,3072]{1,0:T(8,128)(2,1)}, bf16[1024,3072]{1,0:T(8,128)(2,1)}, bf16[1024,768]{1,0:T(8,128)(2,1)}) custom-call(s32[1]{0:T(128)} %bitcast.64.core_ref, s32[2]{0:T(128)S(1)} %copy-done.38, s32[32]{0:T(128)S(1)} %convert_element_type.409.seat_ref, bf16[1024,768]{1,0:T(8,128)(2,1)} %copy-done, ...), custom_call_target="tpu_custom_call" | custom-call | flops 24000000000 | bytes 120000000 | tf_op jit(solution)/shard_map/up/pallas_call | solution.py:458
  110.4 9.5 %grad_down.1 = (bf16[3072,384]{1,0:T(8,128)(2,1)S(1)}, bf16[3072,384]{1,0:T(8,128)(2,1)}) custom-call(s32[1]{0:T(128)} %bitcast.64.core_ref, bf16[1024,3072]{1,0:T(8,128)(2,1)} %get-tuple-element.167.refs_0_.e_ref, bf16[1024,768]{1,0:T(8,128)(2,1)S(1)} %copy-done.48), custom_call_target="tpu_custom_call" | custom-call | flops 19327352832 | bytes 50331648 | tf_op jit(solution)/shard_map/grad_down/pallas_call | solution.py:660
  121.9 22.1 %down.1 = (bf16[1024,3072]{1,0:T(8,128)(2,1)}, bf16[1024,768]{1,0:T(8,128)(2,1)}, f32[1024,768]{1,0:T(8,128)}, bf16[1024,768]{1,0:T(8,128)(2,1)}, f32[16,768]{1,0:T(8,128)S(1)}) custom-call(s32[1]{0:T(128)} %bitcast.64.core_ref, s32[32]{0:T(128)S(1)} %convert_element_type.409.seat_ref, f32[1024,768]{1,0:T(8,128)} %get-tuple-element.218.mid_ref, ...), custom_call_target="tpu_custom_call" | custom-call | flops 44000002048 | bytes 112000000 | tf_op jit(solution)/shard_map/down/pallas_call | solution.py:537
  147.3 11.9 %grad_up.1 = (bf16[768,1920]{1,0:T(8,128)(2,1)}, bf16[768,1920]{1,0:T(8,128)(2,1)}) custom-call(s32[1]{0:T(128)} %bitcast.64.core_ref, bf16[1024,768]{1,0:T(8,128)(2,1)S(1)} %copy-done.51, bf16[1024,768]{1,0:T(8,128)(2,1)S(1)} %copy-done.49, bf16[1024,768]{1,0:T(8,128)(2,1)S(1)} %copy-done.52, bf16[1024,3072]{1,0:T(8,128)(2,1)} %get-tuple-element.179.refs_3_), custom_call_target="tpu_custom_call" | custom-call | flops 24159191040 | bytes 61341696 | tf_op jit(solution)/shard_map/grad_up/pallas_call | solution.py:660
  163.2 8.2 %attend_back.2 = (bf16[1024,768]{1,0:T(8,128)(2,1)S(1)}, bf16[1024,768]{1,0:T(8,128)(2,1)S(1)}, bf16[1024,768]{1,0:T(8,128)(2,1)S(1)}) custom-call(s32[1]{0:T(128)} %bitcast.64.core_ref, s32[2]{0:T(128)S(1)} %copy-done.38, bf16[1024,2304]{1,0:T(8,128)(2,1)S(1)} %bitcast.276, bf16[1024,2304]{1,0:T(8,128)(2,1)S(1)} %bitcast.276, ...), custom_call_target="tpu_custom_call" | custom-call | flops 48000000000 | bytes 16000000 | tf_op jit(solution)/shard_map/attend_back/pallas_call | solution.py:371
  175.8 15.4 %attend_back.3 = (bf16[1024,768]{1,0:T(8,128)(2,1)S(1)}, bf16[1024,768]{1,0:T(8,128)(2,1)S(1)}, bf16[1024,768]{1,0:T(8,128)(2,1)S(1)}) custom-call(s32[1]{0:T(128)} %bitcast.64.core_ref, s32[2]{0:T(128)S(1)} %copy-done.38, bf16[1024,2304]{1,0:T(8,128)(2,1)S(1)} %bitcast.276, ...), custom_call_target="tpu_custom_call", output_to_operand_aliasing={{0}: (8, {}), {1}: (9, {}), {2}: (10, {})} | custom-call | flops 96000000000 | bytes 32000000 | tf_op jit(solution)/shard_map/attend_back/pallas_call | solution.py:371
  191.2 3.3 %collective-permute-done.32 = bf16[2,4,1,48,1920]{4,3,1,2,0:T(8,128)(2,1)S(1)} collective-permute-done((bf16[2,4,1,48,1920]{4,3,1,2,0:T(8,128)(2,1)S(1)}, bf16[2,4,1,48,1920]{4,3,1,2,0:T(8,128)(2,1)S(1)}, u32[]{:S(2)}, u32[]{:S(2)}) %collective-permute-start.32) | collective-permute-done | bytes 1474592 | tf_op jit(solution)/shard_map/ppermute | solution.py:858
  195.6 4.9 %grad_qkv.1 = (bf16[768,1152]{1,0:T(8,128)(2,1)S(1)}, bf16[768,1152]{1,0:T(8,128)(2,1)S(1)}) custom-call(s32[1]{0:T(128)} %bitcast.64.core_ref, bf16[1024,768]{1,0:T(8,128)(2,1)S(1)} %copy-done.47, bf16[1024,768]{1,0:T(8,128)(2,1)S(1)} %get-tuple-element.208.refs_1_.dq_ref, bf16[1024,768]{1,0:T(8,128)(2,1)S(1)} %get-tuple-element.198.refs_2_.dk_ref, ...), custom_call_target="tpu_custom_call" | custom-call | flops 14495514624 | bytes 39321600 | tf_op jit(solution)/shard_map/grad_qkv/pallas_call | solution.py:660
  200.6 5.7 %collective-permute-done.33 = bf16[4,1,48,1920]{3,2,1,0:T(8,128)(2,1)S(1)} collective-permute-done((bf16[4,1,48,1920]{3,2,1,0:T(8,128)(2,1)S(1)}, bf16[4,1,48,1920]{3,2,1,0:T(8,128)(2,1)S(1)}, u32[]{:S(2)}, u32[]{:S(2)}) %collective-permute-start.33) | collective-permute-done | bytes 737312 | tf_op jit(solution)/shard_map/ppermute | solution.py:858
  211.4 7.2 %last.1 = (f32[512,768]{1,0:T(8,128)S(1)}, f32[2,512,768]{2,1,0:T(8,128)}, f32[16,768]{1,0:T(8,128)S(1)}) custom-call(s32[1]{0:T(128)} %bitcast.64.core_ref, bf16[1024,768]{1,0:T(8,128)(2,1)S(1)} %copy-done.1, f32[1024,768]{1,0:T(8,128)S(1)} %copy-done.44, bf16[1024,768]{1,0:T(8,128)(2,1)S(1)} %get-tuple-element.208.refs_1_.dq_ref, ...), custom_call_target="tpu_custom_call" | custom-call | flops 14495514624 | bytes 64000000 | tf_op jit(solution)/shard_map/last/pallas_call | solution.py:724
  221.0 2.4 collective-permute-done.35
  224.5 2.7 %collective-permute-done.37 = bf16[2,48,1920]{2,1,0:T(8,128)(2,1)S(1)} collective-permute-done((bf16[2,48,1920]{2,1,0:T(8,128)(2,1)S(1)}, bf16[2,48,1920]{2,1,0:T(8,128)(2,1)S(1)}, u32[]{:S(2)}, u32[]{:S(2)}) %collective-permute-start.37) | collective-permute-done | bytes 368672 | tf_op jit(solution)/shard_map/ppermute | solution.py:858
  234.7 2.6 %collective-permute-start.43 = (bf16[2,48,1152]{2,1,0:T(8,128)(2,1)S(1)}, bf16[2,48,1152]{2,1,0:T(8,128)(2,1)S(1)}, u32[]{:S(2)}, u32[]{:S(2)}) collective-permute-start(bf16[2,48,1152]{2,1,0:T(8,128)(2,1)S(1)} %pad_maximum_fusion.9), channel_id=1, source_target_pairs={{0,16},{1,17},{2,18},{3,19},{4,20},{5,21},{6,22},{7,23},{8,24},{9,... | collective-permute-start | bytes 663560 | tf_op jit(solution)/shard_map/ppermute | solution.py:858
  237.4 8.0 %out.1 = (bf16[512,768]{1,0:T(8,128)(2,1)S(1)}, bf16[2,512,768]{2,1,0:T(8,128)(2,1)}) custom-call(s32[1]{0:T(128)} %bitcast.64.core_ref, s32[2]{0:T(128)S(1)} %copy-done.38, s32[32]{0:T(128)S(1)} %copy-done.40, f32[1024,768]{1,0:T(8,128)S(1)} %copy-done.45, bf16[1024,3072]{1,0:T(8,128)(2,1)S(1)} %bitcast.278, f32[16,768]{1,0:T(8,128)S(1)} %get-tuple-element.155.vec_ref, ...), custom_call_target="tpu_custom_call" | custom-call | flops 19599998976 | bytes 64000000 | tf_op jit(solution)/shard_map/out/pallas_call | solution.py:599
  247.9 3.5 %collective-permute-done.51 = f32[16,768]{1,0:T(8,128)S(1)} collective-permute-done((f32[16,768]{1,0:T(8,128)S(1)}, f32[16,768]{1,0:T(8,128)S(1)}, u32[]{:S(2)}, u32[]{:S(2)}) %collective-permute-start.51) | collective-permute-done | bytes 49184 | tf_op jit(solution)/shard_map/ppermute | solution.py:858
  256.4 2.8 %bitcast_dynamic-update-slice_fusion = f32[2,512,768]{2,1,0:T(8,128)} fusion(f32[2,512,768]{2,1,0:T(8,128)} %get-tuple-element.221, u32[]{:T(128)S(6)} %convert_element_type.395, f32[512,768]{1,0:T(8,128)} %collective-permute-done.42), kind=kLoop, calls=%fused_computation.2 | loop fusion | bytes 3145732 | tf_op jit(solution)/shard_map/dynamic_update_slice | solution.py:978
  (290 shorter events, 78.7 us)
Async XLA Ops:
  3.2 13.6 %collective-permute-start.2 = (bf16[48,1280]{1,0:T(8,128)(2,1)S(1)}, bf16[48,1280]{1,0:T(8,128)(2,1)S(1)}, u32[]{:S(2)}, u32[]{:S(2)}) collective-permute-start(bf16[48,1280]{1,0:T(8,128)(2,1)S(1)} %get-tuple-element.271), channel_id=1, source_target_pairs={{0,16},{1,17},{2,18},{3,19},{4,20},{5,21},{6,22},{7,23},{8,24},{9,... | collective-permute-start | bytes 368648 | tf_op jit(solution)/shard_map/ppermute | solution.py:858
  28.3 19.1 %collective-permute-start.7 = (bf16[2,4,48,1280]{3,2,1,0:T(8,128)(2,1)S(1)}, bf16[2,4,48,1280]{3,2,1,0:T(8,128)(2,1)}, u32[]{:S(2)}, u32[]{:S(2)}) collective-permute-start(bf16[2,4,48,1280]{3,2,1,0:T(8,128)(2,1)S(1)} %pad_maximum_fusion.2.refs_0_), channel_id=1, source_target_pairs={{0,4},{1,3},{2,6},{3,1},{4,0},{5,7},{6,2},{7,5},{8,12},{9,11},{10,... | collective-permute-start | bytes 2949128 | tf_op jit(solution)/shard_map/ppermute | solution.py:858
  29.9 17.4 %collective-permute-start.9 = (bf16[2,48,1920]{2,1,0:T(8,128)(2,1)S(1)}, bf16[2,48,1920]{2,1,0:T(8,128)(2,1)S(1)}, u32[]{:S(2)}, u32[]{:S(2)}) collective-permute-start(bf16[2,48,1920]{2,1,0:T(8,128)(2,1)S(1)} %pad_maximum_fusion.5), channel_id=1, source_target_pairs={{0,16},{1,17},{2,18},{3,19},{4,20},{5,21},{6,22},{7,23},{8,24},{9,... | collective-permute-start | bytes 1105928 | tf_op jit(solution)/shard_map/ppermute | solution.py:858
  31.8 17.7 %collective-permute-start.8 = (bf16[2,4,48,1280]{3,2,1,0:T(8,128)(2,1)S(1)}, bf16[2,4,48,1280]{3,2,1,0:T(8,128)(2,1)}, u32[]{:S(2)}, u32[]{:S(2)}) collective-permute-start(bf16[2,4,48,1280]{3,2,1,0:T(8,128)(2,1)S(1)} %pad_maximum_fusion.2.refs_0_), channel_id=1, source_target_pairs={{0,1},{1,0},{2,3},{3,2},{4,5},{5,4},{6,7},{7,6},{8,9},{9,8},{10,11... | collective-permute-start | bytes 2949128 | tf_op jit(solution)/shard_map/ppermute | solution.py:858
  47.5 30.6 %collective-permute-start.16 = (bf16[4,48,1920]{2,1,0:T(8,128)(2,1)S(1)}, bf16[4,48,1920]{2,1,0:T(8,128)(2,1)S(1)}, u32[]{:S(2)}, u32[]{:S(2)}) collective-permute-start(bf16[4,48,1920]{2,1,0:T(8,128)(2,1)S(1)} %constant_dynamic-update-slice_fusion), channel_id=1, source_target_pairs={{0,1},{1,0},{2,3},{3,2},{4,5},{5,4},{6,7},{7,6},{8,9},{9,8},{10,11... | collective-permute-start | bytes 2211848 | tf_op jit(solution)/shard_map/ppermute | solution.py:858
  48.0 17.8 %collective-permute-start.13 = (bf16[4,48,1920]{2,1,0:T(8,128)(2,1)S(1)}, bf16[4,48,1920]{2,1,0:T(8,128)(2,1)S(1)}, u32[]{:S(2)}, u32[]{:S(2)}) collective-permute-start(bf16[4,48,1920]{2,1,0:T(8,128)(2,1)S(1)} %constant_dynamic-update-slice_fusion), channel_id=1, source_target_pairs={{0,2},{1,5},{2,0},{3,7},{4,6},{5,1},{6,4},{7,3},{8,10},{9,13},{10,... | collective-permute-start | bytes 2211848 | tf_op jit(solution)/shard_map/ppermute | solution.py:858
  48.5 20.0 %collective-permute-start.11 = (bf16[2,192,384]{2,1,0:T(8,128)(2,1)}, bf16[2,192,384]{2,1,0:T(8,128)(2,1)S(1)}, u32[]{:S(2)}, u32[]{:S(2)}) collective-permute-start(bf16[2,192,384]{2,1,0:T(8,128)(2,1)} %pad_maximum_fusion.7), channel_id=1, source_target_pairs={{0,16},{1,17},{2,18},{3,19},{4,20},{5,21},{6,22},{7,23},{8,24},{9,... | collective-permute-start | bytes 884744 | tf_op jit(solution)/shard_map/ppermute | solution.py:858
  49.5 28.6 %collective-permute-start.12 = (bf16[4,48,1920]{2,1,0:T(8,128)(2,1)S(1)}, bf16[4,48,1920]{2,1,0:T(8,128)(2,1)S(1)}, u32[]{:S(2)}, u32[]{:S(2)}) collective-permute-start(bf16[4,48,1920]{2,1,0:T(8,128)(2,1)S(1)} %constant_dynamic-update-slice_fusion), channel_id=1, source_target_pairs={{0,4},{1,3},{2,6},{3,1},{4,0},{5,7},{6,2},{7,5},{8,12},{9,11},{10,... | collective-permute-start | bytes 2211848 | tf_op jit(solution)/shard_map/ppermute | solution.py:858
  65.8 14.2 %collective-permute-start.17 = (bf16[4,48,1920]{2,1,0:T(8,128)(2,1)S(1)}, bf16[4,48,1920]{2,1,0:T(8,128)(2,1)S(1)}, u32[]{:S(2)}, u32[]{:S(2)}) collective-permute-start(bf16[4,48,1920]{2,1,0:T(8,128)(2,1)S(1)} %collective-permute-done.13), channel_id=1, source_target_pairs={{0,1},{1,0},{2,3},{3,2},{4,5},{5,4},{6,7},{7,6},{8,9},{9,8},{10,11... | collective-permute-start | bytes 2211848 | tf_op jit(solution)/shard_map/ppermute | solution.py:858
  68.7 16.8 %collective-permute-start.15 = (bf16[512,768]{1,0:T(8,128)(2,1)S(1)}, bf16[512,768]{1,0:T(8,128)(2,1)S(1)}, u32[]{:S(2)}, u32[]{:S(2)}) collective-permute-start(bf16[512,768]{1,0:T(8,128)(2,1)S(1)} %get-tuple-element.259), channel_id=1, source_target_pairs={{0,1},{1,0},{2,3},{3,2},{4,5},{5,4},{6,7},{7,6},{8,9},{9,8},{10,11... | collective-permute-start | bytes 2359304 | tf_op jit(solution)/shard_map/ppermute | solution.py:858
  78.3 41.9 %collective-permute-start.23 = (bf16[4,192,384]{2,1,0:T(8,128)(2,1)S(1)}, bf16[4,192,384]{2,1,0:T(8,128)(2,1)S(1)}, u32[]{:S(2)}, u32[]{:S(2)}) collective-permute-start(bf16[4,192,384]{2,1,0:T(8,128)(2,1)S(1)} %constant_dynamic-update-slice_fusion.2), channel_id=1, source_target_pairs={{0,1},{1,0},{2,3},{3,2},{4,5},{5,4},{6,7},{7,6},{8,9},{9,8},{10,11... | collective-permute-start | bytes 1769480 | tf_op jit(solution)/shard_map/ppermute | solution.py:858
  78.8 30.0 %collective-permute-start.21 = (bf16[4,192,384]{2,1,0:T(8,128)(2,1)S(1)}, bf16[4,192,384]{2,1,0:T(8,128)(2,1)S(1)}, u32[]{:S(2)}, u32[]{:S(2)}) collective-permute-start(bf16[4,192,384]{2,1,0:T(8,128)(2,1)S(1)} %constant_dynamic-update-slice_fusion.2), channel_id=1, source_target_pairs={{0,4},{1,3},{2,6},{3,1},{4,0},{5,7},{6,2},{7,5},{8,12},{9,11},{10,... | collective-permute-start | bytes 1769480 | tf_op jit(solution)/shard_map/ppermute | solution.py:858
  84.8 22.3 %collective-permute-start.20 = (bf16[4,192,384]{2,1,0:T(8,128)(2,1)S(1)}, bf16[4,192,384]{2,1,0:T(8,128)(2,1)S(1)}, u32[]{:S(2)}, u32[]{:S(2)}) collective-permute-start(bf16[4,192,384]{2,1,0:T(8,128)(2,1)S(1)} %constant_dynamic-update-slice_fusion.2), channel_id=1, source_target_pairs={{0,2},{1,5},{2,0},{3,7},{4,6},{5,1},{6,4},{7,3},{8,10},{9,13},{10,... | collective-permute-start | bytes 1769480 | tf_op jit(solution)/shard_map/ppermute | solution.py:858
  107.0 13.4 %collective-permute-start.24 = (bf16[4,192,384]{2,1,0:T(8,128)(2,1)S(1)}, bf16[4,192,384]{2,1,0:T(8,128)(2,1)S(1)}, u32[]{:S(2)}, u32[]{:S(2)}) collective-permute-start(bf16[4,192,384]{2,1,0:T(8,128)(2,1)S(1)} %collective-permute-done.20), channel_id=1, source_target_pairs={{0,1},{1,0},{2,3},{3,2},{4,5},{5,4},{6,7},{7,6},{8,9},{9,8},{10,11... | collective-permute-start | bytes 1769480 | tf_op jit(solution)/shard_map/ppermute | solution.py:858
  120.2 23.9 %collective-permute-start.27 = (bf16[3072,384]{1,0:T(8,128)(2,1)}, bf16[3072,384]{1,0:T(8,128)(2,1)S(1)}, u32[]{:S(2)}, u32[]{:S(2)}) collective-permute-start(bf16[3072,384]{1,0:T(8,128)(2,1)} %get-tuple-element.177), channel_id=1, source_target_pairs={{0,1},{1,0},{2,3},{3,2},{4,5},{5,4},{6,7},{7,6},{8,9},{9,8},{10,11... | collective-permute-start | bytes 7077896 | tf_op jit(solution)/shard_map/ppermute | solution.py:858
  144.5 16.4 %collective-permute-start.29 = (bf16[2,4,1,192,384]{4,3,1,2,0:T(8,128)(2,1)S(1)}, bf16[2,4,1,192,384]{4,3,1,2,0:T(8,128)(2,1)}, u32[]{:S(2)}, u32[]{:S(2)}) collective-permute-start(bf16[2,4,1,192,384]{4,3,1,2,0:T(8,128)(2,1)S(1)} %pad_maximum_fusion.1), channel_id=1, source_target_pairs={{0,2},{1,5},{2,0},{3,7},{4,6},{5,1},{6,4},{7,3},{8,10},{9,13},{10,... | collective-permute-start | bytes 3538952 | tf_op jit(solution)/shard_map/ppermute | solution.py:858
  159.2 15.0 %collective-permute-start.28 = (bf16[768,1920]{1,0:T(8,128)(2,1)}, bf16[768,1920]{1,0:T(8,128)(2,1)S(1)}, u32[]{:S(2)}, u32[]{:S(2)}) collective-permute-start(bf16[768,1920]{1,0:T(8,128)(2,1)} %get-tuple-element.180), channel_id=1, source_target_pairs={{0,1},{1,0},{2,3},{3,2},{4,5},{5,4},{6,7},{7,6},{8,9},{9,8},{10,11... | collective-permute-start | bytes 8847368 | tf_op jit(solution)/shard_map/ppermute | solution.py:858
  174.1 17.1 %collective-permute-start.31 = (bf16[2,192,384]{2,1,0:T(8,128)(2,1)S(1)}, bf16[2,192,384]{2,1,0:T(8,128)(2,1)S(1)}, u32[]{:S(2)}, u32[]{:S(2)}) collective-permute-start(bf16[2,192,384]{2,1,0:T(8,128)(2,1)S(1)} %pad_maximum_fusion.8), channel_id=1, source_target_pairs={{0,16},{1,17},{2,18},{3,19},{4,20},{5,21},{6,22},{7,23},{8,24},{9,... | collective-permute-start | bytes 884744 | tf_op jit(solution)/shard_map/ppermute | solution.py:858
  175.0 19.4 %collective-permute-start.32 = (bf16[2,4,1,48,1920]{4,3,1,2,0:T(8,128)(2,1)S(1)}, bf16[2,4,1,48,1920]{4,3,1,2,0:T(8,128)(2,1)S(1)}, u32[]{:S(2)}, u32[]{:S(2)}) collective-permute-start(bf16[2,4,1,48,1920]{4,3,1,2,0:T(8,128)(2,1)S(1)} %pad_maximum_fusion), channel_id=1, source_target_pairs={{0,2},{1,5},{2,0},{3,7},{4,6},{5,1},{6,4},{7,3},{8,10},{9,13},{10,... | collective-permute-start | bytes 4423688 | tf_op jit(solution)/shard_map/ppermute | solution.py:858
  207.6 19.6 %collective-permute-start.37 = (bf16[2,48,1920]{2,1,0:T(8,128)(2,1)S(1)}, bf16[2,48,1920]{2,1,0:T(8,128)(2,1)S(1)}, u32[]{:S(2)}, u32[]{:S(2)}) collective-permute-start(bf16[2,48,1920]{2,1,0:T(8,128)(2,1)S(1)} %pad_maximum_fusion.6), channel_id=1, source_target_pairs={{0,16},{1,17},{2,18},{3,19},{4,20},{5,21},{6,22},{7,23},{8,24},{9,... | collective-permute-start | bytes 1105928 | tf_op jit(solution)/shard_map/ppermute | solution.py:858
  210.3 13.1 %collective-permute-start.35 = (bf16[2,4,1,48,1152]{4,3,1,2,0:T(8,128)(2,1)S(1)}, bf16[2,4,1,48,1152]{4,3,1,2,0:T(8,128)(2,1)S(1)}, u32[]{:S(2)}, u32[]{:S(2)}) collective-permute-start(bf16[2,4,1,48,1152]{4,3,1,2,0:T(8,128)(2,1)S(1)} %pad_maximum_fusion.3), channel_id=1, source_target_pairs={{0,2},{1,5},{2,0},{3,7},{4,6},{5,1},{6,4},{7,3},{8,10},{9,13},{10,... | collective-permute-start | bytes 2654216 | tf_op jit(solution)/shard_map/ppermute | solution.py:858
  227.9 28.4 %collective-permute-start.42 = (f32[512,768]{1,0:T(8,128)S(1)}, f32[512,768]{1,0:T(8,128)}, u32[]{:S(2)}, u32[]{:S(2)}) collective-permute-start(f32[512,768]{1,0:T(8,128)S(1)} %get-tuple-element.222), channel_id=1, source_target_pairs={{0,1},{1,0},{2,3},{3,2},{4,5},{5,4},{6,7},{7,6},{8,9},{9,8},{10,11... | collective-permute-start | bytes 4718600 | tf_op jit(solution)/shard_map/ppermute | solution.py:858
  232.5 13.0 %collective-permute-start.50 = (f32[16,768]{1,0:T(8,128)S(1)}, f32[16,768]{1,0:T(8,128)S(1)}, u32[]{:S(2)}, u32[]{:S(2)}) collective-permute-start(f32[16,768]{1,0:T(8,128)S(1)} %add.658), channel_id=1, source_target_pairs={{0,8},{1,9},{2,10},{3,11},{4,12},{5,13},{6,14},{7,15},{8,0},{9,1},... | collective-permute-start | bytes 147464 | tf_op jit(solution)/shard_map/ppermute | solution.py:858
  247.8 12.7 %collective-permute-start.47 = (f32[48,1920]{1,0:T(8,128)S(1)}, f32[48,1920]{1,0:T(8,128)S(1)}, u32[]{:S(2)}, u32[]{:S(2)}) collective-permute-start(f32[48,1920]{1,0:T(8,128)S(1)} %convert_add_fusion.8.refs_0_), channel_id=1, source_target_pairs={{0,1},{1,0},{2,3},{3,2},{4,5},{5,4},{6,7},{7,6},{8,9},{9,8},{10,11... | collective-permute-start | bytes 1105928 | tf_op jit(solution)/shard_map/ppermute | solution.py:858
  (94 other events, 912.3 us)

commit v6 on v5

--- a/solution.py
+++ b/solution.py
@@ -1079,7 +1079,7 @@
     vec_total, _ = grid.small(vec_total, "first", shifts, *q_kept[1])
     vec_total, vec_here_got = grid.small(vec_total, "second", shifts, *q_here)
     out_theirs, out_mine = out_call(
-        core_arr, lengths, seats, after(mid, *q_here, *vec_here_got), e, vec, d_group
+        core_arr, lengths, seats, after(mid, in_grad, *q_here, *vec_here_got), e, vec, d_group
     )
     u_mine = grid.scatter_z([after(part, *q_here) for part in u_parts], out_theirs)
     u_other_mine = grid.swap(u_mine)

time: 267 us -> 272 us (1.019)
    dynamic_update_slice x2, local copies, waits for them, and re-layouts: 4.84 us -> 1.3 us  [both_slots(): lax.dynamic_update_slice(mine, got[None], (places['other'], zero, zero))]
    unnamed x134 -> x130, local copies, waits for them, and re-layouts: 9.51 us -> 12 us
  transfers between devices with their start and end apart: 52 -> 52, of which waited for: 20 -> 18; matrix products, arithmetic and copies ran while one was open for 7% -> 6% of each run, Pallas kernels for 50% -> 51%
where the time goes in v6:
time: 272 us; the launch traced here: 268 us
  Pallas kernels  136 us (50%)
  waiting for transfers between devices  55.9 us (21%)
  starting transfers between devices  40.9 us (15%)
  local copies, waits for them, and re-layouts  17.9 us (7%)
  other arithmetic  15.3 us (6%)
    ppermute x52, waiting for transfers between devices, permute(): return lax.ppermute(value, ('dp', 'seq'), pairs)  55.9 us
    ppermute x52, starting transfers between devices, permute(): return lax.ppermute(value, ('dp', 'seq'), pairs)  40.9 us
    pallas_call x3, Pallas kernels, weight_grad_call(): pl.pallas_call(functools.partial(weight_grad_kernel, len(lefts), [len(gro...  26.3 us
    pallas_call x2, Pallas kernels, attend_back_call(): pl.pallas_call(attend_back_kernel, name='attend_back', grid_spec=pltpu.Pr...  23.6 us
    pallas_call x1, Pallas kernels, down_call(): pl.pallas_call(functools.partial(down_kernel, up_group, down_group), name...  22.1 us
    pallas_call x1, Pallas kernels, up_call(): pl.pallas_call(functools.partial(up_kernel, group), name='up', grid_spec=...  19.7 us
    pallas_call x2, Pallas kernels, attend_call(): pl.pallas_call(functools.partial(attend_kernel, first), name='attend', gr...  13.7 us
    unnamed x130, local copies, waits for them, and re-layouts  12 us
  transfers between devices with their start and end apart: 52, of which 18 were waited for; matrix products, arithmetic and copies ran while one was open for 6% of the time, Pallas kernels for 51%

profile of v6, /device:TPU:0, one launch (start us, length us, event | category | flops | bytes accessed | tf_op | source)
XLA Modules:
  0.0 268.3 jit_solution(12333905325624619218)
XLA Ops:
  3.2 4.1 %collective-permute-start.2 = (bf16[48,1280]{1,0:T(8,128)(2,1)S(1)}, bf16[48,1280]{1,0:T(8,128)(2,1)S(1)}, u32[]{:S(2)}, u32[]{:S(2)}) collective-permute-start(bf16[48,1280]{1,0:T(8,128)(2,1)S(1)} %get-tuple-element.271), channel_id=1, source_target_pairs={{0,16},{1,17},{2,18},{3,19},{4,20},{5,21},{6,22},{7,23},{8,24},{9,... | collective-permute-start | bytes 368648 | tf_op jit(solution)/shard_map/ppermute | solution.py:858
  8.8 2.2 collective-permute-start.3
  13.0 3.8 %collective-permute-done.2 = bf16[48,1280]{1,0:T(8,128)(2,1)S(1)} collective-permute-done((bf16[48,1280]{1,0:T(8,128)(2,1)S(1)}, bf16[48,1280]{1,0:T(8,128)(2,1)S(1)}, u32[]{:S(2)}, u32[]{:S(2)}) %collective-permute-start.2) | collective-permute-done | bytes 122912 | tf_op jit(solution)/shard_map/ppermute | solution.py:858
  25.3 2.9 %collective-permute-done.4 = bf16[4,48,1280]{2,1,0:T(8,128)(2,1)S(1)} collective-permute-done((bf16[4,48,1280]{2,1,0:T(8,128)(2,1)S(1)}, bf16[4,48,1280]{2,1,0:T(8,128)(2,1)S(1)}, u32[]{:S(2)}, u32[]{:S(2)}) %collective-permute-start.4) | collective-permute-done | bytes 491552 | tf_op jit(solution)/shard_map/ppermute | solution.py:858
  31.9 15.5 %collective-permute-done.9 = bf16[2,48,1920]{2,1,0:T(8,128)(2,1)S(1)} collective-permute-done((bf16[2,48,1920]{2,1,0:T(8,128)(2,1)S(1)}, bf16[2,48,1920]{2,1,0:T(8,128)(2,1)S(1)}, u32[]{:S(2)}, u32[]{:S(2)}) %collective-permute-start.9) | collective-permute-done | bytes 368672 | tf_op jit(solution)/shard_map/ppermute | solution.py:858
  51.1 9.5 %qkv.1 = (bf16[1024,768]{1,0:T(8,128)(2,1)S(1)}, bf16[1024,2304]{1,0:T(8,128)(2,1)S(1)}, f32[16,768]{1,0:T(8,128)S(1)}, bf16[2304,768]{1,0:T(8,128)(2,1)S(1)}) custom-call(s32[1]{0:T(128)} %bitcast.64.core_ref, s32[32]{0:T(128)S(1)} %convert_element_type.410.seat_ref, bf16[1024,768]{1,0:T(8,128)(2,1)S(1)} %maximum_select_fusion.x_ref, ...), custom_call_target="tpu_custom_call" | custom-call | flops 14495514624 | bytes 40000000 | tf_op jit(solution)/shard_map/qkv/pallas_call | solution.py:161
  65.8 2.7 collective-permute-start.14
  69.2 8.9 %attend.2 = (bf16[1024,768]{1,0:T(8,128)(2,1)S(1)}, f32[6,8,1024]{2,1,0:T(8,128)S(1)}) custom-call(s32[1]{0:T(128)} %bitcast.64.core_ref, s32[2]{0:T(128)S(1)} %copy-done.34, bf16[1024,2304]{1,0:T(8,128)(2,1)S(1)} %get-tuple-element.152.qkv_ref.q_ref.k_ref.v_ref), custom_call_target="tpu_custom_call" | custom-call | flops 48000000000 | bytes 19200000 | tf_op jit(solution)/shard_map/attend/pallas_call | solution.py:274
  80.0 4.8 %attend.3 = (bf16[1024,768]{1,0:T(8,128)(2,1)S(1)}, f32[6,8,1024]{2,1,0:T(8,128)S(1)}) custom-call(s32[1]{0:T(128)} %bitcast.64.core_ref, s32[2]{0:T(128)S(1)} %copy-done.34, bf16[1024,2304]{1,0:T(8,128)(2,1)S(1)} %get-tuple-element.152.qkv_ref.q_ref.k_ref.v_ref, ...), custom_call_target="tpu_custom_call", output_to_operand_aliasing={{0}: (3, {}), {1}: (4, {})} | custom-call | flops 24000000000 | bytes 9600000 | tf_op jit(solution)/shard_map/attend/pallas_call | solution.py:274
  87.4 19.7 %up.1 = (f32[1024,768]{1,0:T(8,128)}, bf16[1024,768]{1,0:T(8,128)(2,1)}, bf16[1024,3072]{1,0:T(8,128)(2,1)}, bf16[1024,3072]{1,0:T(8,128)(2,1)}, bf16[1024,768]{1,0:T(8,128)(2,1)}) custom-call(s32[1]{0:T(128)} %bitcast.64.core_ref, s32[2]{0:T(128)S(1)} %copy-done.34, s32[32]{0:T(128)S(1)} %convert_element_type.409.seat_ref, bf16[1024,768]{1,0:T(8,128)(2,1)} %copy-done, ...), custom_call_target="tpu_custom_call" | custom-call | flops 24000000000 | bytes 120000000 | tf_op jit(solution)/shard_map/up/pallas_call | solution.py:458
  110.5 9.5 %grad_down.1 = (bf16[3072,384]{1,0:T(8,128)(2,1)S(1)}, bf16[3072,384]{1,0:T(8,128)(2,1)}) custom-call(s32[1]{0:T(128)} %bitcast.64.core_ref, bf16[1024,3072]{1,0:T(8,128)(2,1)} %get-tuple-element.166.refs_0_.e_ref, bf16[1024,768]{1,0:T(8,128)(2,1)S(1)} %copy-done.44), custom_call_target="tpu_custom_call" | custom-call | flops 19327352832 | bytes 50331648 | tf_op jit(solution)/shard_map/grad_down/pallas_call | solution.py:660
  121.9 22.1 %down.1 = (bf16[1024,3072]{1,0:T(8,128)(2,1)}, bf16[1024,768]{1,0:T(8,128)(2,1)}, f32[1024,768]{1,0:T(8,128)}, bf16[1024,768]{1,0:T(8,128)(2,1)}, f32[16,768]{1,0:T(8,128)S(1)}) custom-call(s32[1]{0:T(128)} %bitcast.64.core_ref, s32[32]{0:T(128)S(1)} %convert_element_type.409.seat_ref, f32[1024,768]{1,0:T(8,128)} %get-tuple-element.221.mid_ref, ...), custom_call_target="tpu_custom_call" | custom-call | flops 44000002048 | bytes 112000000 | tf_op jit(solution)/shard_map/down/pallas_call | solution.py:537
  147.7 11.9 %grad_up.1 = (bf16[768,1920]{1,0:T(8,128)(2,1)}, bf16[768,1920]{1,0:T(8,128)(2,1)}) custom-call(s32[1]{0:T(128)} %bitcast.64.core_ref, bf16[1024,768]{1,0:T(8,128)(2,1)S(1)} %copy-done.47, bf16[1024,768]{1,0:T(8,128)(2,1)S(1)} %copy-done.45, bf16[1024,768]{1,0:T(8,128)(2,1)S(1)} %copy-done.48, bf16[1024,3072]{1,0:T(8,128)(2,1)} %get-tuple-element.179.refs_3_), custom_call_target="tpu_custom_call" | custom-call | flops 24159191040 | bytes 61341696 | tf_op jit(solution)/shard_map/grad_up/pallas_call | solution.py:660
  164.2 8.2 %attend_back.2 = (bf16[1024,768]{1,0:T(8,128)(2,1)S(1)}, bf16[1024,768]{1,0:T(8,128)(2,1)S(1)}, bf16[1024,768]{1,0:T(8,128)(2,1)S(1)}) custom-call(s32[1]{0:T(128)} %bitcast.64.core_ref, s32[2]{0:T(128)S(1)} %copy-done.34, bf16[1024,2304]{1,0:T(8,128)(2,1)S(1)} %bitcast.276, bf16[1024,2304]{1,0:T(8,128)(2,1)S(1)} %bitcast.276, ...), custom_call_target="tpu_custom_call" | custom-call | flops 48000000000 | bytes 16000000 | tf_op jit(solution)/shard_map/attend_back/pallas_call | solution.py:371
  176.6 15.4 %attend_back.3 = (bf16[1024,768]{1,0:T(8,128)(2,1)S(1)}, bf16[1024,768]{1,0:T(8,128)(2,1)S(1)}, bf16[1024,768]{1,0:T(8,128)(2,1)S(1)}) custom-call(s32[1]{0:T(128)} %bitcast.64.core_ref, s32[2]{0:T(128)S(1)} %copy-done.34, bf16[1024,2304]{1,0:T(8,128)(2,1)S(1)} %bitcast.276, ...), custom_call_target="tpu_custom_call", output_to_operand_aliasing={{0}: (8, {}), {1}: (9, {}), {2}: (10, {})} | custom-call | flops 96000000000 | bytes 32000000 | tf_op jit(solution)/shard_map/attend_back/pallas_call | solution.py:371
  192.0 3.3 %collective-permute-done.32 = bf16[2,4,1,48,1920]{4,3,1,2,0:T(8,128)(2,1)S(1)} collective-permute-done((bf16[2,4,1,48,1920]{4,3,1,2,0:T(8,128)(2,1)S(1)}, bf16[2,4,1,48,1920]{4,3,1,2,0:T(8,128)(2,1)S(1)}, u32[]{:S(2)}, u32[]{:S(2)}) %collective-permute-start.32) | collective-permute-done | bytes 1474592 | tf_op jit(solution)/shard_map/ppermute | solution.py:858
  196.4 4.9 %grad_qkv.1 = (bf16[768,1152]{1,0:T(8,128)(2,1)S(1)}, bf16[768,1152]{1,0:T(8,128)(2,1)S(1)}) custom-call(s32[1]{0:T(128)} %bitcast.64.core_ref, bf16[1024,768]{1,0:T(8,128)(2,1)S(1)} %copy-done.43, bf16[1024,768]{1,0:T(8,128)(2,1)S(1)} %get-tuple-element.208.refs_1_.dq_ref, bf16[1024,768]{1,0:T(8,128)(2,1)S(1)} %get-tuple-element.199.refs_2_.dk_ref, ...), custom_call_target="tpu_custom_call" | custom-call | flops 14495514624 | bytes 39321600 | tf_op jit(solution)/shard_map/grad_qkv/pallas_call | solution.py:660
  201.4 5.7 %collective-permute-done.33 = bf16[4,1,48,1920]{3,2,1,0:T(8,128)(2,1)S(1)} collective-permute-done((bf16[4,1,48,1920]{3,2,1,0:T(8,128)(2,1)S(1)}, bf16[4,1,48,1920]{3,2,1,0:T(8,128)(2,1)S(1)}, u32[]{:S(2)}, u32[]{:S(2)}) %collective-permute-start.33) | collective-permute-done | bytes 737312 | tf_op jit(solution)/shard_map/ppermute | solution.py:858
  213.1 7.2 %last.1 = (f32[512,768]{1,0:T(8,128)S(1)}, f32[2,512,768]{2,1,0:T(8,128)}, f32[16,768]{1,0:T(8,128)S(1)}) custom-call(s32[1]{0:T(128)} %bitcast.64.core_ref, bf16[1024,768]{1,0:T(8,128)(2,1)S(1)} %copy-done.1, f32[1024,768]{1,0:T(8,128)S(1)} %copy-done.40, bf16[1024,768]{1,0:T(8,128)(2,1)S(1)} %get-tuple-element.208.refs_1_.dq_ref, ...), custom_call_target="tpu_custom_call" | custom-call | flops 14495514624 | bytes 64000000 | tf_op jit(solution)/shard_map/last/pallas_call | solution.py:724
  222.7 2.4 collective-permute-done.35
  226.2 3.1 %collective-permute-done.38 = bf16[2,48,1920]{2,1,0:T(8,128)(2,1)S(1)} collective-permute-done((bf16[2,48,1920]{2,1,0:T(8,128)(2,1)S(1)}, bf16[2,48,1920]{2,1,0:T(8,128)(2,1)S(1)}, u32[]{:S(2)}, u32[]{:S(2)}) %collective-permute-start.38) | collective-permute-done | bytes 368672 | tf_op jit(solution)/shard_map/ppermute | solution.py:858
  240.2 8.2 %out.1 = (bf16[512,768]{1,0:T(8,128)(2,1)}, bf16[2,512,768]{2,1,0:T(8,128)(2,1)}) custom-call(s32[1]{0:T(128)} %bitcast.64.core_ref, s32[2]{0:T(128)S(1)} %copy-done.34, s32[32]{0:T(128)S(1)} %copy-done.36, f32[1024,768]{1,0:T(8,128)S(1)} %copy-done.41, bf16[1024,3072]{1,0:T(8,128)(2,1)S(1)} %bitcast.278, f32[16,768]{1,0:T(8,128)S(1)} %get-tuple-element.155.vec_ref, ...), custom_call_target="tpu_custom_call" | custom-call | flops 19599998976 | bytes 64000000 | tf_op jit(solution)/shard_map/out/pallas_call | solution.py:599
  252.1 3.9 %collective-permute-done.44 = bf16[48,1152]{1,0:T(8,128)(2,1)S(1)} collective-permute-done((bf16[48,1152]{1,0:T(8,128)(2,1)S(1)}, bf16[48,1152]{1,0:T(8,128)(2,1)S(1)}, u32[]{:S(2)}, u32[]{:S(2)}) %collective-permute-start.44) | collective-permute-done | bytes 110624 | tf_op jit(solution)/shard_map/ppermute | solution.py:858
  262.8 2.9 %adam.4 = (f32[48,768]{1,0:T(8,128)}, f32[48,768]{1,0:T(8,128)}, f32[48,768]{1,0:T(8,128)}, f32[48,3072]{1,0:T(8,128)}, f32[48,3072]{1,0:T(8,128)}, /*index=5*/f32[48,3072]{1,0:T(8,128)}) custom-call(s32[1]{0:T(128)} %bitcast.64.core_ref, f32[48,1920]{1,0:T(8,128)S(1)} %convert_add_fusion.8.refs_0_, f32[48,1920]{1,0:T(8,128)} %collective-permute-done.47.refs_1_, ...), custom_call_target="tpu_custom_call" | custom-call | flops 4000000 | bytes 17694720 | tf_op jit(solution)/shard_map/adam/pallas_call | solution.py:774
  (286 shorter events, 83.2 us)
Async XLA Ops:
  3.2 13.6 %collective-permute-start.2 = (bf16[48,1280]{1,0:T(8,128)(2,1)S(1)}, bf16[48,1280]{1,0:T(8,128)(2,1)S(1)}, u32[]{:S(2)}, u32[]{:S(2)}) collective-permute-start(bf16[48,1280]{1,0:T(8,128)(2,1)S(1)} %get-tuple-element.271), channel_id=1, source_target_pairs={{0,16},{1,17},{2,18},{3,19},{4,20},{5,21},{6,22},{7,23},{8,24},{9,... | collective-permute-start | bytes 368648 | tf_op jit(solution)/shard_map/ppermute | solution.py:858
  28.3 19.1 %collective-permute-start.7 = (bf16[2,4,48,1280]{3,2,1,0:T(8,128)(2,1)S(1)}, bf16[2,4,48,1280]{3,2,1,0:T(8,128)(2,1)}, u32[]{:S(2)}, u32[]{:S(2)}) collective-permute-start(bf16[2,4,48,1280]{3,2,1,0:T(8,128)(2,1)S(1)} %pad_maximum_fusion.2.refs_0_), channel_id=1, source_target_pairs={{0,4},{1,3},{2,6},{3,1},{4,0},{5,7},{6,2},{7,5},{8,12},{9,11},{10,... | collective-permute-start | bytes 2949128 | tf_op jit(solution)/shard_map/ppermute | solution.py:858
  29.9 17.4 %collective-permute-start.9 = (bf16[2,48,1920]{2,1,0:T(8,128)(2,1)S(1)}, bf16[2,48,1920]{2,1,0:T(8,128)(2,1)S(1)}, u32[]{:S(2)}, u32[]{:S(2)}) collective-permute-start(bf16[2,48,1920]{2,1,0:T(8,128)(2,1)S(1)} %pad_maximum_fusion.5), channel_id=1, source_target_pairs={{0,16},{1,17},{2,18},{3,19},{4,20},{5,21},{6,22},{7,23},{8,24},{9,... | collective-permute-start | bytes 1105928 | tf_op jit(solution)/shard_map/ppermute | solution.py:858
  31.8 17.7 %collective-permute-start.8 = (bf16[2,4,48,1280]{3,2,1,0:T(8,128)(2,1)S(1)}, bf16[2,4,48,1280]{3,2,1,0:T(8,128)(2,1)}, u32[]{:S(2)}, u32[]{:S(2)}) collective-permute-start(bf16[2,4,48,1280]{3,2,1,0:T(8,128)(2,1)S(1)} %pad_maximum_fusion.2.refs_0_), channel_id=1, source_target_pairs={{0,1},{1,0},{2,3},{3,2},{4,5},{5,4},{6,7},{7,6},{8,9},{9,8},{10,11... | collective-permute-start | bytes 2949128 | tf_op jit(solution)/shard_map/ppermute | solution.py:858
  47.5 30.6 %collective-permute-start.16 = (bf16[4,48,1920]{2,1,0:T(8,128)(2,1)S(1)}, bf16[4,48,1920]{2,1,0:T(8,128)(2,1)S(1)}, u32[]{:S(2)}, u32[]{:S(2)}) collective-permute-start(bf16[4,48,1920]{2,1,0:T(8,128)(2,1)S(1)} %constant_dynamic-update-slice_fusion), channel_id=1, source_target_pairs={{0,1},{1,0},{2,3},{3,2},{4,5},{5,4},{6,7},{7,6},{8,9},{9,8},{10,11... | collective-permute-start | bytes 2211848 | tf_op jit(solution)/shard_map/ppermute | solution.py:858
  48.0 17.8 %collective-permute-start.13 = (bf16[4,48,1920]{2,1,0:T(8,128)(2,1)S(1)}, bf16[4,48,1920]{2,1,0:T(8,128)(2,1)S(1)}, u32[]{:S(2)}, u32[]{:S(2)}) collective-permute-start(bf16[4,48,1920]{2,1,0:T(8,128)(2,1)S(1)} %constant_dynamic-update-slice_fusion), channel_id=1, source_target_pairs={{0,2},{1,5},{2,0},{3,7},{4,6},{5,1},{6,4},{7,3},{8,10},{9,13},{10,... | collective-permute-start | bytes 2211848 | tf_op jit(solution)/shard_map/ppermute | solution.py:858
  48.5 20.0 %collective-permute-start.11 = (bf16[2,192,384]{2,1,0:T(8,128)(2,1)}, bf16[2,192,384]{2,1,0:T(8,128)(2,1)S(1)}, u32[]{:S(2)}, u32[]{:S(2)}) collective-permute-start(bf16[2,192,384]{2,1,0:T(8,128)(2,1)} %pad_maximum_fusion.7), channel_id=1, source_target_pairs={{0,16},{1,17},{2,18},{3,19},{4,20},{5,21},{6,22},{7,23},{8,24},{9,... | collective-permute-start | bytes 884744 | tf_op jit(solution)/shard_map/ppermute | solution.py:858
  49.5 28.6 %collective-permute-start.12 = (bf16[4,48,1920]{2,1,0:T(8,128)(2,1)S(1)}, bf16[4,48,1920]{2,1,0:T(8,128)(2,1)S(1)}, u32[]{:S(2)}, u32[]{:S(2)}) collective-permute-start(bf16[4,48,1920]{2,1,0:T(8,128)(2,1)S(1)} %constant_dynamic-update-slice_fusion), channel_id=1, source_target_pairs={{0,4},{1,3},{2,6},{3,1},{4,0},{5,7},{6,2},{7,5},{8,12},{9,11},{10,... | collective-permute-start | bytes 2211848 | tf_op jit(solution)/shard_map/ppermute | solution.py:858
  65.8 14.2 %collective-permute-start.17 = (bf16[4,48,1920]{2,1,0:T(8,128)(2,1)S(1)}, bf16[4,48,1920]{2,1,0:T(8,128)(2,1)S(1)}, u32[]{:S(2)}, u32[]{:S(2)}) collective-permute-start(bf16[4,48,1920]{2,1,0:T(8,128)(2,1)S(1)} %collective-permute-done.13), channel_id=1, source_target_pairs={{0,1},{1,0},{2,3},{3,2},{4,5},{5,4},{6,7},{7,6},{8,9},{9,8},{10,11... | collective-permute-start | bytes 2211848 | tf_op jit(solution)/shard_map/ppermute | solution.py:858
  68.7 16.8 %collective-permute-start.15 = (bf16[512,768]{1,0:T(8,128)(2,1)S(1)}, bf16[512,768]{1,0:T(8,128)(2,1)S(1)}, u32[]{:S(2)}, u32[]{:S(2)}) collective-permute-start(bf16[512,768]{1,0:T(8,128)(2,1)S(1)} %get-tuple-element.259), channel_id=1, source_target_pairs={{0,1},{1,0},{2,3},{3,2},{4,5},{5,4},{6,7},{7,6},{8,9},{9,8},{10,11... | collective-permute-start | bytes 2359304 | tf_op jit(solution)/shard_map/ppermute | solution.py:858
  78.3 41.9 %collective-permute-start.23 = (bf16[4,192,384]{2,1,0:T(8,128)(2,1)S(1)}, bf16[4,192,384]{2,1,0:T(8,128)(2,1)S(1)}, u32[]{:S(2)}, u32[]{:S(2)}) collective-permute-start(bf16[4,192,384]{2,1,0:T(8,128)(2,1)S(1)} %constant_dynamic-update-slice_fusion.2), channel_id=1, source_target_pairs={{0,1},{1,0},{2,3},{3,2},{4,5},{5,4},{6,7},{7,6},{8,9},{9,8},{10,11... | collective-permute-start | bytes 1769480 | tf_op jit(solution)/shard_map/ppermute | solution.py:858
  78.8 30.1 %collective-permute-start.21 = (bf16[4,192,384]{2,1,0:T(8,128)(2,1)S(1)}, bf16[4,192,384]{2,1,0:T(8,128)(2,1)S(1)}, u32[]{:S(2)}, u32[]{:S(2)}) collective-permute-start(bf16[4,192,384]{2,1,0:T(8,128)(2,1)S(1)} %constant_dynamic-update-slice_fusion.2), channel_id=1, source_target_pairs={{0,4},{1,3},{2,6},{3,1},{4,0},{5,7},{6,2},{7,5},{8,12},{9,11},{10,... | collective-permute-start | bytes 1769480 | tf_op jit(solution)/shard_map/ppermute | solution.py:858
  84.8 22.3 %collective-permute-start.20 = (bf16[4,192,384]{2,1,0:T(8,128)(2,1)S(1)}, bf16[4,192,384]{2,1,0:T(8,128)(2,1)S(1)}, u32[]{:S(2)}, u32[]{:S(2)}) collective-permute-start(bf16[4,192,384]{2,1,0:T(8,128)(2,1)S(1)} %constant_dynamic-update-slice_fusion.2), channel_id=1, source_target_pairs={{0,2},{1,5},{2,0},{3,7},{4,6},{5,1},{6,4},{7,3},{8,10},{9,13},{10,... | collective-permute-start | bytes 1769480 | tf_op jit(solution)/shard_map/ppermute | solution.py:858
  107.1 13.4 %collective-permute-start.24 = (bf16[4,192,384]{2,1,0:T(8,128)(2,1)S(1)}, bf16[4,192,384]{2,1,0:T(8,128)(2,1)S(1)}, u32[]{:S(2)}, u32[]{:S(2)}) collective-permute-start(bf16[4,192,384]{2,1,0:T(8,128)(2,1)S(1)} %collective-permute-done.20), channel_id=1, source_target_pairs={{0,1},{1,0},{2,3},{3,2},{4,5},{5,4},{6,7},{7,6},{8,9},{9,8},{10,11... | collective-permute-start | bytes 1769480 | tf_op jit(solution)/shard_map/ppermute | solution.py:858
  120.2 23.9 %collective-permute-start.27 = (bf16[3072,384]{1,0:T(8,128)(2,1)}, bf16[3072,384]{1,0:T(8,128)(2,1)S(1)}, u32[]{:S(2)}, u32[]{:S(2)}) collective-permute-start(bf16[3072,384]{1,0:T(8,128)(2,1)} %get-tuple-element.177), channel_id=1, source_target_pairs={{0,1},{1,0},{2,3},{3,2},{4,5},{5,4},{6,7},{7,6},{8,9},{9,8},{10,11... | collective-permute-start | bytes 7077896 | tf_op jit(solution)/shard_map/ppermute | solution.py:858
  145.7 16.4 %collective-permute-start.29 = (bf16[2,4,1,192,384]{4,3,1,2,0:T(8,128)(2,1)}, bf16[2,4,1,192,384]{4,3,1,2,0:T(8,128)(2,1)S(1)}, u32[]{:S(2)}, u32[]{:S(2)}) collective-permute-start(bf16[2,4,1,192,384]{4,3,1,2,0:T(8,128)(2,1)} %pad_maximum_fusion.1), channel_id=1, source_target_pairs={{0,2},{1,5},{2,0},{3,7},{4,6},{5,1},{6,4},{7,3},{8,10},{9,13},{10,... | collective-permute-start | bytes 3538952 | tf_op jit(solution)/shard_map/ppermute | solution.py:858
  159.7 15.3 %collective-permute-start.28 = (bf16[768,1920]{1,0:T(8,128)(2,1)}, bf16[768,1920]{1,0:T(8,128)(2,1)S(1)}, u32[]{:S(2)}, u32[]{:S(2)}) collective-permute-start(bf16[768,1920]{1,0:T(8,128)(2,1)} %get-tuple-element.180), channel_id=1, source_target_pairs={{0,1},{1,0},{2,3},{3,2},{4,5},{5,4},{6,7},{7,6},{8,9},{9,8},{10,11... | collective-permute-start | bytes 8847368 | tf_op jit(solution)/shard_map/ppermute | solution.py:858
  174.9 17.1 %collective-permute-start.31 = (bf16[2,192,384]{2,1,0:T(8,128)(2,1)S(1)}, bf16[2,192,384]{2,1,0:T(8,128)(2,1)S(1)}, u32[]{:S(2)}, u32[]{:S(2)}) collective-permute-start(bf16[2,192,384]{2,1,0:T(8,128)(2,1)S(1)} %pad_maximum_fusion.8), channel_id=1, source_target_pairs={{0,16},{1,17},{2,18},{3,19},{4,20},{5,21},{6,22},{7,23},{8,24},{9,... | collective-permute-start | bytes 884744 | tf_op jit(solution)/shard_map/ppermute | solution.py:858
  175.9 19.4 %collective-permute-start.32 = (bf16[2,4,1,48,1920]{4,3,1,2,0:T(8,128)(2,1)S(1)}, bf16[2,4,1,48,1920]{4,3,1,2,0:T(8,128)(2,1)S(1)}, u32[]{:S(2)}, u32[]{:S(2)}) collective-permute-start(bf16[2,4,1,48,1920]{4,3,1,2,0:T(8,128)(2,1)S(1)} %pad_maximum_fusion), channel_id=1, source_target_pairs={{0,2},{1,5},{2,0},{3,7},{4,6},{5,1},{6,4},{7,3},{8,10},{9,13},{10,... | collective-permute-start | bytes 4423688 | tf_op jit(solution)/shard_map/ppermute | solution.py:858
  207.1 13.2 %collective-permute-start.48 = (bf16[192,384]{1,0:T(8,128)(2,1)S(1)}, bf16[192,384]{1,0:T(8,128)(2,1)S(1)}, u32[]{:S(2)}, u32[]{:S(2)}) collective-permute-start(bf16[192,384]{1,0:T(8,128)(2,1)S(1)} %fusion.15), channel_id=1, source_target_pairs={{0,8},{1,9},{2,10},{3,11},{4,12},{5,13},{6,14},{7,15},{8,0},{9,1},... | collective-permute-start | bytes 442376 | tf_op jit(solution)/shard_map/ppermute | solution.py:858
  209.7 19.6 %collective-permute-start.38 = (bf16[2,48,1920]{2,1,0:T(8,128)(2,1)S(1)}, bf16[2,48,1920]{2,1,0:T(8,128)(2,1)S(1)}, u32[]{:S(2)}, u32[]{:S(2)}) collective-permute-start(bf16[2,48,1920]{2,1,0:T(8,128)(2,1)S(1)} %pad_maximum_fusion.6), channel_id=1, source_target_pairs={{0,16},{1,17},{2,18},{3,19},{4,20},{5,21},{6,22},{7,23},{8,24},{9,... | collective-permute-start | bytes 1105928 | tf_op jit(solution)/shard_map/ppermute | solution.py:858
  212.0 13.1 %collective-permute-start.35 = (bf16[2,4,1,48,1152]{4,3,1,2,0:T(8,128)(2,1)S(1)}, bf16[2,4,1,48,1152]{4,3,1,2,0:T(8,128)(2,1)S(1)}, u32[]{:S(2)}, u32[]{:S(2)}) collective-permute-start(bf16[2,4,1,48,1152]{4,3,1,2,0:T(8,128)(2,1)S(1)} %pad_maximum_fusion.3), channel_id=1, source_target_pairs={{0,2},{1,5},{2,0},{3,7},{4,6},{5,1},{6,4},{7,3},{8,10},{9,13},{10,... | collective-permute-start | bytes 2654216 | tf_op jit(solution)/shard_map/ppermute | solution.py:858
  234.3 14.3 %collective-permute-start.50 = (f32[16,768]{1,0:T(8,128)S(1)}, f32[16,768]{1,0:T(8,128)S(1)}, u32[]{:S(2)}, u32[]{:S(2)}) collective-permute-start(f32[16,768]{1,0:T(8,128)S(1)} %add.658), channel_id=1, source_target_pairs={{0,8},{1,9},{2,10},{3,11},{4,12},{5,13},{6,14},{7,15},{8,0},{9,1},... | collective-permute-start | bytes 147464 | tf_op jit(solution)/shard_map/ppermute | solution.py:858
  248.5 17.2 %collective-permute-start.42 = (bf16[512,768]{1,0:T(8,128)(2,1)}, bf16[512,768]{1,0:T(8,128)(2,1)}, u32[]{:S(2)}, u32[]{:S(2)}) collective-permute-start(bf16[512,768]{1,0:T(8,128)(2,1)} %get-tuple-element.223), channel_id=1, source_target_pairs={{0,1},{1,0},{2,3},{3,2},{4,5},{5,4},{6,7},{7,6},{8,9},{9,8},{10,11... | collective-permute-start | bytes 2359304 | tf_op jit(solution)/shard_map/ppermute | solution.py:858
  (92 other events, 881.6 us)
